TPU v7x, 256 devices: a whole 4x4x8 slice. The times are simulated.
256 devices in a mesh: row: 16 (over x_hi, z), col: 16 (over x_lo, y, core).
Axes of the slice: x: 4 (x_hi: 2, x_lo: 2; x = x_hi * 2 + x_lo), y: 4, z: 8, core: 2. Of those that a mesh axis runs over, the one named last changes fastest.
Arguments:
- charges: float32 [48, 64], P('row', 'col'), may hold values from -6 to 6
- hubbard: float32 [48, 64], P('row', 'col'), may hold values from 0.2 to 2
- coupling: float32 [3, 3], replicated, may hold values from 0.1 to 0.6
- orbital_atom: int32 [16, 16, 24], P('row', 'col'), may hold values from 0 to 11
- block_mask: int32 [64, 64], P('row', 'col'), may hold values from 0 to 1, as said below
- bare_ham: bfloat16 [6144, 6144], P('row', 'col'), as said below
- intersection: bfloat16 [6144, 6144], P('row', 'col'), as said below
Outputs:
- purified: float32 [6144, 6144], P('row', 'col')
Inputs may be any that keep to these rules, and one draw needn't show every extreme that they name: `block_mask`: symmetric; blocks whose domain rows lie within 2 of each other, counted around the slab's periodic first dimension, are always occupied, other blocks only in part. `bare_ham`: symmetric. `intersection`: symmetric.
All inputs are finite; a program needn't handle non-finite values.
Results may differ from a plain program's by a relative error of at most 0.009.
Values may be sent and summed in bfloat16 or wider, within the bound.
No kernel may reach another device: no remote copies, remote signals or barrier semaphores. Data moves between devices by JAX's collectives and lax.ppermute only.
A program may use at most 64 MiB of HBM per device.

v0:
```python
import jax
import jax.numpy as jnp
from jax import lax
from jax.sharding import PartitionSpec as P

BLK = 96


def padded_2(value, sides, width):
    for axis, dim in sides:
        peers, length = (lax.axis_size(axis), value.shape[dim])
        up = [(i, (i + 1) % peers) for i in range(peers)]
        down = [(j, i) for i, j in up]
        last = lax.slice_in_dim(value, length - width, length, axis=dim)
        leading = lax.slice_in_dim(value, 0, width, axis=dim)
        before = lax.ppermute(last, axis, up)
        after = lax.ppermute(leading, axis, down)
        value = jnp.concatenate([before, value, after], axis=dim)
    return value


def strip_product(left_strip, right_tile):
    return jnp.dot(
        left_strip,
        lax.all_gather(right_tile, "row", axis=0, tiled=True),
        preferred_element_type=jnp.float32,
    )


def per_device(charges, hubbard, coupling, orbital_atom, block_mask, bare_ham, intersection):
    rows_here = bare_ham.shape[0]
    cols_here = bare_ham.shape[1]
    atom_rows = charges.shape[0]
    atom_cols = charges.shape[1]
    padded = padded_2(charges, (("row", 0), ("col", 1)), 1)
    shift_grid = hubbard * charges
    for a in range(3):
        for b in range(3):
            shift_grid = shift_grid + coupling[a, b] * padded[a : a + atom_rows, b : b + atom_cols]
    flat_shift = shift_grid.reshape(atom_rows * atom_cols)
    orbital_picks = orbital_atom.reshape(-1)
    onehot = orbital_picks[:, None] == jnp.arange(atom_rows * atom_cols, dtype=jnp.int32)[None, :]
    local_shift = jnp.sum(jnp.where(onehot, flat_shift[None, :], 0.0), axis=1)
    every_shift = lax.all_gather(local_shift, ("row", "col"), axis=0, tiled=True)
    row_index = lax.axis_index("row")
    col_index = lax.axis_index("col")
    row_shift = lax.dynamic_slice_in_dim(every_shift, row_index * rows_here, rows_here)
    col_shift = lax.dynamic_slice_in_dim(every_shift, col_index * cols_here, cols_here)
    hamilton = bare_ham.astype(jnp.float32) + 0.5 * intersection.astype(jnp.float32) * (
        row_shift[:, None] + col_shift[None, :]
    )
    block_rows = rows_here // BLK
    block_cols = cols_here // BLK
    masked = (
        hamilton.reshape(block_rows, BLK, block_cols, BLK)
        * block_mask.astype(jnp.float32)[:, None, :, None]
    ).reshape(rows_here, cols_here)
    global_rows = row_index * rows_here + jnp.arange(rows_here, dtype=jnp.int32)
    global_cols = col_index * cols_here + jnp.arange(cols_here, dtype=jnp.int32)
    identity = (global_rows[:, None] == global_cols[None, :]).astype(jnp.float32)
    initial = (0.5 * identity - masked).astype(jnp.bfloat16)
    initial_strip = lax.all_gather(initial, "col", axis=1, tiled=True)
    square_term = strip_product(initial_strip, initial)
    square_half = square_term.astype(jnp.bfloat16)
    square_strip = lax.all_gather(square_half, "col", axis=1, tiled=True)
    cube_term = strip_product(square_strip, initial)
    return 3.0 * square_term - 2.0 * cube_term


def solution(mesh):
    placed = (
        P("row", "col"),
        P("row", "col"),
        P(),
        P("row", "col", None),
        P("row", "col"),
        P("row", "col"),
        P("row", "col"),
    )
    return jax.shard_map(
        per_device, mesh=mesh, in_specs=placed, out_specs=P("row", "col"), check_vma=False
    )
```

profile of v0, /device:TPU:1, one launch (start us, length us, event | category | flops | bytes accessed | tf_op | source)
XLA Modules:
  0.0 314.6 jit_solution(15423646652929637312)
XLA Ops:
  6.5 0.0 all-gather.4.cloned.1.call-start
  6.5 0.8 fusion.4
  7.3 2.5 collective-permute-start
  9.8 6.4 %collective-permute-start.1 = (f32[1,4]{1,0:T(1,128)S(1)}, f32[1,4]{1,0:T(1,128)S(1)}, u32[]{:S(2)}, u32[]{:S(2)}) collective-permute-start(f32[1,4]{1,0:T(1,128)S(1)} %get-tuple-element.23), channel_id=1, source_target_pairs={{16,0},{32,16},{48,32},{64,48},{80,64},{96,80},{112,96},{128,112},... | collective-permute-start | bytes 56 | tf_op jit(solution)/shard_map/ppermute | solution.py:17
  16.2 0.7 convert_element_type.18
  16.9 1.7 fusion.3
  18.5 0.2 mul.121
  18.7 0.4 mul.122
  19.1 0.0 collective-permute-done
  19.1 0.0 collective-permute-done.1
  19.1 0.7 pad_maximum_fusion
  19.8 0.1 fusion.2
  19.9 2.1 collective-permute-start.2
  22.0 0.0 collective-permute-start.3
  22.0 0.8 pad_maximum_fusion.2
  22.8 0.0 collective-permute-done.2
  22.8 2.6 collective-permute-done.3
  25.4 0.8 maximum_maximum_fusion
  26.2 6.4 %multiply_add_fusion = f32[3,4]{1,0:T(4,128)S(1)} fusion(f32[5,5]{1,0:T(8,128)S(1)} %get-tuple-element.10, f32[4,4]{1,0:T(4,128)S(1)} %get-tuple-element.21, f32[5,5]{1,0:T(8,128)S(1)} %get-tuple-element.9, f32[3,4]{1,0:T(4,128)} %param.7, f32[4,4]{1,0:T(4,128)S(1)} %get-tuple-element.20, f32[3,4]{1,0:T(4,128)} %param.8, f32[]{:T(128)} %bitcast.9, ...), kind=kLoop, calls=%fused_computation.10 | loop fusion | flops 228 | bytes 564 | tf_op jit(solution)/shard_map/add | solution.py:39
  32.6 0.1 broadcast_in_dim.20
  32.7 0.7 select_reduce_fusion
  33.4 0.3 dynamic-update-slice
  33.7 77.3 %all-reduce = f32[6144]{0:T(1024)S(1)} all-reduce(f32[6144]{0:T(1024)S(1)} %dynamic-update-slice), channel_id=1, replica_groups=mesh['row'=16,'col'=16] {'row','col'}, use_global_device_ids=true, to_apply=%add | all-reduce | flops 6144 | bytes 49152
  111.0 0.1 fusion.1
  111.1 2.0 subtract_convert_fusion
  113.1 0.0 all-gather.4.cloned.1.call-update
  113.1 0.0 all-gather.6.cloned.1.call-start
  113.2 0.7 all-gather.6.cloned.1.call-update
  113.9 0.0 all-gather.8.cloned.1.call-start
  113.9 35.4 %all-gather.4.cloned.1.call-done = bf16[384,6144]{1,0:T(8,128)(2,1)} async-done(((bf16[384,384]{1,0:T(8,128)(2,1)}), bf16[384,6144]{1,0:T(8,128)(2,1)}) %all-gather.4.cloned.1.call-update) | async-done | bytes 4718608 | tf_op jit(solution)/shard_map/all_gather | solution.py:62
  149.3 103.0 %all-gather.6.cloned.1.call-done = bf16[6144,384]{1,0:T(8,128)(2,1)} async-done(((bf16[384,384]{1,0:T(8,128)(2,1)}), bf16[6144,384]{1,0:T(8,128)(2,1)}) %all-gather.6.cloned.1.call-update) | async-done | bytes 4718608 | tf_op jit(solution)/shard_map/all_gather | solution.py:25
  252.3 7.1 %fusion.5 = (bf16[384,384]{1,0:T(8,128)(2,1)}, f32[384,384]{1,0:T(8,128)S(1)}) fusion(bf16[384,6144]{1,0:T(8,128)(2,1)} %all-gather.4.cloned.1.call-done, bf16[6144,384]{1,0:T(8,128)(2,1)} %all-gather.6.cloned.1.call-done), kind=kOutput, calls=%fused_computation.17 | convolution fusion | flops 1812086784 | bytes 10321920 | tf_op jit(solution)/shard_map/dot_general | solution.py:23
  259.4 0.0 all-gather.8.cloned.1.call-update
  259.4 41.5 %all-gather.8.cloned.1.call-done = bf16[384,6144]{1,0:T(8,128)(2,1)} async-done(((bf16[384,384]{1,0:T(8,128)(2,1)}), bf16[384,6144]{1,0:T(8,128)(2,1)}) %all-gather.8.cloned.1.call-update) | async-done | bytes 4718608 | tf_op jit(solution)/shard_map/all_gather | solution.py:65
  300.9 7.2 %fusion = f32[384,384]{1,0:T(8,128)} fusion(bf16[384,6144]{1,0:T(8,128)(2,1)} %all-gather.8.cloned.1.call-done, bf16[6144,384]{1,0:T(8,128)(2,1)} %all-gather.6.cloned.1.call-done, f32[384,384]{1,0:T(8,128)S(1)} %get-tuple-element.25), kind=kOutput, calls=%fused_computation.1 | convolution fusion | flops 1812381696 | bytes 10616832 | tf_op jit(solution)/shard_map/dot_general | solution.py:23
  (2 shorter events, 0.0 us)
Async XLA Ops:
  6.5 142.7 %all-gather.4.cloned.1.call-start = ((), (), s32[]{:S(2)}) async-start(), calls=%async_computation | async-start | bytes 5013504 | tf_op jit(solution)/shard_map/all_gather | solution.py:62
  7.3 11.8 %collective-permute-start = (f32[1,4]{1,0:T(1,128)S(1)}, f32[1,4]{1,0:T(1,128)S(1)}, u32[]{:S(2)}, u32[]{:S(2)}) collective-permute-start(f32[1,4]{1,0:T(1,128)S(1)} %get-tuple-element.22), channel_id=1, source_target_pairs={{0,16},{16,32},{32,48},{48,64},{64,80},{80,96},{96,112},{112,128},... | collective-permute-start | bytes 56 | tf_op jit(solution)/shard_map/ppermute | solution.py:16
  9.8 9.4 %collective-permute-start.1 = (f32[1,4]{1,0:T(1,128)S(1)}, f32[1,4]{1,0:T(1,128)S(1)}, u32[]{:S(2)}, u32[]{:S(2)}) collective-permute-start(f32[1,4]{1,0:T(1,128)S(1)} %get-tuple-element.23), channel_id=1, source_target_pairs={{16,0},{32,16},{48,32},{64,48},{80,64},{96,80},{112,96},{128,112},... | collective-permute-start | bytes 56 | tf_op jit(solution)/shard_map/ppermute | solution.py:17
  19.9 2.9 collective-permute-start.2
  22.0 3.3 %collective-permute-start.3 = (f32[5,1]{1,0:T(8,128)S(1)}, f32[5,1]{1,0:T(8,128)S(1)}, u32[]{:S(2)}, u32[]{:S(2)}) collective-permute-start(f32[5,1]{1,0:T(8,128)S(1)} %get-tuple-element.8), channel_id=1, source_target_pairs={{1,0},{2,1},{3,2},{4,3},{5,4},{6,5},{7,6},{8,7},{9,8},{10,9},{11,1... | collective-permute-start | bytes 68 | tf_op jit(solution)/shard_map/ppermute | solution.py:17
  113.1 139.2 %all-gather.6.cloned.1.call-start = ((), (), s32[]{:S(2)}) async-start(), calls=%async_computation.1 | async-start | bytes 5013504 | tf_op jit(solution)/shard_map/all_gather | solution.py:25
  113.9 187.0 %all-gather.8.cloned.1.call-start = ((), (), s32[]{:S(2)}) async-start(), calls=%async_computation.2 | async-start | bytes 5013504 | tf_op jit(solution)/shard_map/all_gather | solution.py:65
Sparse Core Ops, SparseCore 0:
  113.2 36.0 all-gather.3
  151.9 100.3 all-gather.5
  259.5 41.3 all-gather.7
where the time goes:
time: 315 us
  waiting for transfers between devices  183 us (58%)
  blocking collectives  77.3 us (25%)
  matrix products  14.3 us (5%)
  between operations  13.2 us (4%)
  other arithmetic  12.2 us (4%)
  starting transfers between devices  11.1 us (4%)
  local copies, waits for them, and re-layouts  3.51 us (1%)
    all_gather x1, waiting for transfers between devices, strip_product(): lax.all_gather(right_tile, 'row', axis=0, tiled=True)  103 us
    unnamed x1, blocking collectives  77.3 us
    all_gather x1, waiting for transfers between devices, per_device(): square_strip = lax.all_gather(square_half, 'col', axis=1, tiled=True)  41.5 us
    all_gather x1, waiting for transfers between devices, per_device(): initial_strip = lax.all_gather(initial, 'col', axis=1, tiled=True)  35.4 us
    dot_general x2, matrix products, strip_product(): jnp.dot(left_strip, lax.all_gather(right_tile, 'row', axis=0, tiled=True)...  14.3 us
    add x1, other arithmetic, per_device(): shift_grid + coupling[a, b] * padded[a:a + atom_rows, b:b + atom_cols]  6.41 us
    ppermute x2, starting transfers between devices, padded_2(): after = lax.ppermute(leading, axis, down)  6.4 us
  transfers between devices with their start and end apart: 7, of which 4 were waited for; matrix products, arithmetic and copies ran while one was open for 1% of the time, Pallas kernels for 0%

commit v1 on v0

v1 whole, which is shorter than its diff:
```python
import functools

import jax
import jax.numpy as jnp
from jax import lax
from jax.experimental import pallas as pl
from jax.experimental.pallas import tpu as pltpu
from jax.sharding import PartitionSpec as P

BLK = 96
TILE = 384
NROW = 16
ORBD = 24
LANES = 128
RING = 8
HIGH = lax.Precision.HIGHEST
F32 = jnp.float32
VMEM = pl.BlockSpec(memory_space=pltpu.VMEM)
SMEM = pl.BlockSpec(memory_space=pltpu.SMEM)
ANY = pl.BlockSpec(memory_space=pl.ANY)


def iota(shape, dim):
    return lax.broadcasted_iota(jnp.int32, shape, dim)


def pack_kernel(charges, hubbard, picks, out):
    col = lax.axis_index("col")
    out[...] = jnp.zeros_like(out)
    spread = (iota((4, LANES), 1) % 64 == 4 * col + iota((4, LANES), 0)).astype(F32)
    for first, ref in ((0, charges), (3, hubbard)):
        for i in range(3):
            row = jnp.zeros((1, LANES), F32)
            for j in range(4):
                row = row + spread[j : j + 1] * ref[i, j]
            out[first + i : first + i + 1, :] = row
    for part in range(3):
        lane = iota((1, LANES), 1) + part * LANES
        row = jnp.zeros((1, LANES), F32)
        for o in range(ORBD):
            row = jnp.where(lane == ORBD * col + o, picks[0, 0, o].astype(F32), row)
        out[6 + part : 7 + part, :] = row


def pack(charges, hubbard, orbital_atom):
    return pl.pallas_call(
        pack_kernel,
        out_shape=jax.ShapeDtypeStruct((16, LANES), F32),
        in_specs=[SMEM, SMEM, SMEM],
        out_specs=VMEM,
    )(charges, hubbard, orbital_atom)


def sum_kernel(parts, out):
    total = parts[0]
    for i in range(1, NROW):
        total = total + parts[i]
    out[...] = total


def sum_parts(parts):
    return pl.pallas_call(
        sum_kernel,
        out_shape=jax.ShapeDtypeStruct(parts.shape[1:], F32),
        in_specs=[VMEM],
        out_specs=VMEM,
    )(parts)


def everywhere(value, axis):
    copies = jnp.broadcast_to(value[None], (NROW,) + value.shape)
    return lax.all_to_all(copies, axis, 0, 0)


def row_shift(strips, coupling, q):
    above = strips[(q + NROW - 1) % NROW]
    here = strips[q]
    below = strips[(q + 1) % NROW]
    atoms = [above[2:3], here[0:1], here[1:2], here[2:3], below[0:1]]
    rolled = [[pltpu.roll(v, 1, 1), v, pltpu.roll(v, LANES - 1, 1)] for v in atoms]
    grids = []
    for i in range(3):
        shift = here[3 + i : 4 + i] * here[i : i + 1]
        for a in range(3):
            for b in range(3):
                shift = shift + coupling[a, b] * rolled[i + a][b]
        grids.append(shift)
    lane = iota((8, LANES), 0)
    grid = jnp.where(lane == 0, grids[0], jnp.where(lane == 1, grids[1], jnp.where(lane == 2, grids[2], 0.0)))
    picks = jnp.concatenate([here[6:7], here[7:8], here[8:9]], axis=1).astype(jnp.int32)
    orbital = iota((1, TILE), 1)
    atom_row = picks // 4
    atom_col = 4 * (orbital // ORBD) + picks % 4
    onehot = (iota((LANES, TILE), 0) == atom_col).astype(F32)
    by_row = jnp.dot(grid, onehot, precision=HIGH, preferred_element_type=F32)
    return jnp.sum(jnp.where(iota((8, TILE), 0) == atom_row, by_row, 0.0), axis=0, keepdims=True)


def initial_kernel(strips, coupling, mask, bare, inter, out):
    row = lax.axis_index("row")
    col = lax.axis_index("col")
    along_cols = row_shift(strips, coupling, col)
    along_rows = jnp.broadcast_to(row_shift(strips, coupling, row), (LANES, TILE)).T[:, :1]
    block = iota((1, TILE), 1) // BLK
    diagonal = jnp.where(row == col, 0.5, 0.0)
    for i in range(TILE // BLK):
        rows = slice(i * BLK, (i + 1) * BLK)
        keep = jnp.zeros((1, TILE), F32)
        for j in range(TILE // BLK):
            keep = jnp.where(block == j, mask[i, j].astype(F32), keep)
        ham = bare[rows, :].astype(F32) + 0.5 * inter[rows, :].astype(F32) * (along_rows[rows] + along_cols)
        eye = jnp.where(iota((BLK, TILE), 0) + i * BLK == iota((BLK, TILE), 1), diagonal, 0.0)
        out[rows, :] = (eye - keep * ham).astype(jnp.bfloat16)


def initial_tile(strips, coupling, mask, bare, inter):
    return pl.pallas_call(
        initial_kernel,
        out_shape=jax.ShapeDtypeStruct((TILE, TILE), jnp.bfloat16),
        in_specs=[VMEM, SMEM, SMEM, VMEM, VMEM],
        out_specs=VMEM,
        compiler_params=pltpu.CompilerParams(vmem_limit_bytes=32 << 20),
    )(strips, coupling, mask, bare, inter)


def ring_step(value, by):
    return lax.ppermute(value, "row", [(h * RING + i, h * RING + (i + by) % RING) for h in range(2) for i in range(RING)])


def column_tiles(tile):
    other = lax.ppermute(tile, "row", [(i, i ^ RING) for i in range(NROW)])
    found = [(0, 0, tile), (1, 0, other)]
    up, down = [tile, other], [tile, other]
    for step in (1, 2, 3):
        for half in (0, 1):
            up[half] = ring_step(up[half], 1)
            down[half] = ring_step(down[half], -1)
            found += [(half, step, up[half]), (half, -step, down[half])]
    found.append((0, 4, ring_step(up[0], 1)))
    found.append((1, -4, ring_step(down[1], -1)))
    return found


CHUNK = 4


def load(strip_ref, tile_refs, places, strip, column, sems):
    row = lax.axis_index("row")
    half, z = row // RING, row % RING
    copies = [pltpu.make_async_copy(strip_ref, strip, sems.at[0])]
    for n, (ref, (flip, distance)) in enumerate(zip(tile_refs, places)):
        k = (half + flip) % 2 * RING + (z - distance + RING) % RING
        to = column.at[pl.ds(pl.multiple_of(k * TILE, TILE), TILE), :]
        copies.append(pltpu.make_async_copy(ref, to, sems.at[n + 1]))
    for copy in copies:
        copy.start()
    for copy in copies:
        copy.wait()


def product(strip, column, acc):
    span = CHUNK * TILE
    for k in range(NROW // CHUNK):
        part = jnp.dot(strip[:, k * span : (k + 1) * span], column[k * span : (k + 1) * span, :], preferred_element_type=F32)
        if k == 0:
            acc[...] = part
        else:
            acc[...] += part


def square_kernel(places, strip_ref, *refs):
    tile_refs, (full, half, strip, column, sems) = refs[:NROW], refs[NROW:]
    load(strip_ref, tile_refs, places, strip, column, sems)
    product(strip, column, full)
    half[...] = full[...].astype(jnp.bfloat16)


def cube_kernel(places, strip_ref, square, *refs):
    tile_refs, (out, strip, column, acc, sems) = refs[:NROW], refs[NROW:]
    load(strip_ref, tile_refs, places, strip, column, sems)
    product(strip, column, acc)
    out[...] = 3.0 * square[...] - 2.0 * acc[...]


SCRATCH = [
    pltpu.VMEM((TILE, NROW * TILE), jnp.bfloat16),
    pltpu.VMEM((NROW * TILE, TILE), jnp.bfloat16),
]
SEMS = pltpu.SemaphoreType.DMA((NROW + 1,))
PARAMS = pltpu.CompilerParams(vmem_limit_bytes=40 << 20)
COST = pl.CostEstimate(flops=2 * TILE * TILE * TILE * NROW, bytes_accessed=4 * TILE * TILE * NROW, transcendentals=0)


def square_of(strip, tiles, places):
    return pl.pallas_call(
        functools.partial(square_kernel, places),
        out_shape=[jax.ShapeDtypeStruct((TILE, TILE), F32), jax.ShapeDtypeStruct((TILE, TILE), jnp.bfloat16)],
        in_specs=[ANY] * (1 + NROW),
        out_specs=[VMEM, VMEM],
        scratch_shapes=SCRATCH + [SEMS],
        compiler_params=PARAMS,
        cost_estimate=COST,
    )(strip, *tiles)


def purified_of(strip, square, tiles, places):
    return pl.pallas_call(
        functools.partial(cube_kernel, places),
        out_shape=jax.ShapeDtypeStruct((TILE, TILE), F32),
        in_specs=[ANY, VMEM] + [ANY] * NROW,
        out_specs=VMEM,
        scratch_shapes=SCRATCH + [pltpu.VMEM((TILE, TILE), F32), SEMS],
        compiler_params=PARAMS,
        cost_estimate=COST,
    )(strip, square, *tiles)


def per_device(charges, hubbard, coupling, orbital_atom, block_mask, bare_ham, intersection):
    packed = pack(charges, hubbard, orbital_atom)
    strip = sum_parts(everywhere(packed, "col"))
    strips = everywhere(strip, "row")
    initial = initial_tile(strips, coupling, block_mask, bare_ham, intersection)
    initial_strip = lax.all_gather(initial, "col", axis=1, tiled=True)
    found = column_tiles(initial)
    places = tuple((half, distance) for half, distance, _ in found)
    tiles = [tile for _, _, tile in found]
    square, square_half = square_of(initial_strip, tiles, places)
    square_strip = lax.all_gather(square_half, "col", axis=1, tiled=True)
    return purified_of(square_strip, square, tiles, places)


def solution(mesh):
    placed = (
        P("row", "col"),
        P("row", "col"),
        P(),
        P("row", "col", None),
        P("row", "col"),
        P("row", "col"),
        P("row", "col"),
    )
    return jax.shard_map(
        per_device, mesh=mesh, in_specs=placed, out_specs=P("row", "col"), check_vma=False
    )
```

time: 315 us -> 172 us (0.55)
  waiting for transfers between devices: 183 us -> 70.3 us
  blocking collectives: 77.3 us -> 32.1 us
  local copies, waits for them, and re-layouts: 3.51 us -> 19.9 us
  matrix products: 14.3 us -> 0 us
  Pallas kernels: 0 us -> 14 us
  other arithmetic: 12.2 us -> 0 us
  starting transfers between devices: 11.1 us -> 21.2 us
    all_gather x1 -> x0, waiting for transfers between devices: 103 us -> none  [strip_product(): lax.all_gather(right_tile, 'row', axis=0, tiled=True)]
    unnamed x1 -> x0, blocking collectives: 77.3 us -> none
    all_gather x1, waiting for transfers between devices: 35.4 us -> 0.01 us  [per_device(): initial_strip = lax.all_gather(initial, 'col', axis=1, tiled=True)]
    all_to_all x0 -> x2, blocking collectives: none -> 32.1 us  [everywhere(): return lax.all_to_all(copies, axis, 0, 0)]
    ppermute x4 -> x15, waiting for transfers between devices: 2.56 us -> 28.6 us  [the longest x14 22.4 us: ring_step(): lax.ppermute(value, 'row', [(h * RING + i, h * RING + (i + by) % RING) fo...]
    unnamed x2 -> x36, local copies, waits for them, and re-layouts: 0.28 us -> 18.5 us
    dot_general x2 -> x0, matrix products: 14.3 us -> none  [strip_product(): jnp.dot(left_strip, lax.all_gather(right_tile, 'row', axis=0, tiled=True)...]
    pallas_call x0 -> x5, Pallas kernels: none -> 14 us  [the longest x1 4.92 us: purified_of(): pl.pallas_call(functools.partial(cube_kernel, places), out_shape=jax.Shap...]
  transfers between devices with their start and end apart: 7 -> 17, of which waited for: 4 -> 10; matrix products, arithmetic and copies ran while one was open for 1% -> 0% of each run, Pallas kernels for 0% -> 0%
where the time goes in v1:
time: 172 us; the launch traced here: 171 us
  waiting for transfers between devices  70.3 us (41%)
  blocking collectives  32.1 us (19%)
  starting transfers between devices  21.2 us (12%)
  local copies, waits for them, and re-layouts  19.9 us (12%)
  Pallas kernels  14 us (8%)
  between operations  13.5 us (8%)
    all_gather x1, waiting for transfers between devices, per_device(): square_strip = lax.all_gather(square_half, 'col', axis=1, tiled=True)  41.7 us
    all_to_all x2, blocking collectives, everywhere(): return lax.all_to_all(copies, axis, 0, 0)  32.1 us
    ppermute x14, waiting for transfers between devices, ring_step(): lax.ppermute(value, 'row', [(h * RING + i, h * RING + (i + by) % RING) fo...  22.4 us
    ppermute x14, starting transfers between devices, ring_step(): lax.ppermute(value, 'row', [(h * RING + i, h * RING + (i + by) % RING) fo...  20.2 us
    unnamed x36, local copies, waits for them, and re-layouts  18.5 us
    ppermute x1, waiting for transfers between devices, column_tiles(): other = lax.ppermute(tile, 'row', [(i, i ^ RING) for i in range(NROW)])  6.22 us
    pallas_call x1, Pallas kernels, purified_of(): pl.pallas_call(functools.partial(cube_kernel, places), out_shape=jax.Shap...  4.92 us
    pallas_call x1, Pallas kernels, square_of(): pl.pallas_call(functools.partial(square_kernel, places), out_shape=[jax.S...  4.11 us
  transfers between devices with their start and end apart: 17, of which 10 were waited for; matrix products, arithmetic and copies ran while one was open for 0% of the time, Pallas kernels for 0%

profile of v1, /device:TPU:1, one launch (start us, length us, event | category | flops | bytes accessed | tf_op | source)
XLA Modules:
  0.0 171.1 jit_solution(16569467358780361608)
XLA Ops:
  6.5 1.4 shard_map.73
  7.9 0.7 broadcast_in_dim.4
  8.6 13.0 %all_to_all.10.parts = f32[16,16,128]{2,1,0:T(8,128)} all-to-all(f32[16,16,128]{2,1,0:T(8,128)S(1)} %broadcast_in_dim.4), channel_id=1, replica_groups=mesh['row'=16,'col'=16] {'col'}, dimensions={0} | all-to-all | bytes 262144 | tf_op jit(solution)/shard_map/all_to_all | solution.py:72
  21.6 1.5 shard_map.74
  23.1 0.7 broadcast_in_dim.5
  23.8 19.2 %all_to_all.11.strips = f32[16,16,128]{2,1,0:T(8,128)S(1)} all-to-all(f32[16,16,128]{2,1,0:T(8,128)S(1)} %broadcast_in_dim.5), channel_id=1, replica_groups=mesh['row'=16,'col'=16] {'row'}, dimensions={0} | all-to-all | bytes 262144 | tf_op jit(solution)/shard_map/all_to_all | solution.py:72
  43.0 1.0 copy-done.14
  44.0 1.0 copy-done.15
  44.9 0.7 copy-done.16
  45.6 0.7 copy-done.17
  46.3 2.1 %shard_map.75.refs_0_ = bf16[384,384]{1,0:T(8,128)(2,1)} custom-call(f32[16,16,128]{2,1,0:T(8,128)S(1)} %all_to_all.11.strips, f32[3,3]{1,0:T(4,128)S(1)} %copy-done.16, s32[4,4]{1,0:T(4,128)S(1)} %copy-done.17, bf16[384,384]{1,0:T(8,128)(2,1)S(1)} %copy-done.14, bf16[384,384]{1,0:T(8,128)(2,1)S(1)} %copy-done.15), custom_call_target="tpu_custom_call" | custom-call | tf_op jit(solution)/shard_map/pallas_call | solution.py:117
  48.4 1.0 collective-permute-start
  49.4 1.0 collective-permute-start.1
  50.4 6.2 %collective-permute-done.refs_1_ = bf16[384,384]{1,0:T(8,128)(2,1)S(1)} collective-permute-done((bf16[384,384]{1,0:T(8,128)(2,1)}, bf16[384,384]{1,0:T(8,128)(2,1)S(1)}, u32[]{:S(2)}, u32[]{:S(2)}) %collective-permute-start) | collective-permute-done | bytes 294944 | tf_op jit(solution)/shard_map/ppermute | solution.py:131
  56.6 1.6 collective-permute-start.4
  58.3 1.4 collective-permute-start.5
  59.8 2.9 %collective-permute-done.4.refs_5_ = bf16[384,384]{1,0:T(8,128)(2,1)S(1)} collective-permute-done((bf16[384,384]{1,0:T(8,128)(2,1)S(1)}, bf16[384,384]{1,0:T(8,128)(2,1)S(1)}, u32[]{:S(2)}, u32[]{:S(2)}) %collective-permute-start.4) | collective-permute-done | bytes 294944 | tf_op jit(solution)/shard_map/ppermute | solution.py:127
  62.7 2.3 %collective-permute-start.8 = (bf16[384,384]{1,0:T(8,128)(2,1)S(1)}, bf16[384,384]{1,0:T(8,128)(2,1)S(1)}, u32[]{:S(2)}, u32[]{:S(2)}) collective-permute-start(bf16[384,384]{1,0:T(8,128)(2,1)S(1)} %collective-permute-done.4.refs_5_), channel_id=1, source_target_pairs={{0,112},{16,0},{32,16},{48,32},{64,48},{80,64},{96,80},{112,96},{1... | collective-permute-start | bytes 884744 | tf_op jit(solution)/shard_map/ppermute | solution.py:127
  65.1 3.1 %collective-permute-done.2.refs_3_ = bf16[384,384]{1,0:T(8,128)(2,1)S(1)} collective-permute-done((bf16[384,384]{1,0:T(8,128)(2,1)}, bf16[384,384]{1,0:T(8,128)(2,1)S(1)}, u32[]{:S(2)}, u32[]{:S(2)}) %collective-permute-start.2) | collective-permute-done | bytes 294944 | tf_op jit(solution)/shard_map/ppermute | solution.py:127
  68.2 3.3 %collective-permute-start.6 = (bf16[384,384]{1,0:T(8,128)(2,1)S(1)}, bf16[384,384]{1,0:T(8,128)(2,1)S(1)}, u32[]{:S(2)}, u32[]{:S(2)}) collective-permute-start(bf16[384,384]{1,0:T(8,128)(2,1)S(1)} %collective-permute-done.2.refs_3_), channel_id=1, source_target_pairs={{0,112},{16,0},{32,16},{48,32},{64,48},{80,64},{96,80},{112,96},{1... | collective-permute-start | bytes 884744 | tf_op jit(solution)/shard_map/ppermute | solution.py:127
  71.5 0.1 collective-permute-start.7
  71.6 2.8 %collective-permute-done.8.refs_9_ = bf16[384,384]{1,0:T(8,128)(2,1)S(1)} collective-permute-done((bf16[384,384]{1,0:T(8,128)(2,1)S(1)}, bf16[384,384]{1,0:T(8,128)(2,1)S(1)}, u32[]{:S(2)}, u32[]{:S(2)}) %collective-permute-start.8) | collective-permute-done | bytes 294944 | tf_op jit(solution)/shard_map/ppermute | solution.py:127
  74.4 3.4 %collective-permute-start.12 = (bf16[384,384]{1,0:T(8,128)(2,1)S(1)}, bf16[384,384]{1,0:T(8,128)(2,1)S(1)}, u32[]{:S(2)}, u32[]{:S(2)}) collective-permute-start(bf16[384,384]{1,0:T(8,128)(2,1)S(1)} %collective-permute-done.8.refs_9_), channel_id=1, source_target_pairs={{0,112},{16,0},{32,16},{48,32},{64,48},{80,64},{96,80},{112,96},{1... | collective-permute-start | bytes 884744 | tf_op jit(solution)/shard_map/ppermute | solution.py:127
  77.8 2.9 %collective-permute-done.6.refs_7_ = bf16[384,384]{1,0:T(8,128)(2,1)S(1)} collective-permute-done((bf16[384,384]{1,0:T(8,128)(2,1)S(1)}, bf16[384,384]{1,0:T(8,128)(2,1)S(1)}, u32[]{:S(2)}, u32[]{:S(2)}) %collective-permute-start.6) | collective-permute-done | bytes 294944 | tf_op jit(solution)/shard_map/ppermute | solution.py:127
  80.7 3.4 %collective-permute-start.10 = (bf16[384,384]{1,0:T(8,128)(2,1)S(1)}, bf16[384,384]{1,0:T(8,128)(2,1)S(1)}, u32[]{:S(2)}, u32[]{:S(2)}) collective-permute-start(bf16[384,384]{1,0:T(8,128)(2,1)S(1)} %collective-permute-done.6.refs_7_), channel_id=1, source_target_pairs={{0,112},{16,0},{32,16},{48,32},{64,48},{80,64},{96,80},{112,96},{1... | collective-permute-start | bytes 884744 | tf_op jit(solution)/shard_map/ppermute | solution.py:127
  84.2 0.1 collective-permute-start.11
  84.3 2.8 %collective-permute-done.12.refs_13_ = bf16[384,384]{1,0:T(8,128)(2,1)S(1)} collective-permute-done((bf16[384,384]{1,0:T(8,128)(2,1)S(1)}, bf16[384,384]{1,0:T(8,128)(2,1)S(1)}, u32[]{:S(2)}, u32[]{:S(2)}) %collective-permute-start.12) | collective-permute-done | bytes 294944 | tf_op jit(solution)/shard_map/ppermute | solution.py:127
  87.1 3.4 %collective-permute-start.14 = (bf16[384,384]{1,0:T(8,128)(2,1)S(1)}, bf16[384,384]{1,0:T(8,128)(2,1)S(1)}, u32[]{:S(2)}, u32[]{:S(2)}) collective-permute-start(bf16[384,384]{1,0:T(8,128)(2,1)S(1)} %collective-permute-done.12.refs_13_), channel_id=1, source_target_pairs={{0,112},{16,0},{32,16},{48,32},{64,48},{80,64},{96,80},{112,96},{1... | collective-permute-start | bytes 884744 | tf_op jit(solution)/shard_map/ppermute | solution.py:127
  90.5 2.9 %collective-permute-done.10.refs_11_ = bf16[384,384]{1,0:T(8,128)(2,1)S(1)} collective-permute-done((bf16[384,384]{1,0:T(8,128)(2,1)S(1)}, bf16[384,384]{1,0:T(8,128)(2,1)S(1)}, u32[]{:S(2)}, u32[]{:S(2)}) %collective-permute-start.10) | collective-permute-done | bytes 294944 | tf_op jit(solution)/shard_map/ppermute | solution.py:127
  93.4 0.7 copy-done.2
  94.1 1.5 collective-permute-done.11.refs_12_
  95.6 0.7 copy-done.5
  96.3 3.4 %collective-permute-done.14.refs_15_ = bf16[384,384]{1,0:T(8,128)(2,1)S(1)} collective-permute-done((bf16[384,384]{1,0:T(8,128)(2,1)S(1)}, bf16[384,384]{1,0:T(8,128)(2,1)S(1)}, u32[]{:S(2)}, u32[]{:S(2)}) %collective-permute-start.14) | collective-permute-done | bytes 294944 | tf_op jit(solution)/shard_map/ppermute | solution.py:127
  99.7 0.7 copy-done.8
  100.4 2.3 %copy-done = bf16[384,6144]{1,0:T(8,128)(2,1)S(1)} copy-done((bf16[384,6144]{1,0:T(8,128)(2,1)S(1)}, bf16[384,6144]{1,0:T(8,128)(2,1)}, u32[]{:S(2)}) %copy-start) | copy-done | bytes 4718616
  102.8 1.0 copy-done.3
  103.7 1.0 copy-done.6
  104.7 1.0 copy-done.9
  105.7 4.1 %shard_map.76 = (f32[384,384]{1,0:T(8,128)S(1)}, bf16[384,384]{1,0:T(8,128)(2,1)S(1)}) custom-call(bf16[384,6144]{1,0:T(8,128)(2,1)S(1)} %copy-done, bf16[384,384]{1,0:T(8,128)(2,1)} %shard_map.75.refs_0_, bf16[384,384]{1,0:T(8,128)(2,1)S(1)} %collective-permute-done.refs_1_, bf16[384,384]{1,0:T(8,128)(2,1)S(1)} %collective-permute-done.1.refs_2_, ...), custom_call_target="tpu_custom_call" | custom-call | flops 1811939328 | bytes 9437184 | tf_op jit(solution)/shard_map/pallas_call | solution.py:195
  109.8 0.8 copy-done.11
  110.6 0.7 copy-done.13
  111.3 41.7 %all-gather.5.cloned.1.call-done.strip_ref = bf16[384,6144]{1,0:T(8,128)(2,1)} async-done(((bf16[384,384]{1,0:T(8,128)(2,1)}), bf16[384,6144]{1,0:T(8,128)(2,1)}) %all-gather.5.cloned.1.call-update) | async-done | bytes 4718608 | tf_op jit(solution)/shard_map/all_gather | solution.py:228
  153.0 2.3 %copy-done.1 = bf16[384,6144]{1,0:T(8,128)(2,1)S(1)} copy-done((bf16[384,6144]{1,0:T(8,128)(2,1)S(1)}, bf16[384,6144]{1,0:T(8,128)(2,1)}, u32[]{:S(2)}) %copy-start.1) | copy-done | bytes 4718616
  155.3 1.0 copy-done.4
  156.3 1.0 copy-done.7
  157.3 1.0 copy-done.10
  158.2 1.1 copy-done.12
  159.3 4.9 %shard_map.77 = f32[384,384]{1,0:T(8,128)} custom-call(bf16[384,6144]{1,0:T(8,128)(2,1)S(1)} %copy-done.1, f32[384,384]{1,0:T(8,128)S(1)} %copy-done.12, bf16[384,384]{1,0:T(8,128)(2,1)} %shard_map.75.refs_0_, bf16[384,384]{1,0:T(8,128)(2,1)S(1)} %collective-permute-done.refs_1_, bf16[384,384]{1,0:T(8,128)(2,1)S(1)} %collective-permute-done.1.refs_2_, ...), custom_call_target="tpu_custom_call" | custom-call | flops 1811939328 | bytes 9437184 | tf_op jit(solution)/shard_map/pallas_call | solution.py:207
  (33 shorter events, 0.2 us)
Async XLA Ops:
  6.5 93.9 %all-gather.3.cloned.1.call-start = ((), (), s32[]{:S(2)}) async-start(), calls=%async_computation.2 | async-start | bytes 5013504 | tf_op jit(solution)/shard_map/all_gather | solution.py:223
  43.0 1.0 copy-start.14
  44.0 1.0 copy-start.15
  44.9 0.7 copy-start.16
  45.6 0.7 copy-start.17
  48.4 104.6 %all-gather.5.cloned.1.call-start = ((), (), s32[]{:S(2)}) async-start(), calls=%async_computation.3 | async-start | bytes 5013504 | tf_op jit(solution)/shard_map/all_gather | solution.py:228
  48.4 8.2 %collective-permute-start = (bf16[384,384]{1,0:T(8,128)(2,1)}, bf16[384,384]{1,0:T(8,128)(2,1)S(1)}, u32[]{:S(2)}, u32[]{:S(2)}) collective-permute-start(bf16[384,384]{1,0:T(8,128)(2,1)} %shard_map.75.refs_0_), channel_id=1, source_target_pairs={{0,128},{16,144},{32,160},{48,176},{64,192},{80,208},{96,224},{112... | collective-permute-start | bytes 884744 | tf_op jit(solution)/shard_map/ppermute | solution.py:131
  49.4 8.9 %collective-permute-start.1 = (bf16[384,384]{1,0:T(8,128)(2,1)}, bf16[384,384]{1,0:T(8,128)(2,1)S(1)}, u32[]{:S(2)}, u32[]{:S(2)}) collective-permute-start(bf16[384,384]{1,0:T(8,128)(2,1)} %shard_map.75.refs_0_), channel_id=1, source_target_pairs={{0,16},{16,32},{32,48},{48,64},{64,80},{80,96},{96,112},{112,0},{1... | collective-permute-start | bytes 884744 | tf_op jit(solution)/shard_map/ppermute | solution.py:127
  56.6 6.1 %collective-permute-start.4 = (bf16[384,384]{1,0:T(8,128)(2,1)S(1)}, bf16[384,384]{1,0:T(8,128)(2,1)S(1)}, u32[]{:S(2)}, u32[]{:S(2)}) collective-permute-start(bf16[384,384]{1,0:T(8,128)(2,1)S(1)} %collective-permute-done.refs_1_), channel_id=1, source_target_pairs={{0,112},{16,0},{32,16},{48,32},{64,48},{80,64},{96,80},{112,96},{1... | collective-permute-start | bytes 884744 | tf_op jit(solution)/shard_map/ppermute | solution.py:127
  58.3 9.9 %collective-permute-start.2 = (bf16[384,384]{1,0:T(8,128)(2,1)}, bf16[384,384]{1,0:T(8,128)(2,1)S(1)}, u32[]{:S(2)}, u32[]{:S(2)}) collective-permute-start(bf16[384,384]{1,0:T(8,128)(2,1)} %shard_map.75.refs_0_), channel_id=1, source_target_pairs={{0,112},{16,0},{32,16},{48,32},{64,48},{80,64},{96,80},{112,96},{1... | collective-permute-start | bytes 884744 | tf_op jit(solution)/shard_map/ppermute | solution.py:127
  58.3 13.2 %collective-permute-start.5 = (bf16[384,384]{1,0:T(8,128)(2,1)S(1)}, bf16[384,384]{1,0:T(8,128)(2,1)S(1)}, u32[]{:S(2)}, u32[]{:S(2)}) collective-permute-start(bf16[384,384]{1,0:T(8,128)(2,1)S(1)} %collective-permute-done.1.refs_2_), channel_id=1, source_target_pairs={{0,16},{16,32},{32,48},{48,64},{64,80},{80,96},{96,112},{112,0},{1... | collective-permute-start | bytes 884744 | tf_op jit(solution)/shard_map/ppermute | solution.py:127
  59.8 11.8 %collective-permute-start.3 = (bf16[384,384]{1,0:T(8,128)(2,1)S(1)}, bf16[384,384]{1,0:T(8,128)(2,1)S(1)}, u32[]{:S(2)}, u32[]{:S(2)}) collective-permute-start(bf16[384,384]{1,0:T(8,128)(2,1)S(1)} %collective-permute-done.refs_1_), channel_id=1, source_target_pairs={{0,16},{16,32},{32,48},{48,64},{64,80},{80,96},{96,112},{112,0},{1... | collective-permute-start | bytes 884744 | tf_op jit(solution)/shard_map/ppermute | solution.py:127
  62.7 11.7 %collective-permute-start.8 = (bf16[384,384]{1,0:T(8,128)(2,1)S(1)}, bf16[384,384]{1,0:T(8,128)(2,1)S(1)}, u32[]{:S(2)}, u32[]{:S(2)}) collective-permute-start(bf16[384,384]{1,0:T(8,128)(2,1)S(1)} %collective-permute-done.4.refs_5_), channel_id=1, source_target_pairs={{0,112},{16,0},{32,16},{48,32},{64,48},{80,64},{96,80},{112,96},{1... | collective-permute-start | bytes 884744 | tf_op jit(solution)/shard_map/ppermute | solution.py:127
  68.2 12.5 %collective-permute-start.6 = (bf16[384,384]{1,0:T(8,128)(2,1)S(1)}, bf16[384,384]{1,0:T(8,128)(2,1)S(1)}, u32[]{:S(2)}, u32[]{:S(2)}) collective-permute-start(bf16[384,384]{1,0:T(8,128)(2,1)S(1)} %collective-permute-done.2.refs_3_), channel_id=1, source_target_pairs={{0,112},{16,0},{32,16},{48,32},{64,48},{80,64},{96,80},{112,96},{1... | collective-permute-start | bytes 884744 | tf_op jit(solution)/shard_map/ppermute | solution.py:127
  71.5 12.6 %collective-permute-start.9 = (bf16[384,384]{1,0:T(8,128)(2,1)S(1)}, bf16[384,384]{1,0:T(8,128)(2,1)S(1)}, u32[]{:S(2)}, u32[]{:S(2)}) collective-permute-start(bf16[384,384]{1,0:T(8,128)(2,1)S(1)} %collective-permute-done.5.refs_6_), channel_id=1, source_target_pairs={{0,16},{16,32},{32,48},{48,64},{64,80},{80,96},{96,112},{112,0},{1... | collective-permute-start | bytes 884744 | tf_op jit(solution)/shard_map/ppermute | solution.py:127
  71.5 12.6 %collective-permute-start.7 = (bf16[384,384]{1,0:T(8,128)(2,1)S(1)}, bf16[384,384]{1,0:T(8,128)(2,1)S(1)}, u32[]{:S(2)}, u32[]{:S(2)}) collective-permute-start(bf16[384,384]{1,0:T(8,128)(2,1)S(1)} %collective-permute-done.3.refs_4_), channel_id=1, source_target_pairs={{0,16},{16,32},{32,48},{48,64},{64,80},{80,96},{96,112},{112,0},{1... | collective-permute-start | bytes 884744 | tf_op jit(solution)/shard_map/ppermute | solution.py:127
  74.4 12.6 %collective-permute-start.12 = (bf16[384,384]{1,0:T(8,128)(2,1)S(1)}, bf16[384,384]{1,0:T(8,128)(2,1)S(1)}, u32[]{:S(2)}, u32[]{:S(2)}) collective-permute-start(bf16[384,384]{1,0:T(8,128)(2,1)S(1)} %collective-permute-done.8.refs_9_), channel_id=1, source_target_pairs={{0,112},{16,0},{32,16},{48,32},{64,48},{80,64},{96,80},{112,96},{1... | collective-permute-start | bytes 884744 | tf_op jit(solution)/shard_map/ppermute | solution.py:127
  80.7 12.6 %collective-permute-start.10 = (bf16[384,384]{1,0:T(8,128)(2,1)S(1)}, bf16[384,384]{1,0:T(8,128)(2,1)S(1)}, u32[]{:S(2)}, u32[]{:S(2)}) collective-permute-start(bf16[384,384]{1,0:T(8,128)(2,1)S(1)} %collective-permute-done.6.refs_7_), channel_id=1, source_target_pairs={{0,112},{16,0},{32,16},{48,32},{64,48},{80,64},{96,80},{112,96},{1... | collective-permute-start | bytes 884744 | tf_op jit(solution)/shard_map/ppermute | solution.py:127
  84.2 9.2 %collective-permute-start.13 = (bf16[384,384]{1,0:T(8,128)(2,1)S(1)}, bf16[384,384]{1,0:T(8,128)(2,1)S(1)}, u32[]{:S(2)}, u32[]{:S(2)}) collective-permute-start(bf16[384,384]{1,0:T(8,128)(2,1)S(1)} %collective-permute-done.9.refs_10_), channel_id=1, source_target_pairs={{0,16},{16,32},{32,48},{48,64},{64,80},{80,96},{96,112},{112,0},{1... | collective-permute-start | bytes 884744 | tf_op jit(solution)/shard_map/ppermute | solution.py:127
  84.2 11.4 %collective-permute-start.11 = (bf16[384,384]{1,0:T(8,128)(2,1)S(1)}, bf16[384,384]{1,0:T(8,128)(2,1)S(1)}, u32[]{:S(2)}, u32[]{:S(2)}) collective-permute-start(bf16[384,384]{1,0:T(8,128)(2,1)S(1)} %collective-permute-done.7.refs_8_), channel_id=1, source_target_pairs={{0,16},{16,32},{32,48},{48,64},{64,80},{80,96},{96,112},{112,0},{1... | collective-permute-start | bytes 884744 | tf_op jit(solution)/shard_map/ppermute | solution.py:127
  87.1 12.6 %collective-permute-start.14 = (bf16[384,384]{1,0:T(8,128)(2,1)S(1)}, bf16[384,384]{1,0:T(8,128)(2,1)S(1)}, u32[]{:S(2)}, u32[]{:S(2)}) collective-permute-start(bf16[384,384]{1,0:T(8,128)(2,1)S(1)} %collective-permute-done.12.refs_13_), channel_id=1, source_target_pairs={{0,112},{16,0},{32,16},{48,32},{64,48},{80,64},{96,80},{112,96},{1... | collective-permute-start | bytes 884744 | tf_op jit(solution)/shard_map/ppermute | solution.py:127
  93.4 0.7 copy-start.2
  95.6 0.7 copy-start.5
  99.7 0.7 copy-start.8
  100.4 2.3 %copy-start = (bf16[384,6144]{1,0:T(8,128)(2,1)S(1)}, bf16[384,6144]{1,0:T(8,128)(2,1)}, u32[]{:S(2)}) copy-start(bf16[384,6144]{1,0:T(8,128)(2,1)} %all-gather.3.cloned.1.call-done.strip_ref) | copy-start | bytes 14155780
  102.8 1.0 copy-start.3
  103.7 1.0 copy-start.6
  104.7 1.0 copy-start.9
  109.8 0.8 copy-start.11
  110.6 0.7 copy-start.13
  153.0 2.3 %copy-start.1 = (bf16[384,6144]{1,0:T(8,128)(2,1)S(1)}, bf16[384,6144]{1,0:T(8,128)(2,1)}, u32[]{:S(2)}) copy-start(bf16[384,6144]{1,0:T(8,128)(2,1)} %all-gather.5.cloned.1.call-done.strip_ref) | copy-start | bytes 14155780
  155.3 1.0 copy-start.4
  156.3 1.0 copy-start.7
  157.3 1.0 copy-start.10
  158.2 1.1 copy-start.12
Sparse Core Ops, SparseCore 0:
  48.5 36.3 all-gather.2
  111.4 41.5 all-gather.4

commit v2 on v1

--- a/solution.py
+++ b/solution.py
@@ -24,58 +24,89 @@
     return lax.broadcasted_iota(jnp.int32, shape, dim)
 
 
-def pack_kernel(charges, hubbard, picks, out):
+def position(index):
+    row, col = divmod(index, NROW)
+    return row // RING, row % RING, col // RING, col % RING // 2, col % 2
+
+
+def groups(key):
+    found = {}
+    for index in range(NROW * NROW):
+        found.setdefault(key(*position(index)), []).append(index)
+    return list(found.values())
+
+
+PLANE = groups(lambda xh, z, xl, y, core: (z, core))
+PILLAR = groups(lambda xh, z, xl, y, core: (xh, xl, y))
+
+
+def pack_kernel(charges, hubbard, picks, mask, out):
     col = lax.axis_index("col")
-    out[...] = jnp.zeros_like(out)
     spread = (iota((4, LANES), 1) % 64 == 4 * col + iota((4, LANES), 0)).astype(F32)
-    for first, ref in ((0, charges), (3, hubbard)):
-        for i in range(3):
+    rows = []
+    for ref, height in ((charges, 3), (hubbard, 3)):
+        for i in range(height):
             row = jnp.zeros((1, LANES), F32)
             for j in range(4):
                 row = row + spread[j : j + 1] * ref[i, j]
-            out[first + i : first + i + 1, :] = row
+            rows.append(row)
     for part in range(3):
         lane = iota((1, LANES), 1) + part * LANES
         row = jnp.zeros((1, LANES), F32)
         for o in range(ORBD):
             row = jnp.where(lane == ORBD * col + o, picks[0, 0, o].astype(F32), row)
-        out[6 + part : 7 + part, :] = row
-
-
-def pack(charges, hubbard, orbital_atom):
+        rows.append(row)
+    for i in range(4):
+        row = jnp.zeros((1, LANES), F32)
+        for j in range(4):
+            row = row + spread[j : j + 1] * mask[i, j].astype(F32)
+        rows.append(row)
+    rows += [jnp.zeros((1, LANES), F32)] * (16 - len(rows))
+    packed = jnp.concatenate(rows, axis=0)
+    for n in range(NROW):
+        out[n] = packed
+
+
+def pack(charges, hubbard, orbital_atom, block_mask):
     return pl.pallas_call(
         pack_kernel,
-        out_shape=jax.ShapeDtypeStruct((16, LANES), F32),
-        in_specs=[SMEM, SMEM, SMEM],
+        out_shape=jax.ShapeDtypeStruct((NROW, 16, LANES), F32),
+        in_specs=[SMEM, SMEM, SMEM, SMEM],
         out_specs=VMEM,
-    )(charges, hubbard, orbital_atom)
+    )(charges, hubbard, orbital_atom, block_mask)
 
 
 def sum_kernel(parts, out):
-    total = parts[0]
-    for i in range(1, NROW):
-        total = total + parts[i]
-    out[...] = total
+    for half in range(2):
+        total = parts[half * RING]
+        for i in range(1, RING):
+            total = total + parts[half * RING + i]
+        for n in range(NROW):
+            out[n, half] = total
 
 
 def sum_parts(parts):
     return pl.pallas_call(
         sum_kernel,
-        out_shape=jax.ShapeDtypeStruct(parts.shape[1:], F32),
+        out_shape=jax.ShapeDtypeStruct((NROW, 2, 16, LANES), F32),
         in_specs=[VMEM],
         out_specs=VMEM,
     )(parts)
 
 
-def everywhere(value, axis):
-    copies = jnp.broadcast_to(value[None], (NROW,) + value.shape)
-    return lax.all_to_all(copies, axis, 0, 0)
-
-
-def row_shift(strips, coupling, q):
-    above = strips[(q + NROW - 1) % NROW]
-    here = strips[q]
-    below = strips[(q + 1) % NROW]
+def exchange(copies, members):
+    return lax.all_to_all(copies, ("row", "col"), 0, 0, axis_index_groups=members)
+
+
+def domain_row(parts, q):
+    half, z = q // RING, q % RING
+    return parts[2 * z, half] + parts[2 * z + 1, half]
+
+
+def row_shift(parts, coupling, q):
+    above = domain_row(parts, (q + NROW - 1) % NROW)
+    here = domain_row(parts, q)
+    below = domain_row(parts, (q + 1) % NROW)
     atoms = [above[2:3], here[0:1], here[1:2], here[2:3], below[0:1]]
     rolled = [[pltpu.roll(v, 1, 1), v, pltpu.roll(v, LANES - 1, 1)] for v in atoms]
     grids = []
@@ -85,8 +116,8 @@
             for b in range(3):
                 shift = shift + coupling[a, b] * rolled[i + a][b]
         grids.append(shift)
-    lane = iota((8, LANES), 0)
-    grid = jnp.where(lane == 0, grids[0], jnp.where(lane == 1, grids[1], jnp.where(lane == 2, grids[2], 0.0)))
+    line = iota((8, LANES), 0)
+    grid = jnp.where(line == 0, grids[0], jnp.where(line == 1, grids[1], jnp.where(line == 2, grids[2], 0.0)))
     picks = jnp.concatenate([here[6:7], here[7:8], here[8:9]], axis=1).astype(jnp.int32)
     orbital = iota((1, TILE), 1)
     atom_row = picks // 4
@@ -96,39 +127,78 @@
     return jnp.sum(jnp.where(iota((8, TILE), 0) == atom_row, by_row, 0.0), axis=0, keepdims=True)
 
 
-def initial_kernel(strips, coupling, mask, bare, inter, out):
-    row = lax.axis_index("row")
-    col = lax.axis_index("col")
-    along_cols = row_shift(strips, coupling, col)
-    along_rows = jnp.broadcast_to(row_shift(strips, coupling, row), (LANES, TILE)).T[:, :1]
-    block = iota((1, TILE), 1) // BLK
-    diagonal = jnp.where(row == col, 0.5, 0.0)
+def as_column(shift):
+    return jnp.broadcast_to(shift, (LANES, TILE)).T
+
+
+def kept(parts, row, col):
+    blocks = domain_row(parts, row)[8:16]
+    onehot = (iota((LANES, TILE), 0) == 4 * col + iota((LANES, TILE), 1) // BLK).astype(F32)
+    return jnp.dot(blocks, onehot, preferred_element_type=F32)[1:5]
+
+
+def form(out, bare, inter, keep, down, along, diagonal):
     for i in range(TILE // BLK):
         rows = slice(i * BLK, (i + 1) * BLK)
-        keep = jnp.zeros((1, TILE), F32)
-        for j in range(TILE // BLK):
-            keep = jnp.where(block == j, mask[i, j].astype(F32), keep)
-        ham = bare[rows, :].astype(F32) + 0.5 * inter[rows, :].astype(F32) * (along_rows[rows] + along_cols)
+        ham = bare[rows, :].astype(F32) + 0.5 * inter[rows, :].astype(F32) * (down[rows, :1] + along)
         eye = jnp.where(iota((BLK, TILE), 0) + i * BLK == iota((BLK, TILE), 1), diagonal, 0.0)
-        out[rows, :] = (eye - keep * ham).astype(jnp.bfloat16)
-
-
-def initial_tile(strips, coupling, mask, bare, inter):
+        out[rows, :] = (eye - keep[i : i + 1] * ham).astype(jnp.bfloat16)
+
+
+def initial_kernel(parts, coupling, raw, other, out, out_other):
+    row, col = lax.axis_index("row"), lax.axis_index("col")
+    along = row_shift(parts, coupling, col)
+    for q, source, to in ((row, raw, out), ((row + RING) % NROW, other, out_other)):
+        down = as_column(row_shift(parts, coupling, q))
+        form(to, source.at[:, :TILE], source.at[:, TILE:], kept(parts, q, col), down, along, jnp.where(q == col, 0.5, 0.0))
+
+
+BIG = pltpu.CompilerParams(vmem_limit_bytes=56 << 20)
+
+
+def initial_tiles(parts, coupling, raw, other):
     return pl.pallas_call(
         initial_kernel,
-        out_shape=jax.ShapeDtypeStruct((TILE, TILE), jnp.bfloat16),
-        in_specs=[VMEM, SMEM, SMEM, VMEM, VMEM],
-        out_specs=VMEM,
-        compiler_params=pltpu.CompilerParams(vmem_limit_bytes=32 << 20),
-    )(strips, coupling, mask, bare, inter)
+        out_shape=[jax.ShapeDtypeStruct((TILE, TILE), jnp.bfloat16)] * 2,
+        in_specs=[VMEM, SMEM, VMEM, VMEM],
+        out_specs=[VMEM, VMEM],
+        compiler_params=BIG,
+    )(parts, coupling, raw, other)
+
+
+def strip_kernel(parts, coupling, after, raw, out, down):
+    row, col = lax.axis_index("row"), pl.program_id(0)
+
+    @pl.when(col == 0)
+    def _():
+        down[...] = as_column(row_shift(parts, coupling, row))
+
+    along = row_shift(parts, coupling, col)
+    form(out, raw.at[:, :TILE], raw.at[:, TILE:], kept(parts, row, col), down, along, jnp.where(row == col, 0.5, 0.0))
+
+
+def initial_strip_of(parts, coupling, raw_strip, after):
+    return pl.pallas_call(
+        strip_kernel,
+        grid=(NROW,),
+        out_shape=jax.ShapeDtypeStruct((TILE, NROW * TILE), jnp.bfloat16),
+        in_specs=[VMEM, SMEM, ANY, pl.BlockSpec((TILE, 2 * TILE), lambda k: (0, k))],
+        out_specs=pl.BlockSpec((TILE, TILE), lambda k: (0, k)),
+        scratch_shapes=[pltpu.VMEM((TILE, LANES), F32)],
+        compiler_params=BIG,
+        cost_estimate=pl.CostEstimate(flops=20 * TILE * TILE * NROW, bytes_accessed=6 * TILE * TILE * NROW, transcendentals=0),
+    )(parts, coupling, after, raw_strip)
 
 
 def ring_step(value, by):
     return lax.ppermute(value, "row", [(h * RING + i, h * RING + (i + by) % RING) for h in range(2) for i in range(RING)])
 
 
-def column_tiles(tile):
-    other = lax.ppermute(tile, "row", [(i, i ^ RING) for i in range(NROW)])
+def swap_half(value):
+    return lax.ppermute(value, "row", [(i, i ^ RING) for i in range(NROW)])
+
+
+def column_tiles(tile, other):
     found = [(0, 0, tile), (1, 0, other)]
     up, down = [tile, other], [tile, other]
     for step in (1, 2, 3):
@@ -138,7 +208,7 @@
             found += [(half, step, up[half]), (half, -step, down[half])]
     found.append((0, 4, ring_step(up[0], 1)))
     found.append((1, -4, ring_step(down[1], -1)))
-    return found
+    return found, up[1]
 
 
 CHUNK = 4
@@ -187,7 +257,6 @@
     pltpu.VMEM((NROW * TILE, TILE), jnp.bfloat16),
 ]
 SEMS = pltpu.SemaphoreType.DMA((NROW + 1,))
-PARAMS = pltpu.CompilerParams(vmem_limit_bytes=40 << 20)
 COST = pl.CostEstimate(flops=2 * TILE * TILE * TILE * NROW, bytes_accessed=4 * TILE * TILE * NROW, transcendentals=0)
 
 
@@ -198,7 +267,7 @@
         in_specs=[ANY] * (1 + NROW),
         out_specs=[VMEM, VMEM],
         scratch_shapes=SCRATCH + [SEMS],
-        compiler_params=PARAMS,
+        compiler_params=BIG,
         cost_estimate=COST,
     )(strip, *tiles)
 
@@ -210,18 +279,20 @@
         in_specs=[ANY, VMEM] + [ANY] * NROW,
         out_specs=VMEM,
         scratch_shapes=SCRATCH + [pltpu.VMEM((TILE, TILE), F32), SEMS],
-        compiler_params=PARAMS,
+        compiler_params=BIG,
         cost_estimate=COST,
     )(strip, square, *tiles)
 
 
 def per_device(charges, hubbard, coupling, orbital_atom, block_mask, bare_ham, intersection):
-    packed = pack(charges, hubbard, orbital_atom)
-    strip = sum_parts(everywhere(packed, "col"))
-    strips = everywhere(strip, "row")
-    initial = initial_tile(strips, coupling, block_mask, bare_ham, intersection)
-    initial_strip = lax.all_gather(initial, "col", axis=1, tiled=True)
-    found = column_tiles(initial)
+    raw = jnp.concatenate([bare_ham, intersection], axis=1)
+    raw_strip = lax.all_gather(raw, "col", axis=1, tiled=True)
+    raw_other = swap_half(raw)
+    parts = exchange(pack(charges, hubbard, orbital_atom, block_mask), PLANE)
+    parts = exchange(sum_parts(parts), PILLAR)
+    initial, initial_other = initial_tiles(parts, coupling, raw, raw_other)
+    found, late = column_tiles(initial, initial_other)
+    initial_strip = initial_strip_of(parts, coupling, raw_strip, late)
     places = tuple((half, distance) for half, distance, _ in found)
     tiles = [tile for _, _, tile in found]
     square, square_half = square_of(initial_strip, tiles, places)

time: 172 us -> 178 us (1.035)
  blocking collectives: 32.1 us -> 0 us
  Pallas kernels: 14 us -> 37.7 us
  starting transfers between devices: 21.2 us -> 40.9 us
  local copies, waits for them, and re-layouts: 19.9 us -> 5.54 us
  waiting for transfers between devices: 70.3 us -> 79.2 us
    all_to_all x2 -> x0, blocking collectives: 32.1 us -> none  [everywhere(): return lax.all_to_all(copies, axis, 0, 0)]
    all_to_all x0 -> x2, starting transfers between devices: none -> 19.3 us  [exchange(): lax.all_to_all(copies, ('row', 'col'), 0, 0, axis_index_groups=members)]
    pallas_call x3 -> x4, Pallas kernels: 4.96 us -> 22.2 us  [the longest x1 15.9 us: initial_strip_of(): pl.pallas_call(strip_kernel, grid=(NROW,), out_shape=jax.ShapeDtypeStruct...]
    unnamed x36 -> x33, local copies, waits for them, and re-layouts: 18.5 us -> 4.53 us
    all_to_all x0 -> x2, waiting for transfers between devices: none -> 13 us  [exchange(): lax.all_to_all(copies, ('row', 'col'), 0, 0, axis_index_groups=members)]
    ppermute x1, waiting for transfers between devices: 6.22 us -> 2.57 us  [swap_half(): return lax.ppermute(value, 'row', [(i, i ^ RING) for i in range(NROW)])]
    pallas_call x1, Pallas kernels: 4.92 us -> 8.27 us  [purified_of(): pl.pallas_call(functools.partial(cube_kernel, places), out_shape=jax.Shap...]
    pallas_call x1, Pallas kernels: 4.11 us -> 7.3 us  [square_of(): pl.pallas_call(functools.partial(square_kernel, places), out_shape=[jax.S...]
  transfers between devices with their start and end apart: 17 -> 19, of which waited for: 10 -> 10; matrix products, arithmetic and copies ran while one was open for 0% -> 0% of each run, Pallas kernels for 0% -> 13%
where the time goes in v2:
time: 178 us; the launch traced here: 177 us
  waiting for transfers between devices  79.2 us (44%)
  starting transfers between devices  40.9 us (23%)
  Pallas kernels  37.7 us (21%)
  between operations  13.6 us (8%)
  local copies, waits for them, and re-layouts  5.54 us (3%)
    all_gather x1, waiting for transfers between devices, per_device(): square_strip = lax.all_gather(square_half, 'col', axis=1, tiled=True)  42.6 us
    ppermute x14, waiting for transfers between devices, ring_step(): lax.ppermute(value, 'row', [(h * RING + i, h * RING + (i + by) % RING) fo...  21 us
    all_to_all x2, starting transfers between devices, exchange(): lax.all_to_all(copies, ('row', 'col'), 0, 0, axis_index_groups=members)  19.3 us
    ppermute x14, starting transfers between devices, ring_step(): lax.ppermute(value, 'row', [(h * RING + i, h * RING + (i + by) % RING) fo...  18.7 us
    pallas_call x1, Pallas kernels, initial_strip_of(): pl.pallas_call(strip_kernel, grid=(NROW,), out_shape=jax.ShapeDtypeStruct...  15.9 us
    all_to_all x2, waiting for transfers between devices, exchange(): lax.all_to_all(copies, ('row', 'col'), 0, 0, axis_index_groups=members)  13 us
    pallas_call x1, Pallas kernels, purified_of(): pl.pallas_call(functools.partial(cube_kernel, places), out_shape=jax.Shap...  8.27 us
    pallas_call x1, Pallas kernels, square_of(): pl.pallas_call(functools.partial(square_kernel, places), out_shape=[jax.S...  7.3 us
  transfers between devices with their start and end apart: 19, of which 10 were waited for; matrix products, arithmetic and copies ran while one was open for 0% of the time, Pallas kernels for 13%

profile of v2, /device:TPU:1, one launch (start us, length us, event | category | flops | bytes accessed | tf_op | source)
XLA Modules:
  0.0 176.9 jit_solution(9057881657438470848)
XLA Ops:
  6.5 1.0 constant_dynamic-update-slice_fusion.1
  7.5 1.0 constant_dynamic-update-slice_fusion.raw
  8.5 0.0 copy-start
  8.6 0.8 copy-done
  9.4 0.0 all-gather.3.cloned.1.call-update
  9.4 1.5 shard_map.73
  10.9 7.6 %all-to-all-start = ((f32[16,16,128]{2,1,0:T(8,128)}), f32[16,16,128]{2,1,0:T(8,128)S(1)}, u32[]{:S(2)}, u32[]{:S(2)}) async-start(f32[16,16,128]{2,1,0:T(8,128)} %shard_map.73), calls=%async_computation | async-start | bytes 262144 | tf_op jit(solution)/shard_map/all_to_all | solution.py:98
  18.5 2.9 %collective-permute-start = (bf16[384,768]{1,0:T(8,128)(2,1)}, bf16[384,768]{1,0:T(8,128)(2,1)S(1)}, u32[]{:S(2)}, u32[]{:S(2)}) collective-permute-start(bf16[384,768]{1,0:T(8,128)(2,1)} %copy-done), channel_id=1, source_target_pairs={{0,128},{16,144},{32,160},{48,176},{64,192},{80,208},{96,224},{112... | collective-permute-start | bytes 1769480 | tf_op jit(solution)/shard_map/ppermute | solution.py:198
  21.3 3.9 %all-to-all-done.parts = f32[16,16,128]{2,1,0:T(8,128)S(1)} async-done(((f32[16,16,128]{2,1,0:T(8,128)}), f32[16,16,128]{2,1,0:T(8,128)S(1)}, u32[]{:S(2)}, u32[]{:S(2)}) %all-to-all-start) | async-done | bytes 131104 | tf_op jit(solution)/shard_map/all_to_all | solution.py:98
  25.3 0.7 copy-done.15
  25.9 1.7 shard_map.74
  27.6 11.7 %all-to-all-start.1 = ((f32[16,2,16,128]{3,2,1,0:T(8,128)}), f32[16,2,16,128]{3,2,1,0:T(8,128)S(1)}, u32[]{:S(2)}, u32[]{:S(2)}) async-start(f32[16,2,16,128]{3,2,1,0:T(8,128)} %shard_map.74), calls=%async_computation.1 | async-start | bytes 524288 | tf_op jit(solution)/shard_map/all_to_all | solution.py:98
  39.3 0.0 all-gather.5.cloned.1.call-start
  39.3 2.6 %collective-permute-done.other = bf16[384,768]{1,0:T(8,128)(2,1)S(1)} collective-permute-done((bf16[384,768]{1,0:T(8,128)(2,1)}, bf16[384,768]{1,0:T(8,128)(2,1)S(1)}, u32[]{:S(2)}, u32[]{:S(2)}) %collective-permute-start) | collective-permute-done | bytes 589856 | tf_op jit(solution)/shard_map/ppermute | solution.py:198
  41.9 9.1 %all-to-all-done.1.parts = f32[16,2,16,128]{3,2,1,0:T(8,128)S(1)} async-done(((f32[16,2,16,128]{3,2,1,0:T(8,128)}), f32[16,2,16,128]{3,2,1,0:T(8,128)S(1)}, u32[]{:S(2)}, u32[]{:S(2)}) %all-to-all-start.1) | async-done | bytes 262176 | tf_op jit(solution)/shard_map/all_to_all | solution.py:98
  51.0 0.7 copy-done.2
  51.7 3.1 %shard_map.75 = (bf16[384,384]{1,0:T(8,128)(2,1)}, bf16[384,384]{1,0:T(8,128)(2,1)}) custom-call(f32[16,2,16,128]{3,2,1,0:T(8,128)} %copy-done.2, f32[3,3]{1,0:T(4,128)} %coupling.3, bf16[384,768]{1,0:T(8,128)(2,1)} %copy-done, bf16[384,768]{1,0:T(8,128)(2,1)} %copy-done.14), custom_call_target="tpu_custom_call" | custom-call | tf_op jit(solution)/shard_map/pallas_call | solution.py:160
  54.8 2.7 %collective-permute-start.6 = (bf16[384,384]{1,0:T(8,128)(2,1)}, bf16[384,384]{1,0:T(8,128)(2,1)S(1)}, u32[]{:S(2)}, u32[]{:S(2)}) collective-permute-start(bf16[384,384]{1,0:T(8,128)(2,1)} %get-tuple-element.9.refs_1_), channel_id=1, source_target_pairs={{0,112},{16,0},{32,16},{48,32},{64,48},{80,64},{96,80},{112,96},{1... | collective-permute-start | bytes 884744 | tf_op jit(solution)/shard_map/ppermute | solution.py:194
  57.5 0.0 collective-permute-start.1
  57.5 2.7 %collective-permute-start.5 = (bf16[384,384]{1,0:T(8,128)(2,1)}, bf16[384,384]{1,0:T(8,128)(2,1)S(1)}, u32[]{:S(2)}, u32[]{:S(2)}) collective-permute-start(bf16[384,384]{1,0:T(8,128)(2,1)} %get-tuple-element.10.refs_0_), channel_id=1, source_target_pairs={{0,112},{16,0},{32,16},{48,32},{64,48},{80,64},{96,80},{112,96},{1... | collective-permute-start | bytes 884744 | tf_op jit(solution)/shard_map/ppermute | solution.py:194
  60.2 2.8 %collective-permute-done.4.refs_2_ = bf16[384,384]{1,0:T(8,128)(2,1)S(1)} collective-permute-done((bf16[384,384]{1,0:T(8,128)(2,1)}, bf16[384,384]{1,0:T(8,128)(2,1)S(1)}, u32[]{:S(2)}, u32[]{:S(2)}) %collective-permute-start.4) | collective-permute-done | bytes 294944 | tf_op jit(solution)/shard_map/ppermute | solution.py:194
  63.0 1.0 collective-permute-start.7
  64.0 0.0 collective-permute-done.6.refs_5_
  64.0 1.7 collective-permute-start.9
  65.7 3.6 %collective-permute-done.1.refs_4_ = bf16[384,384]{1,0:T(8,128)(2,1)S(1)} collective-permute-done((bf16[384,384]{1,0:T(8,128)(2,1)}, bf16[384,384]{1,0:T(8,128)(2,1)S(1)}, u32[]{:S(2)}, u32[]{:S(2)}) %collective-permute-start.1) | collective-permute-done | bytes 294944 | tf_op jit(solution)/shard_map/ppermute | solution.py:194
  69.3 1.0 collective-permute-start.2
  70.3 0.0 collective-permute-done.5.refs_3_
  70.3 1.7 collective-permute-start.8
  72.0 3.6 %collective-permute-done.7.refs_6_ = bf16[384,384]{1,0:T(8,128)(2,1)S(1)} collective-permute-done((bf16[384,384]{1,0:T(8,128)(2,1)S(1)}, bf16[384,384]{1,0:T(8,128)(2,1)S(1)}, u32[]{:S(2)}, u32[]{:S(2)}) %collective-permute-start.7) | collective-permute-done | bytes 294944 | tf_op jit(solution)/shard_map/ppermute | solution.py:194
  75.6 0.7 collective-permute-start.10
  76.3 0.0 collective-permute-done.9.refs_9_
  76.3 2.0 %collective-permute-start.12 = (bf16[384,384]{1,0:T(8,128)(2,1)S(1)}, bf16[384,384]{1,0:T(8,128)(2,1)S(1)}, u32[]{:S(2)}, u32[]{:S(2)}) collective-permute-start(bf16[384,384]{1,0:T(8,128)(2,1)S(1)} %collective-permute-done.9.refs_9_), channel_id=1, source_target_pairs={{0,112},{16,0},{32,16},{48,32},{64,48},{80,64},{96,80},{112,96},{1... | collective-permute-start | bytes 884744 | tf_op jit(solution)/shard_map/ppermute | solution.py:194
  78.3 3.6 %collective-permute-done.2.refs_8_ = bf16[384,384]{1,0:T(8,128)(2,1)S(1)} collective-permute-done((bf16[384,384]{1,0:T(8,128)(2,1)S(1)}, bf16[384,384]{1,0:T(8,128)(2,1)S(1)}, u32[]{:S(2)}, u32[]{:S(2)}) %collective-permute-start.2) | collective-permute-done | bytes 294944 | tf_op jit(solution)/shard_map/ppermute | solution.py:194
  82.0 0.6 collective-permute-start.3
  82.5 0.0 collective-permute-done.8.refs_7_
  82.5 2.1 %collective-permute-start.11 = (bf16[384,384]{1,0:T(8,128)(2,1)S(1)}, bf16[384,384]{1,0:T(8,128)(2,1)S(1)}, u32[]{:S(2)}, u32[]{:S(2)}) collective-permute-start(bf16[384,384]{1,0:T(8,128)(2,1)S(1)} %collective-permute-done.8.refs_7_), channel_id=1, source_target_pairs={{0,112},{16,0},{32,16},{48,32},{64,48},{80,64},{96,80},{112,96},{1... | collective-permute-start | bytes 884744 | tf_op jit(solution)/shard_map/ppermute | solution.py:194
  84.6 3.6 %collective-permute-done.10.refs_10_ = bf16[384,384]{1,0:T(8,128)(2,1)S(1)} collective-permute-done((bf16[384,384]{1,0:T(8,128)(2,1)S(1)}, bf16[384,384]{1,0:T(8,128)(2,1)S(1)}, u32[]{:S(2)}, u32[]{:S(2)}) %collective-permute-start.10) | collective-permute-done | bytes 294944 | tf_op jit(solution)/shard_map/ppermute | solution.py:194
  88.3 0.6 collective-permute-start.13
  88.8 2.1 %collective-permute-start.14 = (bf16[384,384]{1,0:T(8,128)(2,1)S(1)}, bf16[384,384]{1,0:T(8,128)(2,1)}, u32[]{:S(2)}, u32[]{:S(2)}) collective-permute-start(bf16[384,384]{1,0:T(8,128)(2,1)S(1)} %collective-permute-done.12.refs_13_), channel_id=1, source_target_pairs={{0,112},{16,0},{32,16},{48,32},{64,48},{80,64},{96,80},{112,96},{1... | collective-permute-start | bytes 884744 | tf_op jit(solution)/shard_map/ppermute | solution.py:194
  91.0 3.6 %collective-permute-done.3.after.refs_12_ = bf16[384,384]{1,0:T(8,128)(2,1)S(1)} collective-permute-done((bf16[384,384]{1,0:T(8,128)(2,1)S(1)}, bf16[384,384]{1,0:T(8,128)(2,1)S(1)}, u32[]{:S(2)}, u32[]{:S(2)}) %collective-permute-start.3) | collective-permute-done | bytes 294944 | tf_op jit(solution)/shard_map/ppermute | solution.py:194
  94.6 0.7 copy-done.1
  95.3 15.9 %shard_map.76.strip_ref = bf16[384,6144]{1,0:T(8,128)(2,1)} custom-call(f32[16,2,16,128]{3,2,1,0:T(8,128)} %copy-done.2, f32[3,3]{1,0:T(4,128)} %coupling.3, bf16[384,384]{1,0:T(8,128)(2,1)} %copy-done.1, bf16[384,12288]{1,0:T(8,128)(2,1)} %all-gather.3.cloned.1.call-done.raw), custom_call_target="tpu_custom_call" | custom-call | flops 47185920 | bytes 14155776 | tf_op jit(solution)/shard_map/pallas_call | solution.py:181
  111.2 0.0 collective-permute-done.11.refs_11_
  111.3 0.6 copy-done.13
  111.9 7.3 %shard_map.77 = (f32[384,384]{1,0:T(8,128)}, bf16[384,384]{1,0:T(8,128)(2,1)}) custom-call(bf16[384,6144]{1,0:T(8,128)(2,1)} %shard_map.76.strip_ref, bf16[384,384]{1,0:T(8,128)(2,1)} %get-tuple-element.10.refs_0_, bf16[384,384]{1,0:T(8,128)(2,1)} %get-tuple-element.9.refs_1_, bf16[384,384]{1,0:T(8,128)(2,1)} %copy-done.3, bf16[384,384]{1,0:T(8,128)(2,1)} %copy-done.6, ...), custom_call_target="tpu_custom_call" | custom-call | flops 1811939328 | bytes 9437184 | tf_op jit(solution)/shard_map/pallas_call | solution.py:264
  119.2 0.0 all-gather.5.cloned.1.call-update
  119.2 42.6 %all-gather.5.cloned.1.call-done.strip_ref = bf16[384,6144]{1,0:T(8,128)(2,1)} async-done(((bf16[384,384]{1,0:T(8,128)(2,1)}), bf16[384,6144]{1,0:T(8,128)(2,1)}) %all-gather.5.cloned.1.call-update) | async-done | bytes 4718608 | tf_op jit(solution)/shard_map/all_gather | solution.py:299
  161.8 8.3 %shard_map.78 = f32[384,384]{1,0:T(8,128)} custom-call(bf16[384,6144]{1,0:T(8,128)(2,1)} %all-gather.5.cloned.1.call-done.strip_ref, f32[384,384]{1,0:T(8,128)} %get-tuple-element.12.square, bf16[384,384]{1,0:T(8,128)(2,1)} %get-tuple-element.10.refs_0_, bf16[384,384]{1,0:T(8,128)(2,1)} %get-tuple-element.9.refs_1_, bf16[384,384]{1,0:T(8,128)(2,1)} %copy-done.3, ...), custom_call_target="tpu_custom_call" | custom-call | flops 1811939328 | bytes 9437184 | tf_op jit(solution)/shard_map/pallas_call | solution.py:276
  (32 shorter events, 0.1 us)
Async XLA Ops:
  6.5 88.1 %all-gather.3.cloned.1.call-start = ((), (), s32[]{:S(2)}) async-start(), calls=%async_computation.2 | async-start | bytes 10027008 | tf_op jit(solution)/shard_map/all_gather | solution.py:289
  8.5 0.8 copy-start
  10.9 14.4 %all-to-all-start = ((f32[16,16,128]{2,1,0:T(8,128)}), f32[16,16,128]{2,1,0:T(8,128)S(1)}, u32[]{:S(2)}, u32[]{:S(2)}) async-start(f32[16,16,128]{2,1,0:T(8,128)} %shard_map.73), calls=%async_computation | async-start | bytes 262144 | tf_op jit(solution)/shard_map/all_to_all | solution.py:98
  18.5 23.4 %collective-permute-start = (bf16[384,768]{1,0:T(8,128)(2,1)}, bf16[384,768]{1,0:T(8,128)(2,1)S(1)}, u32[]{:S(2)}, u32[]{:S(2)}) collective-permute-start(bf16[384,768]{1,0:T(8,128)(2,1)} %copy-done), channel_id=1, source_target_pairs={{0,128},{16,144},{32,160},{48,176},{64,192},{80,208},{96,224},{112... | collective-permute-start | bytes 1769480 | tf_op jit(solution)/shard_map/ppermute | solution.py:198
  25.3 0.7 copy-start.15
  27.6 23.4 %all-to-all-start.1 = ((f32[16,2,16,128]{3,2,1,0:T(8,128)}), f32[16,2,16,128]{3,2,1,0:T(8,128)S(1)}, u32[]{:S(2)}, u32[]{:S(2)}) async-start(f32[16,2,16,128]{3,2,1,0:T(8,128)} %shard_map.74), calls=%async_computation.1 | async-start | bytes 524288 | tf_op jit(solution)/shard_map/all_to_all | solution.py:98
  39.3 122.5 %all-gather.5.cloned.1.call-start = ((), (), s32[]{:S(2)}) async-start(), calls=%async_computation.3 | async-start | bytes 5013504 | tf_op jit(solution)/shard_map/all_gather | solution.py:299
  41.9 9.1 %copy-start.14 = (bf16[384,768]{1,0:T(8,128)(2,1)}, bf16[384,768]{1,0:T(8,128)(2,1)S(1)}, u32[]{:S(2)}) copy-start(bf16[384,768]{1,0:T(8,128)(2,1)S(1)} %collective-permute-done.other) | copy-start | bytes 1769476
  51.0 0.7 copy-start.2
  54.8 8.2 %collective-permute-start.4 = (bf16[384,384]{1,0:T(8,128)(2,1)}, bf16[384,384]{1,0:T(8,128)(2,1)S(1)}, u32[]{:S(2)}, u32[]{:S(2)}) collective-permute-start(bf16[384,384]{1,0:T(8,128)(2,1)} %get-tuple-element.10.refs_0_), channel_id=1, source_target_pairs={{0,16},{16,32},{32,48},{48,64},{64,80},{80,96},{96,112},{112,0},{1... | collective-permute-start | bytes 884744 | tf_op jit(solution)/shard_map/ppermute | solution.py:194
  54.8 9.2 %collective-permute-start.6 = (bf16[384,384]{1,0:T(8,128)(2,1)}, bf16[384,384]{1,0:T(8,128)(2,1)S(1)}, u32[]{:S(2)}, u32[]{:S(2)}) collective-permute-start(bf16[384,384]{1,0:T(8,128)(2,1)} %get-tuple-element.9.refs_1_), channel_id=1, source_target_pairs={{0,112},{16,0},{32,16},{48,32},{64,48},{80,64},{96,80},{112,96},{1... | collective-permute-start | bytes 884744 | tf_op jit(solution)/shard_map/ppermute | solution.py:194
  57.5 11.8 %collective-permute-start.1 = (bf16[384,384]{1,0:T(8,128)(2,1)}, bf16[384,384]{1,0:T(8,128)(2,1)S(1)}, u32[]{:S(2)}, u32[]{:S(2)}) collective-permute-start(bf16[384,384]{1,0:T(8,128)(2,1)} %get-tuple-element.9.refs_1_), channel_id=1, source_target_pairs={{0,16},{16,32},{32,48},{48,64},{64,80},{80,96},{96,112},{112,0},{1... | collective-permute-start | bytes 884744 | tf_op jit(solution)/shard_map/ppermute | solution.py:194
  57.5 12.8 %collective-permute-start.5 = (bf16[384,384]{1,0:T(8,128)(2,1)}, bf16[384,384]{1,0:T(8,128)(2,1)S(1)}, u32[]{:S(2)}, u32[]{:S(2)}) collective-permute-start(bf16[384,384]{1,0:T(8,128)(2,1)} %get-tuple-element.10.refs_0_), channel_id=1, source_target_pairs={{0,112},{16,0},{32,16},{48,32},{64,48},{80,64},{96,80},{112,96},{1... | collective-permute-start | bytes 884744 | tf_op jit(solution)/shard_map/ppermute | solution.py:194
  63.0 48.2 %copy-start.3 = (bf16[384,384]{1,0:T(8,128)(2,1)}, bf16[384,384]{1,0:T(8,128)(2,1)S(1)}, u32[]{:S(2)}) copy-start(bf16[384,384]{1,0:T(8,128)(2,1)S(1)} %collective-permute-done.4.refs_2_) | copy-start | bytes 884740
  63.0 12.6 %collective-permute-start.7 = (bf16[384,384]{1,0:T(8,128)(2,1)S(1)}, bf16[384,384]{1,0:T(8,128)(2,1)S(1)}, u32[]{:S(2)}, u32[]{:S(2)}) collective-permute-start(bf16[384,384]{1,0:T(8,128)(2,1)S(1)} %collective-permute-done.4.refs_2_), channel_id=1, source_target_pairs={{0,16},{16,32},{32,48},{48,64},{64,80},{80,96},{96,112},{112,0},{1... | collective-permute-start | bytes 884744 | tf_op jit(solution)/shard_map/ppermute | solution.py:194
  64.0 47.2 %copy-start.4 = (bf16[384,384]{1,0:T(8,128)(2,1)}, bf16[384,384]{1,0:T(8,128)(2,1)S(1)}, u32[]{:S(2)}) copy-start(bf16[384,384]{1,0:T(8,128)(2,1)S(1)} %collective-permute-done.6.refs_5_) | copy-start | bytes 884740
  64.0 12.3 %collective-permute-start.9 = (bf16[384,384]{1,0:T(8,128)(2,1)S(1)}, bf16[384,384]{1,0:T(8,128)(2,1)S(1)}, u32[]{:S(2)}, u32[]{:S(2)}) collective-permute-start(bf16[384,384]{1,0:T(8,128)(2,1)S(1)} %collective-permute-done.6.refs_5_), channel_id=1, source_target_pairs={{0,112},{16,0},{32,16},{48,32},{64,48},{80,64},{96,80},{112,96},{1... | collective-permute-start | bytes 884744 | tf_op jit(solution)/shard_map/ppermute | solution.py:194
  69.3 41.9 %copy-start.5 = (bf16[384,384]{1,0:T(8,128)(2,1)}, bf16[384,384]{1,0:T(8,128)(2,1)S(1)}, u32[]{:S(2)}) copy-start(bf16[384,384]{1,0:T(8,128)(2,1)S(1)} %collective-permute-done.1.refs_4_) | copy-start | bytes 884740
  69.3 12.6 %collective-permute-start.2 = (bf16[384,384]{1,0:T(8,128)(2,1)S(1)}, bf16[384,384]{1,0:T(8,128)(2,1)S(1)}, u32[]{:S(2)}, u32[]{:S(2)}) collective-permute-start(bf16[384,384]{1,0:T(8,128)(2,1)S(1)} %collective-permute-done.1.refs_4_), channel_id=1, source_target_pairs={{0,16},{16,32},{32,48},{48,64},{64,80},{80,96},{96,112},{112,0},{1... | collective-permute-start | bytes 884744 | tf_op jit(solution)/shard_map/ppermute | solution.py:194
  70.3 40.9 %copy-start.6 = (bf16[384,384]{1,0:T(8,128)(2,1)}, bf16[384,384]{1,0:T(8,128)(2,1)S(1)}, u32[]{:S(2)}) copy-start(bf16[384,384]{1,0:T(8,128)(2,1)S(1)} %collective-permute-done.5.refs_3_) | copy-start | bytes 884740
  70.3 12.2 %collective-permute-start.8 = (bf16[384,384]{1,0:T(8,128)(2,1)S(1)}, bf16[384,384]{1,0:T(8,128)(2,1)S(1)}, u32[]{:S(2)}, u32[]{:S(2)}) collective-permute-start(bf16[384,384]{1,0:T(8,128)(2,1)S(1)} %collective-permute-done.5.refs_3_), channel_id=1, source_target_pairs={{0,112},{16,0},{32,16},{48,32},{64,48},{80,64},{96,80},{112,96},{1... | collective-permute-start | bytes 884744 | tf_op jit(solution)/shard_map/ppermute | solution.py:194
  75.6 35.6 %copy-start.7 = (bf16[384,384]{1,0:T(8,128)(2,1)}, bf16[384,384]{1,0:T(8,128)(2,1)S(1)}, u32[]{:S(2)}) copy-start(bf16[384,384]{1,0:T(8,128)(2,1)S(1)} %collective-permute-done.7.refs_6_) | copy-start | bytes 884740
  75.6 12.6 %collective-permute-start.10 = (bf16[384,384]{1,0:T(8,128)(2,1)S(1)}, bf16[384,384]{1,0:T(8,128)(2,1)S(1)}, u32[]{:S(2)}, u32[]{:S(2)}) collective-permute-start(bf16[384,384]{1,0:T(8,128)(2,1)S(1)} %collective-permute-done.7.refs_6_), channel_id=1, source_target_pairs={{0,16},{16,32},{32,48},{48,64},{64,80},{80,96},{96,112},{112,0},{1... | collective-permute-start | bytes 884744 | tf_op jit(solution)/shard_map/ppermute | solution.py:194
  76.3 35.0 %copy-start.8 = (bf16[384,384]{1,0:T(8,128)(2,1)}, bf16[384,384]{1,0:T(8,128)(2,1)S(1)}, u32[]{:S(2)}) copy-start(bf16[384,384]{1,0:T(8,128)(2,1)S(1)} %collective-permute-done.9.refs_9_) | copy-start | bytes 884740
  76.3 12.5 %collective-permute-start.12 = (bf16[384,384]{1,0:T(8,128)(2,1)S(1)}, bf16[384,384]{1,0:T(8,128)(2,1)S(1)}, u32[]{:S(2)}, u32[]{:S(2)}) collective-permute-start(bf16[384,384]{1,0:T(8,128)(2,1)S(1)} %collective-permute-done.9.refs_9_), channel_id=1, source_target_pairs={{0,112},{16,0},{32,16},{48,32},{64,48},{80,64},{96,80},{112,96},{1... | collective-permute-start | bytes 884744 | tf_op jit(solution)/shard_map/ppermute | solution.py:194
  81.9 29.3 %copy-start.9 = (bf16[384,384]{1,0:T(8,128)(2,1)}, bf16[384,384]{1,0:T(8,128)(2,1)S(1)}, u32[]{:S(2)}) copy-start(bf16[384,384]{1,0:T(8,128)(2,1)S(1)} %collective-permute-done.2.refs_8_) | copy-start | bytes 884740
  82.0 12.6 %collective-permute-start.3 = (bf16[384,384]{1,0:T(8,128)(2,1)S(1)}, bf16[384,384]{1,0:T(8,128)(2,1)S(1)}, u32[]{:S(2)}, u32[]{:S(2)}) collective-permute-start(bf16[384,384]{1,0:T(8,128)(2,1)S(1)} %collective-permute-done.2.refs_8_), channel_id=1, source_target_pairs={{0,16},{16,32},{32,48},{48,64},{64,80},{80,96},{96,112},{112,0},{1... | collective-permute-start | bytes 884744 | tf_op jit(solution)/shard_map/ppermute | solution.py:194
  82.5 28.8 %copy-start.10 = (bf16[384,384]{1,0:T(8,128)(2,1)}, bf16[384,384]{1,0:T(8,128)(2,1)S(1)}, u32[]{:S(2)}) copy-start(bf16[384,384]{1,0:T(8,128)(2,1)S(1)} %collective-permute-done.8.refs_7_) | copy-start | bytes 884740
  82.5 28.7 %collective-permute-start.11 = (bf16[384,384]{1,0:T(8,128)(2,1)S(1)}, bf16[384,384]{1,0:T(8,128)(2,1)S(1)}, u32[]{:S(2)}, u32[]{:S(2)}) collective-permute-start(bf16[384,384]{1,0:T(8,128)(2,1)S(1)} %collective-permute-done.8.refs_7_), channel_id=1, source_target_pairs={{0,112},{16,0},{32,16},{48,32},{64,48},{80,64},{96,80},{112,96},{1... | collective-permute-start | bytes 884744 | tf_op jit(solution)/shard_map/ppermute | solution.py:194
  88.3 23.0 %copy-start.11 = (bf16[384,384]{1,0:T(8,128)(2,1)}, bf16[384,384]{1,0:T(8,128)(2,1)S(1)}, u32[]{:S(2)}) copy-start(bf16[384,384]{1,0:T(8,128)(2,1)S(1)} %collective-permute-done.10.refs_10_) | copy-start | bytes 884740
  88.3 22.9 %collective-permute-start.13 = (bf16[384,384]{1,0:T(8,128)(2,1)S(1)}, bf16[384,384]{1,0:T(8,128)(2,1)}, u32[]{:S(2)}, u32[]{:S(2)}) collective-permute-start(bf16[384,384]{1,0:T(8,128)(2,1)S(1)} %collective-permute-done.10.refs_10_), channel_id=1, source_target_pairs={{0,16},{16,32},{32,48},{48,64},{64,80},{80,96},{96,112},{112,0},{1... | collective-permute-start | bytes 884744 | tf_op jit(solution)/shard_map/ppermute | solution.py:194
  88.8 22.5 %copy-start.12 = (bf16[384,384]{1,0:T(8,128)(2,1)}, bf16[384,384]{1,0:T(8,128)(2,1)S(1)}, u32[]{:S(2)}) copy-start(bf16[384,384]{1,0:T(8,128)(2,1)S(1)} %collective-permute-done.12.refs_13_) | copy-start | bytes 884740
  88.8 22.4 %collective-permute-start.14 = (bf16[384,384]{1,0:T(8,128)(2,1)S(1)}, bf16[384,384]{1,0:T(8,128)(2,1)}, u32[]{:S(2)}, u32[]{:S(2)}) collective-permute-start(bf16[384,384]{1,0:T(8,128)(2,1)S(1)} %collective-permute-done.12.refs_13_), channel_id=1, source_target_pairs={{0,112},{16,0},{32,16},{48,32},{64,48},{80,64},{96,80},{112,96},{1... | collective-permute-start | bytes 884744 | tf_op jit(solution)/shard_map/ppermute | solution.py:194
  94.6 0.7 copy-start.1
  111.2 0.7 copy-start.13
Sparse Core Ops, SparseCore 0:
  9.5 72.5 all-gather.2
  119.4 42.3 all-gather.4

commit v3 on v0

v3 whole, which is shorter than its diff:
```python
import functools

import jax
import jax.numpy as jnp
from jax import lax
from jax.experimental import pallas as pl
from jax.experimental.pallas import tpu as pltpu
from jax.sharding import PartitionSpec as P

BLK = 96
TILE = 384
NROW = 16
ORBD = 24
LANES = 128
RING = 8
HIGH = lax.Precision.HIGHEST
F32 = jnp.float32
VMEM = pl.BlockSpec(memory_space=pltpu.VMEM)
SMEM = pl.BlockSpec(memory_space=pltpu.SMEM)
ANY = pl.BlockSpec(memory_space=pl.ANY)


def iota(shape, dim):
    return lax.broadcasted_iota(jnp.int32, shape, dim)


def position(index):
    row, col = divmod(index, NROW)
    return row // RING, row % RING, col // RING, col % RING // 2, col % 2


def groups(key):
    found = {}
    for index in range(NROW * NROW):
        found.setdefault(key(*position(index)), []).append(index)
    return list(found.values())


PLANE = groups(lambda xh, z, xl, y, core: (z, core))
PILLAR = groups(lambda xh, z, xl, y, core: (xh, xl, y))


def pack_kernel(charges, hubbard, picks, mask, out):
    values = [charges[i, j] for i in range(3) for j in range(4)]
    values += [hubbard[i, j] for i in range(3) for j in range(4)]
    values += [picks[0, 0, o].astype(F32) for o in range(ORBD)]
    values += [mask[i, j].astype(F32) for i in range(4) for j in range(4)]
    lane = iota((1, LANES), 1)
    row = jnp.zeros((1, LANES), F32)
    for n, value in enumerate(values):
        row = jnp.where(lane == n, value, row)
    for n in range(NROW):
        out[n] = row


def pack(charges, hubbard, orbital_atom, block_mask):
    return pl.pallas_call(
        pack_kernel,
        out_shape=jax.ShapeDtypeStruct((NROW, 1, LANES), F32),
        in_specs=[SMEM, SMEM, SMEM, SMEM],
        out_specs=VMEM,
    )(charges, hubbard, orbital_atom, block_mask)


def copy_kernel(parts, bare_other, inter_other, out):
    rows = jnp.concatenate([parts[n] for n in range(NROW)], axis=0)
    for n in range(NROW):
        out[n] = rows


def copies_of(parts, bare_other, inter_other):
    return pl.pallas_call(
        copy_kernel,
        out_shape=jax.ShapeDtypeStruct((NROW, NROW, LANES), F32),
        in_specs=[VMEM, ANY, ANY],
        out_specs=VMEM,
    )(parts, bare_other, inter_other)


def exchange(copies, members):
    return lax.all_to_all(copies, ("row", "col"), 0, 0, axis_index_groups=members)


def spread_of():
    value = iota((LANES, LANES), 0)
    lane = iota((LANES, LANES), 1)
    parts = [value == 4 * i + lane % 4 for i in range(6)]
    parts += [value == 24 + (lane + LANES * i) % ORBD for i in range(3)]
    parts += [value == 48 + 4 * i + lane % 4 for i in range(4)]
    return jnp.concatenate([part.astype(F32) for part in parts], axis=1)


def domain_row(parts, spread, q):
    half, z = q // RING, q % RING
    domain = iota((NROW, LANES), 0)
    lane = iota((NROW, LANES), 1)
    block = parts[pl.ds(half * RING, RING), pl.ds(z * 2, 2), :]
    block = jnp.concatenate([block[n // 2, n % 2 : n % 2 + 1] for n in range(NROW)], axis=0)
    wide = jnp.dot(block, spread, precision=HIGH, preferred_element_type=F32)
    rows = []
    for i in range(13):
        here = lane % 64 // 4 == domain
        if 6 <= i < 9:
            here = (lane + LANES * (i - 6)) // ORBD == domain
        piece = wide[:, i * LANES : (i + 1) * LANES]
        rows.append(jnp.sum(jnp.where(here, piece, 0.0), axis=0, keepdims=True))
    return rows


def row_shift(above, here, below, coupling):
    atoms = [above[2], here[0], here[1], here[2], below[0]]
    rolled = [[pltpu.roll(v, 1, 1), v, pltpu.roll(v, LANES - 1, 1)] for v in atoms]
    grids = []
    for i in range(3):
        shift = here[3 + i] * here[i]
        for a in range(3):
            for b in range(3):
                shift = shift + coupling[a, b] * rolled[i + a][b]
        grids.append(shift)
    line = iota((8, LANES), 0)
    grid = jnp.where(line == 0, grids[0], jnp.where(line == 1, grids[1], jnp.where(line == 2, grids[2], 0.0)))
    picks = jnp.concatenate(here[6:9], axis=1).astype(jnp.int32)
    orbital = iota((1, TILE), 1)
    atom_row = picks // 4
    atom_col = 4 * (orbital // ORBD) + picks % 4
    onehot = (iota((LANES, TILE), 0) == atom_col).astype(F32)
    by_row = jnp.dot(grid, onehot, precision=HIGH, preferred_element_type=F32)
    return jnp.sum(jnp.where(iota((8, TILE), 0) == atom_row, by_row, 0.0), axis=0, keepdims=True)


def as_column(shift):
    return jnp.broadcast_to(shift, (LANES, TILE)).T


def kept(here, col):
    blocks = jnp.concatenate(here[9:13] * 2, axis=0)
    onehot = (iota((LANES, TILE), 0) == 4 * col + iota((LANES, TILE), 1) // BLK).astype(F32)
    return jnp.dot(blocks, onehot, preferred_element_type=F32)


def form(out, bare, inter, keep, down, along, diagonal):
    for i in range(TILE // BLK):
        rows = slice(i * BLK, (i + 1) * BLK)
        ham = bare[rows, :].astype(F32) + 0.5 * inter[rows, :].astype(F32) * (down[rows, :1] + along)
        eye = jnp.where(iota((BLK, TILE), 0) + i * BLK == iota((BLK, TILE), 1), diagonal, 0.0)
        out[rows, :] = (eye - keep[i : i + 1] * ham).astype(jnp.bfloat16)


def initial_kernel(parts, coupling, bare, inter, bare_other, inter_other, out, out_other):
    row, col = lax.axis_index("row"), lax.axis_index("col")
    spread = spread_of()

    def around(q):
        return [domain_row(parts, spread, (q + by) % NROW) for by in (NROW - 1, 0, 1)]

    along = row_shift(*around(col), coupling)
    for q, ham, overlap, to in ((row, bare, inter, out), ((row + RING) % NROW, bare_other, inter_other, out_other)):
        near = around(q)
        down = as_column(row_shift(*near, coupling))
        form(to, ham, overlap, kept(near[1], col), down, along, jnp.where(q == col, 0.5, 0.0))


BIG = pltpu.CompilerParams(vmem_limit_bytes=62 << 20)


def initial_tiles(parts, coupling, *sources):
    return pl.pallas_call(
        initial_kernel,
        out_shape=[jax.ShapeDtypeStruct((TILE, TILE), jnp.bfloat16)] * 2,
        in_specs=[VMEM, SMEM] + [VMEM] * 4,
        out_specs=[VMEM, VMEM],
        compiler_params=BIG,
    )(parts, coupling, *sources)


def ring_step(value, by):
    return lax.ppermute(value, "row", [(h * RING + i, h * RING + (i + by) % RING) for h in range(2) for i in range(RING)])


def swap_half(value):
    return lax.ppermute(value, "row", [(i, i ^ RING) for i in range(NROW)])


def column_tiles(tile, other):
    found = {(0, 0): tile, (1, 0): other}
    up, down = [tile, other], [tile, other]
    for step in (1, 2, 3):
        for half in (0, 1):
            up[half] = ring_step(up[half], 1)
            down[half] = ring_step(down[half], -1)
            found[half, step] = up[half]
            found[half, RING - step] = down[half]
    found[0, 4] = ring_step(up[0], 1)
    found[1, 4] = ring_step(down[1], -1)
    return found


def plane_step(value, flip, by):
    pairs = []
    for index in range(NROW):
        half, y, core = index // RING, index % RING // 2, index % 2
        pairs.append((index, (half ^ flip) * RING + (y + by) % 4 * 2 + core))
    return lax.ppermute(value, "col", pairs)


def swap_core(value):
    return lax.ppermute(value, "col", [(i, i ^ 1) for i in range(NROW)])


def square_tiles(tile):
    other = plane_step(tile, 1, 0)
    found = [(0, 0, tile), (1, 0, other)]
    for by in (1, 3, 2):
        found.append((0, by, plane_step(tile, 0, by)))
    far = found[-1][2]
    for by in (1, 3):
        found.append((1, by, plane_step(other, 0, by)))
    found.append((1, 2, plane_step(far, 1, 0)))
    return [(flip, by, side, swap_core(value) if side else value) for flip, by, value in found for side in (0, 1)]


def run(copies):
    for copy in copies:
        copy.start()
    return copies


def settle(copies):
    for copy in copies:
        copy.wait()


def square_kernel(places, first, *refs):
    count = len(places)
    strip_ref, *refs = refs
    held = [] if first else [refs.pop(0)]
    tile_refs, refs = refs[:count], refs[count:]
    outs, (strip, column, sems) = refs[:-3], refs[-3:]
    row = lax.axis_index("row")
    own, z = row // RING, row % RING
    copies = []
    for n, (half, distance) in enumerate(places):
        k = (own + half) % 2 * RING + (z - distance + RING) % RING
        source = strip_ref.at[:, pl.ds(pl.multiple_of(k * TILE, TILE), TILE)]
        copies.append(pltpu.make_async_copy(tile_refs[n], column.at[n * TILE : (n + 1) * TILE, :], sems.at[2 * n]))
        copies.append(pltpu.make_async_copy(source, strip.at[:, n * TILE : (n + 1) * TILE], sems.at[2 * n + 1]))
    run(copies)
    for n in range(0, count, 4):
        upto = min(n + 4, count)
        settle(copies[2 * n : 2 * upto])
        span = slice(n * TILE, upto * TILE)
        part = jnp.dot(strip[:, span], column[span, :], preferred_element_type=F32)
        if n == 0 and not held:
            outs[0][...] = part
        else:
            outs[0][...] = (held[0][...] if n == 0 else outs[0][...]) + part
    if not first:
        outs[1][...] = outs[0][...].astype(jnp.bfloat16)


def square_of(strip, held, found, places):
    count = len(places)
    shapes = [jax.ShapeDtypeStruct((TILE, TILE), F32)]
    if held:
        shapes.append(jax.ShapeDtypeStruct((TILE, TILE), jnp.bfloat16))
    return pl.pallas_call(
        functools.partial(square_kernel, places, not held),
        out_shape=shapes,
        in_specs=[ANY] + [VMEM] * len(held) + [ANY] * count,
        out_specs=[VMEM] * len(shapes),
        scratch_shapes=[
            pltpu.VMEM((TILE, count * TILE), jnp.bfloat16),
            pltpu.VMEM((count * TILE, TILE), jnp.bfloat16),
            pltpu.SemaphoreType.DMA((2 * count,)),
        ],
        compiler_params=BIG,
        cost_estimate=cost(count),
    )(strip, *held, *[found[place] for place in places])


def cost(count):
    return pl.CostEstimate(flops=2 * count * TILE**3, bytes_accessed=4 * count * TILE**2, transcendentals=0)


ORDER = tuple((half, 2 * step + odd) for odd in (0, 1) for half in (0, 1) for step in range(4))
LAST = ((0, 4), (1, 4))
FIRST = tuple(place for place in ORDER if place not in LAST)


def rows_for(flip, by, side):
    row, col = lax.axis_index("row"), lax.axis_index("col")
    k = (col // RING + flip) % 2 * RING + (col % RING // 2 - by + 4) % 4 * 2 + (col + side) % 2
    half, distance = (k // RING + row // RING) % 2, (row % RING - k % RING + RING) % RING
    return pl.ds(pl.multiple_of((distance % 2 * 8 + half * 4 + distance // 2) * TILE, TILE), TILE)


def early_kernel(early, late, *refs):
    count = len(early)
    tile_refs, column_refs, refs = refs[:count], refs[count : count + NROW], refs[count + NROW :]
    out, rest, strip, column, sems, rest_sems = refs
    copies = [pltpu.make_async_copy(ref, column.at[n * TILE : (n + 1) * TILE, :], sems.at[n]) for n, ref in enumerate(column_refs)]
    for n, ref in enumerate(tile_refs):
        copies.append(pltpu.make_async_copy(ref, strip.at[:, n * TILE : (n + 1) * TILE], sems.at[NROW + n]))
    settle(run(copies))
    leaving = []
    for n, place in enumerate(late):
        to = rest.at[n * TILE : (n + 1) * TILE, :]
        leaving.append(pltpu.make_async_copy(column.at[rows_for(*place), :], to, rest_sems.at[n]))
    run(leaving)
    for n, place in enumerate(early):
        part = jnp.dot(strip[:, n * TILE : (n + 1) * TILE], column[rows_for(*place), :], preferred_element_type=F32)
        if n == 0:
            out[...] = part
        else:
            out[...] += part
    settle(leaving)


def early_of(tiles, columns, early, late):
    count = len(early)
    return pl.pallas_call(
        functools.partial(early_kernel, early, late),
        out_shape=[
            jax.ShapeDtypeStruct((TILE, TILE), F32),
            jax.ShapeDtypeStruct((len(late) * TILE, TILE), jnp.bfloat16),
        ],
        in_specs=[ANY] * (count + NROW),
        out_specs=[VMEM, ANY],
        scratch_shapes=[
            pltpu.VMEM((TILE, count * TILE), jnp.bfloat16),
            pltpu.VMEM((NROW * TILE, TILE), jnp.bfloat16),
            pltpu.SemaphoreType.DMA((NROW + count,)),
            pltpu.SemaphoreType.DMA((len(late),)),
        ],
        compiler_params=BIG,
        cost_estimate=cost(NROW),
    )(*tiles, *columns)


def late_kernel(count, square_ref, held_ref, rest_ref, *refs):
    tile_refs, (out, square, held, rest, strip, sems) = refs[:count], refs[count:]
    copies = [pltpu.make_async_copy(ref, strip.at[:, n * TILE : (n + 1) * TILE], sems.at[n]) for n, ref in enumerate(tile_refs)]
    for n, (ref, to) in enumerate(((rest_ref, rest), (square_ref, square), (held_ref, held))):
        copies.append(pltpu.make_async_copy(ref, to, sems.at[count + n]))
    settle(run(copies))
    part = jnp.dot(strip[...], rest[...], preferred_element_type=F32)
    out[...] = 3.0 * square[...] - 2.0 * (held[...] + part)


def late_of(square, held, rest, tiles):
    count = len(tiles)
    return pl.pallas_call(
        functools.partial(late_kernel, count),
        out_shape=jax.ShapeDtypeStruct((TILE, TILE), F32),
        in_specs=[ANY] * (3 + count),
        out_specs=VMEM,
        scratch_shapes=[
            pltpu.VMEM((TILE, TILE), F32),
            pltpu.VMEM((TILE, TILE), F32),
            pltpu.VMEM((count * TILE, TILE), jnp.bfloat16),
            pltpu.VMEM((TILE, count * TILE), jnp.bfloat16),
            pltpu.SemaphoreType.DMA((3 + count,)),
        ],
        compiler_params=BIG,
        cost_estimate=cost(count),
    )(square, held, rest, *tiles)


EARLY = 10


def per_device(charges, hubbard, coupling, orbital_atom, block_mask, bare_ham, intersection):
    bare_other, intersection_other = swap_half(bare_ham), swap_half(intersection)
    parts = exchange(pack(charges, hubbard, orbital_atom, block_mask), PILLAR)
    parts = exchange(copies_of(parts, bare_other, intersection_other), PLANE)
    initial, initial_other = initial_tiles(parts, coupling, bare_ham, intersection, bare_other, intersection_other)
    initial_strip = lax.all_gather(initial, "col", axis=1, tiled=True)
    found = column_tiles(initial, initial_other)
    held = square_of(initial_strip, [], found, FIRST)
    square, square_low = square_of(initial_strip, held, found, LAST)
    tiles = square_tiles(square_low)
    places, values = [tile[:3] for tile in tiles], [tile[3] for tile in tiles]
    held, rest = early_of(values[:EARLY], [found[place] for place in ORDER], places[:EARLY], places[EARLY:])
    return late_of(square, held, rest, values[EARLY:])


def solution(mesh):
    placed = (
        P("row", "col"),
        P("row", "col"),
        P(),
        P("row", "col", None),
        P("row", "col"),
        P("row", "col"),
        P("row", "col"),
    )
    return jax.shard_map(
        per_device, mesh=mesh, in_specs=placed, out_specs=P("row", "col"), check_vma=False
    )
```

time: 315 us -> 146 us (0.46)
  waiting for transfers between devices: 183 us -> 20.1 us
  blocking collectives: 77.3 us -> 30.4 us
  starting transfers between devices: 11.1 us -> 50.6 us
  Pallas kernels: 0 us -> 27.4 us
  matrix products: 14.3 us -> 0 us
  other arithmetic: 12.2 us -> 0 us
    all_gather x2 -> x0, waiting for transfers between devices: 145 us -> none  [the longest x1 103 us: strip_product(): lax.all_gather(right_tile, 'row', axis=0, tiled=True)]
    unnamed x1 -> x0, blocking collectives: 77.3 us -> none
    ppermute x4 -> x31, starting transfers between devices: 11 us -> 50.6 us  [the longest x8 20.9 us: swap_core(): return lax.ppermute(value, 'col', [(i, i ^ 1) for i in range(NROW)])]
    all_gather x1, waiting for transfers between devices: 35.4 us -> 0.01 us  [per_device(): initial_strip = lax.all_gather(initial, 'col', axis=1, tiled=True)]
    all_to_all x0 -> x2, blocking collectives: none -> 30.4 us  [exchange(): lax.all_to_all(copies, ('row', 'col'), 0, 0, axis_index_groups=members)]
    pallas_call x0 -> x7, Pallas kernels: none -> 27.4 us  [the longest x2 9.01 us: square_of(): pl.pallas_call(functools.partial(square_kernel, places, not held), out_sh...]
    ppermute x4 -> x31, waiting for transfers between devices: 2.56 us -> 20.1 us  [the longest x14 20 us: ring_step(): lax.ppermute(value, 'row', [(h * RING + i, h * RING + (i + by) % RING) fo...]
    dot_general x2 -> x0, matrix products: 14.3 us -> none  [strip_product(): jnp.dot(left_strip, lax.all_gather(right_tile, 'row', axis=0, tiled=True)...]
  transfers between devices with their start and end apart: 7 -> 32, of which waited for: 4 -> 8; matrix products, arithmetic and copies ran while one was open for 1% -> 0% of each run, Pallas kernels for 0% -> 10%
where the time goes in v3:
time: 146 us
  starting transfers between devices  50.6 us (35%)
  blocking collectives  30.4 us (21%)
  Pallas kernels  27.4 us (19%)
  waiting for transfers between devices  20.1 us (14%)
  between operations  13.7 us (9%)
  local copies, waits for them, and re-layouts  3.76 us (3%)
    all_to_all x2, blocking collectives, exchange(): lax.all_to_all(copies, ('row', 'col'), 0, 0, axis_index_groups=members)  30.4 us
    ppermute x8, starting transfers between devices, swap_core(): return lax.ppermute(value, 'col', [(i, i ^ 1) for i in range(NROW)])  20.9 us
    ppermute x14, waiting for transfers between devices, ring_step(): lax.ppermute(value, 'row', [(h * RING + i, h * RING + (i + by) % RING) fo...  20 us
    ppermute x14, starting transfers between devices, ring_step(): lax.ppermute(value, 'row', [(h * RING + i, h * RING + (i + by) % RING) fo...  19 us
    pallas_call x2, Pallas kernels, square_of(): pl.pallas_call(functools.partial(square_kernel, places, not held), out_sh...  9.01 us
    pallas_call x1, Pallas kernels, early_of(): pl.pallas_call(functools.partial(early_kernel, early, late), out_shape=[j...  7.21 us
    ppermute x7, starting transfers between devices, plane_step(): return lax.ppermute(value, 'col', pairs)  7.09 us
    pallas_call x1, Pallas kernels, late_of(): pl.pallas_call(functools.partial(late_kernel, count), out_shape=jax.Shape...  4.29 us
  transfers between devices with their start and end apart: 32, of which 8 were waited for; matrix products, arithmetic and copies ran while one was open for 0% of the time, Pallas kernels for 10%

profile of v3, /device:TPU:1, one launch (start us, length us, event | category | flops | bytes accessed | tf_op | source)
XLA Modules:
  0.0 145.9 jit_solution(4222410375850758217)
XLA Ops:
  6.5 3.6 %collective-permute-start = (bf16[384,384]{1,0:T(8,128)(2,1)}, bf16[384,384]{1,0:T(8,128)(2,1)S(1)}, u32[]{:S(2)}, u32[]{:S(2)}) collective-permute-start(bf16[384,384]{1,0:T(8,128)(2,1)} %bare.1), channel_id=1, source_target_pairs={{0,128},{16,144},{32,160},{48,176},{64,192},{80,208},{96,224},{112... | collective-permute-start | bytes 884744 | tf_op jit(solution)/shard_map/ppermute | solution.py:181
  10.1 1.4 shard_map.73
  11.6 16.8 %all_to_all.10.parts = f32[16,1,128]{2,1,0:T(1,128)} all-to-all(f32[16,1,128]{2,1,0:T(1,128)} %shard_map.73), channel_id=1, replica_groups={{0,1,16,17,32,33,48,49,64,65,80,81,96,97,112,113},{2,3,18,19,34,35,50,5..., dimensions={0} | all-to-all | bytes 16384 | tf_op jit(solution)/shard_map/all_to_all | solution.py:81
  28.4 0.7 copy-done
  29.1 0.7 copy-done.1
  29.8 1.4 shard_map.74
  31.2 13.6 %all_to_all.11.parts = f32[16,16,128]{2,1,0:T(8,128)} all-to-all(f32[16,16,128]{2,1,0:T(8,128)} %shard_map.74), channel_id=1, replica_groups={{0,2,4,6,8,10,12,14,128,130,132,134,136,138,140,142},{1,3,5,7,9,11,13,1..., dimensions={0} | all-to-all | bytes 262144 | tf_op jit(solution)/shard_map/all_to_all | solution.py:81
  44.7 4.2 %shard_map.75 = (bf16[384,384]{1,0:T(8,128)(2,1)}, bf16[384,384]{1,0:T(8,128)(2,1)}) custom-call(f32[16,16,128]{2,1,0:T(8,128)} %all_to_all.11.parts, f32[3,3]{1,0:T(4,128)} %coupling.1, bf16[384,384]{1,0:T(8,128)(2,1)} %bare.1, bf16[384,384]{1,0:T(8,128)(2,1)} %inter.1, bf16[384,384]{1,0:T(8,128)(2,1)} %copy-done, bf16[384,384]{1,0:T(8,128)(2,1)} %copy-done.1), custom_call_target="tpu_custom_call" | custom-call | tf_op jit(solution)/shard_map/pallas_call | solution.py:167
  48.9 0.6 collective-permute-start.2
  49.5 2.1 %collective-permute-start.8 = (bf16[384,384]{1,0:T(8,128)(2,1)}, bf16[384,384]{1,0:T(8,128)(2,1)S(1)}, u32[]{:S(2)}, u32[]{:S(2)}) collective-permute-start(bf16[384,384]{1,0:T(8,128)(2,1)} %get-tuple-element.12.refs_4_.refs_14_), channel_id=1, source_target_pairs={{0,112},{16,0},{32,16},{48,32},{64,48},{80,64},{96,80},{112,96},{1... | collective-permute-start | bytes 884744 | tf_op jit(solution)/shard_map/ppermute | solution.py:177
  51.7 1.4 collective-permute-start.6
  53.1 3.5 %collective-permute-done.2.refs_7_.refs_18_ = bf16[384,384]{1,0:T(8,128)(2,1)S(1)} collective-permute-done((bf16[384,384]{1,0:T(8,128)(2,1)}, bf16[384,384]{1,0:T(8,128)(2,1)S(1)}, u32[]{:S(2)}, u32[]{:S(2)}) %collective-permute-start.2) | collective-permute-done | bytes 294944 | tf_op jit(solution)/shard_map/ppermute | solution.py:177
  56.7 2.7 %collective-permute-start.9 = (bf16[384,384]{1,0:T(8,128)(2,1)S(1)}, bf16[384,384]{1,0:T(8,128)(2,1)S(1)}, u32[]{:S(2)}, u32[]{:S(2)}) collective-permute-start(bf16[384,384]{1,0:T(8,128)(2,1)S(1)} %collective-permute-done.8.refs_14_.refs_25_), channel_id=1, source_target_pairs={{0,112},{16,0},{32,16},{48,32},{64,48},{80,64},{96,80},{112,96},{1... | collective-permute-start | bytes 884744 | tf_op jit(solution)/shard_map/ppermute | solution.py:177
  59.4 3.0 %collective-permute-done.4.refs_10_.refs_21_ = bf16[384,384]{1,0:T(8,128)(2,1)S(1)} collective-permute-done((bf16[384,384]{1,0:T(8,128)(2,1)}, bf16[384,384]{1,0:T(8,128)(2,1)S(1)}, u32[]{:S(2)}, u32[]{:S(2)}) %collective-permute-start.4) | collective-permute-done | bytes 294944 | tf_op jit(solution)/shard_map/ppermute | solution.py:177
  62.4 3.0 %collective-permute-start.5 = (bf16[384,384]{1,0:T(8,128)(2,1)S(1)}, bf16[384,384]{1,0:T(8,128)(2,1)S(1)}, u32[]{:S(2)}, u32[]{:S(2)}) collective-permute-start(bf16[384,384]{1,0:T(8,128)(2,1)S(1)} %collective-permute-done.4.refs_10_.refs_21_), channel_id=1, source_target_pairs={{0,112},{16,0},{32,16},{48,32},{64,48},{80,64},{96,80},{112,96},{1... | collective-permute-start | bytes 884744 | tf_op jit(solution)/shard_map/ppermute | solution.py:177
  65.4 3.9 %collective-permute-done.3.refs_2_.refs_11_ = bf16[384,384]{1,0:T(8,128)(2,1)S(1)} collective-permute-done((bf16[384,384]{1,0:T(8,128)(2,1)S(1)}, bf16[384,384]{1,0:T(8,128)(2,1)S(1)}, u32[]{:S(2)}, u32[]{:S(2)}) %collective-permute-start.3) | collective-permute-done | bytes 294944 | tf_op jit(solution)/shard_map/ppermute | solution.py:177
  69.3 2.7 %collective-permute-start.13 = (bf16[384,384]{1,0:T(8,128)(2,1)S(1)}, bf16[384,384]{1,0:T(8,128)(2,1)}, u32[]{:S(2)}, u32[]{:S(2)}) collective-permute-start(bf16[384,384]{1,0:T(8,128)(2,1)S(1)} %collective-permute-done.9.refs_6_.refs_17_), channel_id=1, source_target_pairs={{0,112},{16,0},{32,16},{48,32},{64,48},{80,64},{96,80},{112,96},{1... | collective-permute-start | bytes 884744 | tf_op jit(solution)/shard_map/ppermute | solution.py:177
  72.0 3.0 %collective-permute-done.5.refs_3_.refs_13_ = bf16[384,384]{1,0:T(8,128)(2,1)S(1)} collective-permute-done((bf16[384,384]{1,0:T(8,128)(2,1)S(1)}, bf16[384,384]{1,0:T(8,128)(2,1)S(1)}, u32[]{:S(2)}, u32[]{:S(2)}) %collective-permute-start.5) | collective-permute-done | bytes 294944 | tf_op jit(solution)/shard_map/ppermute | solution.py:177
  75.0 3.0 %collective-permute-start.11 = (bf16[384,384]{1,0:T(8,128)(2,1)S(1)}, bf16[384,384]{1,0:T(8,128)(2,1)S(1)}, u32[]{:S(2)}, u32[]{:S(2)}) collective-permute-start(bf16[384,384]{1,0:T(8,128)(2,1)S(1)} %collective-permute-done.5.refs_3_.refs_13_), channel_id=1, source_target_pairs={{0,112},{16,0},{32,16},{48,32},{64,48},{80,64},{96,80},{112,96},{1... | collective-permute-start | bytes 884744 | tf_op jit(solution)/shard_map/ppermute | solution.py:177
  78.0 2.1 %collective-permute-done.10.refs_8_.refs_19_ = bf16[384,384]{1,0:T(8,128)(2,1)} collective-permute-done((bf16[384,384]{1,0:T(8,128)(2,1)S(1)}, bf16[384,384]{1,0:T(8,128)(2,1)}, u32[]{:S(2)}, u32[]{:S(2)}) %collective-permute-start.10) | collective-permute-done | bytes 294944 | tf_op jit(solution)/shard_map/ppermute | solution.py:177
  80.2 0.3 collective-permute-start.14
  80.5 0.9 collective-permute-done.13.refs_13_.refs_24_
  81.4 3.0 %collective-permute-start.15 = (bf16[384,384]{1,0:T(8,128)(2,1)}, bf16[384,384]{1,0:T(8,128)(2,1)}, u32[]{:S(2)}, u32[]{:S(2)}) collective-permute-start(bf16[384,384]{1,0:T(8,128)(2,1)} %collective-permute-done.13.refs_13_.refs_24_), channel_id=1, source_target_pairs={{0,112},{16,0},{32,16},{48,32},{64,48},{80,64},{96,80},{112,96},{1... | collective-permute-start | bytes 884744 | tf_op jit(solution)/shard_map/ppermute | solution.py:177
  84.5 3.2 %collective-permute-done.11.refs_9_.refs_20_ = bf16[384,384]{1,0:T(8,128)(2,1)S(1)} collective-permute-done((bf16[384,384]{1,0:T(8,128)(2,1)S(1)}, bf16[384,384]{1,0:T(8,128)(2,1)S(1)}, u32[]{:S(2)}, u32[]{:S(2)}) %collective-permute-start.11) | collective-permute-done | bytes 294944 | tf_op jit(solution)/shard_map/ppermute | solution.py:177
  87.6 0.7 copy-done.10
  88.4 5.3 %shard_map.76.refs_1_ = f32[384,384]{1,0:T(8,128)} custom-call(bf16[384,6144]{1,0:T(8,128)(2,1)} %all-gather.2.cloned.1.call-done.refs_0_, bf16[384,384]{1,0:T(8,128)(2,1)} %get-tuple-element.11.refs_1_.refs_10_, bf16[384,384]{1,0:T(8,128)(2,1)} %copy-done.6, bf16[384,384]{1,0:T(8,128)(2,1)} %copy-done.8, ...), custom_call_target="tpu_custom_call" | custom-call | flops 1585446912 | bytes 8257536 | tf_op jit(solution)/shard_map/pallas_call | solution.py:266
  93.7 0.4 collective-permute-done.15.refs_3_.refs_16_
  94.0 3.7 %shard_map.77 = (f32[384,384]{1,0:T(8,128)}, bf16[384,384]{1,0:T(8,128)(2,1)}) custom-call(bf16[384,6144]{1,0:T(8,128)(2,1)} %all-gather.2.cloned.1.call-done.refs_0_, f32[384,384]{1,0:T(8,128)} %shard_map.76.refs_1_, bf16[384,384]{1,0:T(8,128)(2,1)} %collective-permute-done.14.refs_2_.refs_12_, bf16[384,384]{1,0:T(8,128)(2,1)} %collective-permute-done.15.refs_3_.refs_16_), custom_call_target="tpu_custom_call" | custom-call | flops 226492416 | bytes 1179648 | tf_op jit(solution)/shard_map/pallas_call | solution.py:266
  97.8 0.2 collective-permute-start.17
  98.0 0.1 collective-permute-start.19
  98.1 2.5 %collective-permute-start.21 = (bf16[384,384]{1,0:T(8,128)(2,1)}, bf16[384,384]{1,0:T(8,128)(2,1)S(1)}, u32[]{:S(2)}, u32[]{:S(2)}) collective-permute-start(bf16[384,384]{1,0:T(8,128)(2,1)} %get-tuple-element.14.refs_0_), channel_id=1, source_target_pairs={{0,6},{1,7},{2,0},{3,1},{4,2},{5,3},{6,4},{7,5},{8,14},{9,15},{10,... | collective-permute-start | bytes 884744 | tf_op jit(solution)/shard_map/ppermute | solution.py:203
  100.6 0.4 collective-permute-start.23
  101.1 7.1 %collective-permute-start.16 = (bf16[384,384]{1,0:T(8,128)(2,1)}, bf16[384,384]{1,0:T(8,128)(2,1)S(1)}, u32[]{:S(2)}, u32[]{:S(2)}) collective-permute-start(bf16[384,384]{1,0:T(8,128)(2,1)} %get-tuple-element.14.refs_0_), channel_id=1, source_target_pairs={{0,1},{1,0},{2,3},{3,2},{4,5},{5,4},{6,7},{7,6},{8,9},{9,8},{10,11... | collective-permute-start | bytes 884744 | tf_op jit(solution)/shard_map/ppermute | solution.py:207
  108.2 2.6 %collective-permute-start.18 = (bf16[384,384]{1,0:T(8,128)(2,1)S(1)}, bf16[384,384]{1,0:T(8,128)(2,1)S(1)}, u32[]{:S(2)}, u32[]{:S(2)}) collective-permute-start(bf16[384,384]{1,0:T(8,128)(2,1)S(1)} %collective-permute-done.17.refs_2_), channel_id=1, source_target_pairs={{0,1},{1,0},{2,3},{3,2},{4,5},{5,4},{6,7},{7,6},{8,9},{9,8},{10,11... | collective-permute-start | bytes 884744 | tf_op jit(solution)/shard_map/ppermute | solution.py:207
  110.8 1.8 %collective-permute-start.20 = (bf16[384,384]{1,0:T(8,128)(2,1)S(1)}, bf16[384,384]{1,0:T(8,128)(2,1)S(1)}, u32[]{:S(2)}, u32[]{:S(2)}) collective-permute-start(bf16[384,384]{1,0:T(8,128)(2,1)S(1)} %collective-permute-done.19.refs_4_), channel_id=1, source_target_pairs={{0,1},{1,0},{2,3},{3,2},{4,5},{5,4},{6,7},{7,6},{8,9},{9,8},{10,11... | collective-permute-start | bytes 884744 | tf_op jit(solution)/shard_map/ppermute | solution.py:207
  112.7 2.7 %collective-permute-start.27 = (bf16[384,384]{1,0:T(8,128)(2,1)S(1)}, bf16[384,384]{1,0:T(8,128)(2,1)S(1)}, u32[]{:S(2)}, u32[]{:S(2)}) collective-permute-start(bf16[384,384]{1,0:T(8,128)(2,1)S(1)} %collective-permute-done.17.refs_2_), channel_id=1, source_target_pairs={{0,6},{1,7},{2,0},{3,1},{4,2},{5,3},{6,4},{7,5},{8,14},{9,15},{10,... | collective-permute-start | bytes 884744 | tf_op jit(solution)/shard_map/ppermute | solution.py:203
  115.3 1.1 collective-permute-start.29
  116.5 4.1 %collective-permute-start.22 = (bf16[384,384]{1,0:T(8,128)(2,1)S(1)}, bf16[384,384]{1,0:T(8,128)(2,1)S(1)}, u32[]{:S(2)}, u32[]{:S(2)}) collective-permute-start(bf16[384,384]{1,0:T(8,128)(2,1)S(1)} %collective-permute-done.21.refs_6_), channel_id=1, source_target_pairs={{0,1},{1,0},{2,3},{3,2},{4,5},{5,4},{6,7},{7,6},{8,9},{9,8},{10,11... | collective-permute-start | bytes 884744 | tf_op jit(solution)/shard_map/ppermute | solution.py:207
  120.6 0.1 collective-permute-start.24
  120.7 3.1 %collective-permute-start.26 = (bf16[384,384]{1,0:T(8,128)(2,1)S(1)}, bf16[384,384]{1,0:T(8,128)(2,1)S(1)}, u32[]{:S(2)}, u32[]{:S(2)}) collective-permute-start(bf16[384,384]{1,0:T(8,128)(2,1)S(1)} %collective-permute-done.25.refs_0_), channel_id=1, source_target_pairs={{0,1},{1,0},{2,3},{3,2},{4,5},{5,4},{6,7},{7,6},{8,9},{9,8},{10,11... | collective-permute-start | bytes 884744 | tf_op jit(solution)/shard_map/ppermute | solution.py:207
  123.7 0.3 collective-permute-start.28
  124.1 1.8 %collective-permute-start.30 = (bf16[384,384]{1,0:T(8,128)(2,1)S(1)}, bf16[384,384]{1,0:T(8,128)(2,1)S(1)}, u32[]{:S(2)}, u32[]{:S(2)}) collective-permute-start(bf16[384,384]{1,0:T(8,128)(2,1)S(1)} %collective-permute-done.29.refs_4_), channel_id=1, source_target_pairs={{0,1},{1,0},{2,3},{3,2},{4,5},{5,4},{6,7},{7,6},{8,9},{9,8},{10,11... | collective-permute-start | bytes 884744 | tf_op jit(solution)/shard_map/ppermute | solution.py:207
  125.9 0.7 copy-done.24
  126.6 7.2 %shard_map.78 = (f32[384,384]{1,0:T(8,128)}, bf16[2304,384]{1,0:T(8,128)(2,1)}) custom-call(bf16[384,384]{1,0:T(8,128)(2,1)} %get-tuple-element.14.refs_0_, bf16[384,384]{1,0:T(8,128)(2,1)} %copy-done.21, bf16[384,384]{1,0:T(8,128)(2,1)} %copy-done.17, bf16[384,384]{1,0:T(8,128)(2,1)} %copy-done.22, bf16[384,384]{1,0:T(8,128)(2,1)} %copy-done.18, ...), custom_call_target="tpu_custom_call" | custom-call | flops 1811939328 | bytes 9437184 | tf_op jit(solution)/shard_map/pallas_call | solution.py:321
  133.9 0.6 copy-done.14
  134.6 0.1 copy-done.15
  134.7 0.1 copy-done.16
  134.8 4.3 %shard_map.79 = f32[384,384]{1,0:T(8,128)} custom-call(f32[384,384]{1,0:T(8,128)} %get-tuple-element.13.square_ref, f32[384,384]{1,0:T(8,128)} %get-tuple-element.15.held_ref, bf16[2304,384]{1,0:T(8,128)(2,1)} %get-tuple-element.16.rest_ref, bf16[384,384]{1,0:T(8,128)(2,1)} %copy-done.11, bf16[384,384]{1,0:T(8,128)(2,1)} %copy-done.14, ...), custom_call_target="tpu_custom_call" | custom-call | flops 679477248 | bytes 3538944 | tf_op jit(solution)/shard_map/pallas_call | solution.py:352
  (76 shorter events, 0.2 us)
Async XLA Ops:
  6.5 81.8 %all-gather.2.cloned.1.call-start = ((), (), s32[]{:S(2)}) async-start(), calls=%async_computation.2 | async-start | bytes 5013504 | tf_op jit(solution)/shard_map/all_gather | solution.py:377
  6.5 21.8 %collective-permute-start = (bf16[384,384]{1,0:T(8,128)(2,1)}, bf16[384,384]{1,0:T(8,128)(2,1)S(1)}, u32[]{:S(2)}, u32[]{:S(2)}) collective-permute-start(bf16[384,384]{1,0:T(8,128)(2,1)} %bare.1), channel_id=1, source_target_pairs={{0,128},{16,144},{32,160},{48,176},{64,192},{80,208},{96,224},{112... | collective-permute-start | bytes 884744 | tf_op jit(solution)/shard_map/ppermute | solution.py:181
  10.1 18.2 %collective-permute-start.1 = (bf16[384,384]{1,0:T(8,128)(2,1)}, bf16[384,384]{1,0:T(8,128)(2,1)S(1)}, u32[]{:S(2)}, u32[]{:S(2)}) collective-permute-start(bf16[384,384]{1,0:T(8,128)(2,1)} %inter.1), channel_id=1, source_target_pairs={{0,128},{16,144},{32,160},{48,176},{64,192},{80,208},{96,224},{112... | collective-permute-start | bytes 884744 | tf_op jit(solution)/shard_map/ppermute | solution.py:181
  48.9 7.8 %collective-permute-start.2 = (bf16[384,384]{1,0:T(8,128)(2,1)}, bf16[384,384]{1,0:T(8,128)(2,1)S(1)}, u32[]{:S(2)}, u32[]{:S(2)}) collective-permute-start(bf16[384,384]{1,0:T(8,128)(2,1)} %get-tuple-element.11.refs_1_.refs_10_), channel_id=1, source_target_pairs={{0,16},{16,32},{32,48},{48,64},{64,80},{80,96},{96,112},{112,0},{1... | collective-permute-start | bytes 884744 | tf_op jit(solution)/shard_map/ppermute | solution.py:177
  49.5 7.1 %collective-permute-start.8 = (bf16[384,384]{1,0:T(8,128)(2,1)}, bf16[384,384]{1,0:T(8,128)(2,1)S(1)}, u32[]{:S(2)}, u32[]{:S(2)}) collective-permute-start(bf16[384,384]{1,0:T(8,128)(2,1)} %get-tuple-element.12.refs_4_.refs_14_), channel_id=1, source_target_pairs={{0,112},{16,0},{32,16},{48,32},{64,48},{80,64},{96,80},{112,96},{1... | collective-permute-start | bytes 884744 | tf_op jit(solution)/shard_map/ppermute | solution.py:177
  51.7 10.7 %collective-permute-start.4 = (bf16[384,384]{1,0:T(8,128)(2,1)}, bf16[384,384]{1,0:T(8,128)(2,1)S(1)}, u32[]{:S(2)}, u32[]{:S(2)}) collective-permute-start(bf16[384,384]{1,0:T(8,128)(2,1)} %get-tuple-element.11.refs_1_.refs_10_), channel_id=1, source_target_pairs={{0,112},{16,0},{32,16},{48,32},{64,48},{80,64},{96,80},{112,96},{1... | collective-permute-start | bytes 884744 | tf_op jit(solution)/shard_map/ppermute | solution.py:177
  51.7 13.7 %collective-permute-start.6 = (bf16[384,384]{1,0:T(8,128)(2,1)}, bf16[384,384]{1,0:T(8,128)(2,1)S(1)}, u32[]{:S(2)}, u32[]{:S(2)}) collective-permute-start(bf16[384,384]{1,0:T(8,128)(2,1)} %get-tuple-element.12.refs_4_.refs_14_), channel_id=1, source_target_pairs={{0,16},{16,32},{32,48},{48,64},{64,80},{80,96},{96,112},{112,0},{1... | collective-permute-start | bytes 884744 | tf_op jit(solution)/shard_map/ppermute | solution.py:177
  56.7 31.7 %copy-start.2 = (bf16[384,384]{1,0:T(8,128)(2,1)}, bf16[384,384]{1,0:T(8,128)(2,1)S(1)}, u32[]{:S(2)}) copy-start(bf16[384,384]{1,0:T(8,128)(2,1)S(1)} %collective-permute-done.2.refs_7_.refs_18_) | copy-start | bytes 884740
  56.7 12.6 %collective-permute-start.3 = (bf16[384,384]{1,0:T(8,128)(2,1)S(1)}, bf16[384,384]{1,0:T(8,128)(2,1)S(1)}, u32[]{:S(2)}, u32[]{:S(2)}) collective-permute-start(bf16[384,384]{1,0:T(8,128)(2,1)S(1)} %collective-permute-done.2.refs_7_.refs_18_), channel_id=1, source_target_pairs={{0,16},{16,32},{32,48},{48,64},{64,80},{80,96},{96,112},{112,0},{1... | collective-permute-start | bytes 884744 | tf_op jit(solution)/shard_map/ppermute | solution.py:177
  56.7 31.7 %copy-start.3 = (bf16[384,384]{1,0:T(8,128)(2,1)}, bf16[384,384]{1,0:T(8,128)(2,1)S(1)}, u32[]{:S(2)}) copy-start(bf16[384,384]{1,0:T(8,128)(2,1)S(1)} %collective-permute-done.8.refs_14_.refs_25_) | copy-start | bytes 884740
  56.7 12.6 %collective-permute-start.9 = (bf16[384,384]{1,0:T(8,128)(2,1)S(1)}, bf16[384,384]{1,0:T(8,128)(2,1)S(1)}, u32[]{:S(2)}, u32[]{:S(2)}) collective-permute-start(bf16[384,384]{1,0:T(8,128)(2,1)S(1)} %collective-permute-done.8.refs_14_.refs_25_), channel_id=1, source_target_pairs={{0,112},{16,0},{32,16},{48,32},{64,48},{80,64},{96,80},{112,96},{1... | collective-permute-start | bytes 884744 | tf_op jit(solution)/shard_map/ppermute | solution.py:177
  62.3 26.0 %copy-start.4 = (bf16[384,384]{1,0:T(8,128)(2,1)}, bf16[384,384]{1,0:T(8,128)(2,1)S(1)}, u32[]{:S(2)}) copy-start(bf16[384,384]{1,0:T(8,128)(2,1)S(1)} %collective-permute-done.4.refs_10_.refs_21_) | copy-start | bytes 884740
  62.4 12.6 %collective-permute-start.5 = (bf16[384,384]{1,0:T(8,128)(2,1)S(1)}, bf16[384,384]{1,0:T(8,128)(2,1)S(1)}, u32[]{:S(2)}, u32[]{:S(2)}) collective-permute-start(bf16[384,384]{1,0:T(8,128)(2,1)S(1)} %collective-permute-done.4.refs_10_.refs_21_), channel_id=1, source_target_pairs={{0,112},{16,0},{32,16},{48,32},{64,48},{80,64},{96,80},{112,96},{1... | collective-permute-start | bytes 884744 | tf_op jit(solution)/shard_map/ppermute | solution.py:177
  65.4 23.0 %copy-start.5 = (bf16[384,384]{1,0:T(8,128)(2,1)}, bf16[384,384]{1,0:T(8,128)(2,1)S(1)}, u32[]{:S(2)}) copy-start(bf16[384,384]{1,0:T(8,128)(2,1)S(1)} %collective-permute-done.6.refs_11_.refs_22_) | copy-start | bytes 884740
  65.4 12.6 %collective-permute-start.7 = (bf16[384,384]{1,0:T(8,128)(2,1)S(1)}, bf16[384,384]{1,0:T(8,128)(2,1)S(1)}, u32[]{:S(2)}, u32[]{:S(2)}) collective-permute-start(bf16[384,384]{1,0:T(8,128)(2,1)S(1)} %collective-permute-done.6.refs_11_.refs_22_), channel_id=1, source_target_pairs={{0,16},{16,32},{32,48},{48,64},{64,80},{80,96},{96,112},{112,0},{1... | collective-permute-start | bytes 884744 | tf_op jit(solution)/shard_map/ppermute | solution.py:177
  69.3 19.1 %copy-start.6 = (bf16[384,384]{1,0:T(8,128)(2,1)}, bf16[384,384]{1,0:T(8,128)(2,1)S(1)}, u32[]{:S(2)}) copy-start(bf16[384,384]{1,0:T(8,128)(2,1)S(1)} %collective-permute-done.3.refs_2_.refs_11_) | copy-start | bytes 884740
  69.3 10.9 %collective-permute-start.10 = (bf16[384,384]{1,0:T(8,128)(2,1)S(1)}, bf16[384,384]{1,0:T(8,128)(2,1)}, u32[]{:S(2)}, u32[]{:S(2)}) collective-permute-start(bf16[384,384]{1,0:T(8,128)(2,1)S(1)} %collective-permute-done.3.refs_2_.refs_11_), channel_id=1, source_target_pairs={{0,16},{16,32},{32,48},{48,64},{64,80},{80,96},{96,112},{112,0},{1... | collective-permute-start | bytes 884744 | tf_op jit(solution)/shard_map/ppermute | solution.py:177
  69.3 19.1 %copy-start.7 = (bf16[384,384]{1,0:T(8,128)(2,1)}, bf16[384,384]{1,0:T(8,128)(2,1)S(1)}, u32[]{:S(2)}) copy-start(bf16[384,384]{1,0:T(8,128)(2,1)S(1)} %collective-permute-done.9.refs_6_.refs_17_) | copy-start | bytes 884740
  69.3 12.1 %collective-permute-start.13 = (bf16[384,384]{1,0:T(8,128)(2,1)S(1)}, bf16[384,384]{1,0:T(8,128)(2,1)}, u32[]{:S(2)}, u32[]{:S(2)}) collective-permute-start(bf16[384,384]{1,0:T(8,128)(2,1)S(1)} %collective-permute-done.9.refs_6_.refs_17_), channel_id=1, source_target_pairs={{0,112},{16,0},{32,16},{48,32},{64,48},{80,64},{96,80},{112,96},{1... | collective-permute-start | bytes 884744 | tf_op jit(solution)/shard_map/ppermute | solution.py:177
  75.0 12.6 %collective-permute-start.11 = (bf16[384,384]{1,0:T(8,128)(2,1)S(1)}, bf16[384,384]{1,0:T(8,128)(2,1)S(1)}, u32[]{:S(2)}, u32[]{:S(2)}) collective-permute-start(bf16[384,384]{1,0:T(8,128)(2,1)S(1)} %collective-permute-done.5.refs_3_.refs_13_), channel_id=1, source_target_pairs={{0,112},{16,0},{32,16},{48,32},{64,48},{80,64},{96,80},{112,96},{1... | collective-permute-start | bytes 884744 | tf_op jit(solution)/shard_map/ppermute | solution.py:177
  78.0 9.6 %copy-start.9 = (bf16[384,384]{1,0:T(8,128)(2,1)}, bf16[384,384]{1,0:T(8,128)(2,1)S(1)}, u32[]{:S(2)}) copy-start(bf16[384,384]{1,0:T(8,128)(2,1)S(1)} %collective-permute-done.7.refs_5_.refs_15_) | copy-start | bytes 884740
  78.0 10.3 %collective-permute-start.12 = (bf16[384,384]{1,0:T(8,128)(2,1)S(1)}, bf16[384,384]{1,0:T(8,128)(2,1)}, u32[]{:S(2)}, u32[]{:S(2)}) collective-permute-start(bf16[384,384]{1,0:T(8,128)(2,1)S(1)} %collective-permute-done.7.refs_5_.refs_15_), channel_id=1, source_target_pairs={{0,16},{16,32},{32,48},{48,64},{64,80},{80,96},{96,112},{112,0},{1... | collective-permute-start | bytes 884744 | tf_op jit(solution)/shard_map/ppermute | solution.py:177
  80.2 13.5 %collective-permute-start.14 = (bf16[384,384]{1,0:T(8,128)(2,1)}, bf16[384,384]{1,0:T(8,128)(2,1)}, u32[]{:S(2)}, u32[]{:S(2)}) collective-permute-start(bf16[384,384]{1,0:T(8,128)(2,1)} %collective-permute-done.10.refs_8_.refs_19_), channel_id=1, source_target_pairs={{0,16},{16,32},{32,48},{48,64},{64,80},{80,96},{96,112},{112,0},{1... | collective-permute-start | bytes 884744 | tf_op jit(solution)/shard_map/ppermute | solution.py:177
  81.4 12.6 %collective-permute-start.15 = (bf16[384,384]{1,0:T(8,128)(2,1)}, bf16[384,384]{1,0:T(8,128)(2,1)}, u32[]{:S(2)}, u32[]{:S(2)}) collective-permute-start(bf16[384,384]{1,0:T(8,128)(2,1)} %collective-permute-done.13.refs_13_.refs_24_), channel_id=1, source_target_pairs={{0,112},{16,0},{32,16},{48,32},{64,48},{80,64},{96,80},{112,96},{1... | collective-permute-start | bytes 884744 | tf_op jit(solution)/shard_map/ppermute | solution.py:177
  97.8 10.4 %collective-permute-start.17 = (bf16[384,384]{1,0:T(8,128)(2,1)}, bf16[384,384]{1,0:T(8,128)(2,1)S(1)}, u32[]{:S(2)}, u32[]{:S(2)}) collective-permute-start(bf16[384,384]{1,0:T(8,128)(2,1)} %get-tuple-element.14.refs_0_), channel_id=1, source_target_pairs={{0,8},{1,9},{2,10},{3,11},{4,12},{5,13},{6,14},{7,15},{8,0},{9,1},... | collective-permute-start | bytes 884744 | tf_op jit(solution)/shard_map/ppermute | solution.py:203
  98.0 12.8 %collective-permute-start.19 = (bf16[384,384]{1,0:T(8,128)(2,1)}, bf16[384,384]{1,0:T(8,128)(2,1)S(1)}, u32[]{:S(2)}, u32[]{:S(2)}) collective-permute-start(bf16[384,384]{1,0:T(8,128)(2,1)} %get-tuple-element.14.refs_0_), channel_id=1, source_target_pairs={{0,2},{1,3},{2,4},{3,5},{4,6},{5,7},{6,0},{7,1},{8,10},{9,11},{10,... | collective-permute-start | bytes 884744 | tf_op jit(solution)/shard_map/ppermute | solution.py:203
  98.1 14.5 %collective-permute-start.21 = (bf16[384,384]{1,0:T(8,128)(2,1)}, bf16[384,384]{1,0:T(8,128)(2,1)S(1)}, u32[]{:S(2)}, u32[]{:S(2)}) collective-permute-start(bf16[384,384]{1,0:T(8,128)(2,1)} %get-tuple-element.14.refs_0_), channel_id=1, source_target_pairs={{0,6},{1,7},{2,0},{3,1},{4,2},{5,3},{6,4},{7,5},{8,14},{9,15},{10,... | collective-permute-start | bytes 884744 | tf_op jit(solution)/shard_map/ppermute | solution.py:203
  100.6 12.0 %collective-permute-start.23 = (bf16[384,384]{1,0:T(8,128)(2,1)}, bf16[384,384]{1,0:T(8,128)(2,1)S(1)}, u32[]{:S(2)}, u32[]{:S(2)}) collective-permute-start(bf16[384,384]{1,0:T(8,128)(2,1)} %get-tuple-element.14.refs_0_), channel_id=1, source_target_pairs={{0,4},{1,5},{2,6},{3,7},{4,0},{5,1},{6,2},{7,3},{8,12},{9,13},{10,... | collective-permute-start | bytes 884744 | tf_op jit(solution)/shard_map/ppermute | solution.py:203
  101.1 14.2 %collective-permute-start.16 = (bf16[384,384]{1,0:T(8,128)(2,1)}, bf16[384,384]{1,0:T(8,128)(2,1)S(1)}, u32[]{:S(2)}, u32[]{:S(2)}) collective-permute-start(bf16[384,384]{1,0:T(8,128)(2,1)} %get-tuple-element.14.refs_0_), channel_id=1, source_target_pairs={{0,1},{1,0},{2,3},{3,2},{4,5},{5,4},{6,7},{7,6},{8,9},{9,8},{10,11... | collective-permute-start | bytes 884744 | tf_op jit(solution)/shard_map/ppermute | solution.py:207
  108.2 15.9 %copy-start.17 = (bf16[384,384]{1,0:T(8,128)(2,1)}, bf16[384,384]{1,0:T(8,128)(2,1)S(1)}, u32[]{:S(2)}) copy-start(bf16[384,384]{1,0:T(8,128)(2,1)S(1)} %collective-permute-done.17.refs_2_) | copy-start | bytes 884740
  108.2 8.3 %collective-permute-start.18 = (bf16[384,384]{1,0:T(8,128)(2,1)S(1)}, bf16[384,384]{1,0:T(8,128)(2,1)S(1)}, u32[]{:S(2)}, u32[]{:S(2)}) collective-permute-start(bf16[384,384]{1,0:T(8,128)(2,1)S(1)} %collective-permute-done.17.refs_2_), channel_id=1, source_target_pairs={{0,1},{1,0},{2,3},{3,2},{4,5},{5,4},{6,7},{7,6},{8,9},{9,8},{10,11... | collective-permute-start | bytes 884744 | tf_op jit(solution)/shard_map/ppermute | solution.py:207
  110.8 15.1 %copy-start.18 = (bf16[384,384]{1,0:T(8,128)(2,1)}, bf16[384,384]{1,0:T(8,128)(2,1)S(1)}, u32[]{:S(2)}) copy-start(bf16[384,384]{1,0:T(8,128)(2,1)S(1)} %collective-permute-done.19.refs_4_) | copy-start | bytes 884740
  110.8 9.7 %collective-permute-start.20 = (bf16[384,384]{1,0:T(8,128)(2,1)S(1)}, bf16[384,384]{1,0:T(8,128)(2,1)S(1)}, u32[]{:S(2)}, u32[]{:S(2)}) collective-permute-start(bf16[384,384]{1,0:T(8,128)(2,1)S(1)} %collective-permute-done.19.refs_4_), channel_id=1, source_target_pairs={{0,1},{1,0},{2,3},{3,2},{4,5},{5,4},{6,7},{7,6},{8,9},{9,8},{10,11... | collective-permute-start | bytes 884744 | tf_op jit(solution)/shard_map/ppermute | solution.py:207
  112.6 13.2 %copy-start.19 = (bf16[384,384]{1,0:T(8,128)(2,1)}, bf16[384,384]{1,0:T(8,128)(2,1)S(1)}, u32[]{:S(2)}) copy-start(bf16[384,384]{1,0:T(8,128)(2,1)S(1)} %collective-permute-done.21.refs_6_) | copy-start | bytes 884740
  112.6 8.0 %collective-permute-start.25 = (bf16[384,384]{1,0:T(8,128)(2,1)S(1)}, bf16[384,384]{1,0:T(8,128)(2,1)S(1)}, u32[]{:S(2)}, u32[]{:S(2)}) collective-permute-start(bf16[384,384]{1,0:T(8,128)(2,1)S(1)} %collective-permute-done.17.refs_2_), channel_id=1, source_target_pairs={{0,2},{1,3},{2,4},{3,5},{4,6},{5,7},{6,0},{7,1},{8,10},{9,11},{10,... | collective-permute-start | bytes 884744 | tf_op jit(solution)/shard_map/ppermute | solution.py:203
  112.6 13.2 %copy-start.20 = (bf16[384,384]{1,0:T(8,128)(2,1)}, bf16[384,384]{1,0:T(8,128)(2,1)S(1)}, u32[]{:S(2)}) copy-start(bf16[384,384]{1,0:T(8,128)(2,1)S(1)} %collective-permute-done.23.refs_8_) | copy-start | bytes 884740
  112.7 11.1 %collective-permute-start.27 = (bf16[384,384]{1,0:T(8,128)(2,1)S(1)}, bf16[384,384]{1,0:T(8,128)(2,1)S(1)}, u32[]{:S(2)}, u32[]{:S(2)}) collective-permute-start(bf16[384,384]{1,0:T(8,128)(2,1)S(1)} %collective-permute-done.17.refs_2_), channel_id=1, source_target_pairs={{0,6},{1,7},{2,0},{3,1},{4,2},{5,3},{6,4},{7,5},{8,14},{9,15},{10,... | collective-permute-start | bytes 884744 | tf_op jit(solution)/shard_map/ppermute | solution.py:203
  115.3 10.6 %copy-start.21 = (bf16[384,384]{1,0:T(8,128)(2,1)}, bf16[384,384]{1,0:T(8,128)(2,1)S(1)}, u32[]{:S(2)}) copy-start(bf16[384,384]{1,0:T(8,128)(2,1)S(1)} %collective-permute-done.16.refs_1_) | copy-start | bytes 884740
  115.3 8.7 %collective-permute-start.29 = (bf16[384,384]{1,0:T(8,128)(2,1)S(1)}, bf16[384,384]{1,0:T(8,128)(2,1)S(1)}, u32[]{:S(2)}, u32[]{:S(2)}) collective-permute-start(bf16[384,384]{1,0:T(8,128)(2,1)S(1)} %collective-permute-done.23.refs_8_), channel_id=1, source_target_pairs={{0,8},{1,9},{2,10},{3,11},{4,12},{5,13},{6,14},{7,15},{8,0},{9,1},... | collective-permute-start | bytes 884744 | tf_op jit(solution)/shard_map/ppermute | solution.py:203
  116.5 9.4 %copy-start.22 = (bf16[384,384]{1,0:T(8,128)(2,1)}, bf16[384,384]{1,0:T(8,128)(2,1)S(1)}, u32[]{:S(2)}) copy-start(bf16[384,384]{1,0:T(8,128)(2,1)S(1)} %collective-permute-done.18.refs_3_) | copy-start | bytes 884740
  116.5 9.4 %collective-permute-start.22 = (bf16[384,384]{1,0:T(8,128)(2,1)S(1)}, bf16[384,384]{1,0:T(8,128)(2,1)S(1)}, u32[]{:S(2)}, u32[]{:S(2)}) collective-permute-start(bf16[384,384]{1,0:T(8,128)(2,1)S(1)} %collective-permute-done.21.refs_6_), channel_id=1, source_target_pairs={{0,1},{1,0},{2,3},{3,2},{4,5},{5,4},{6,7},{7,6},{8,9},{9,8},{10,11... | collective-permute-start | bytes 884744 | tf_op jit(solution)/shard_map/ppermute | solution.py:207
  120.6 6.1 %collective-permute-start.24 = (bf16[384,384]{1,0:T(8,128)(2,1)S(1)}, bf16[384,384]{1,0:T(8,128)(2,1)}, u32[]{:S(2)}, u32[]{:S(2)}) collective-permute-start(bf16[384,384]{1,0:T(8,128)(2,1)S(1)} %collective-permute-done.23.refs_8_), channel_id=1, source_target_pairs={{0,1},{1,0},{2,3},{3,2},{4,5},{5,4},{6,7},{7,6},{8,9},{9,8},{10,11... | collective-permute-start | bytes 884744 | tf_op jit(solution)/shard_map/ppermute | solution.py:207
  120.7 13.2 %copy-start.11 = (bf16[384,384]{1,0:T(8,128)(2,1)}, bf16[384,384]{1,0:T(8,128)(2,1)S(1)}, u32[]{:S(2)}) copy-start(bf16[384,384]{1,0:T(8,128)(2,1)S(1)} %collective-permute-done.25.refs_0_) | copy-start | bytes 884740
  120.7 13.2 %collective-permute-start.26 = (bf16[384,384]{1,0:T(8,128)(2,1)S(1)}, bf16[384,384]{1,0:T(8,128)(2,1)S(1)}, u32[]{:S(2)}, u32[]{:S(2)}) collective-permute-start(bf16[384,384]{1,0:T(8,128)(2,1)S(1)} %collective-permute-done.25.refs_0_), channel_id=1, source_target_pairs={{0,1},{1,0},{2,3},{3,2},{4,5},{5,4},{6,7},{7,6},{8,9},{9,8},{10,11... | collective-permute-start | bytes 884744 | tf_op jit(solution)/shard_map/ppermute | solution.py:207
  123.7 10.2 %copy-start.12 = (bf16[384,384]{1,0:T(8,128)(2,1)}, bf16[384,384]{1,0:T(8,128)(2,1)S(1)}, u32[]{:S(2)}) copy-start(bf16[384,384]{1,0:T(8,128)(2,1)S(1)} %collective-permute-done.27.refs_2_) | copy-start | bytes 884740
  123.7 10.1 %collective-permute-start.28 = (bf16[384,384]{1,0:T(8,128)(2,1)S(1)}, bf16[384,384]{1,0:T(8,128)(2,1)S(1)}, u32[]{:S(2)}, u32[]{:S(2)}) collective-permute-start(bf16[384,384]{1,0:T(8,128)(2,1)S(1)} %collective-permute-done.27.refs_2_), channel_id=1, source_target_pairs={{0,1},{1,0},{2,3},{3,2},{4,5},{5,4},{6,7},{7,6},{8,9},{9,8},{10,11... | collective-permute-start | bytes 884744 | tf_op jit(solution)/shard_map/ppermute | solution.py:207
  124.1 9.9 %copy-start.13 = (bf16[384,384]{1,0:T(8,128)(2,1)}, bf16[384,384]{1,0:T(8,128)(2,1)S(1)}, u32[]{:S(2)}) copy-start(bf16[384,384]{1,0:T(8,128)(2,1)S(1)} %collective-permute-done.29.refs_4_) | copy-start | bytes 884740
  124.1 9.8 %collective-permute-start.30 = (bf16[384,384]{1,0:T(8,128)(2,1)S(1)}, bf16[384,384]{1,0:T(8,128)(2,1)S(1)}, u32[]{:S(2)}, u32[]{:S(2)}) collective-permute-start(bf16[384,384]{1,0:T(8,128)(2,1)S(1)} %collective-permute-done.29.refs_4_), channel_id=1, source_target_pairs={{0,1},{1,0},{2,3},{3,2},{4,5},{5,4},{6,7},{7,6},{8,9},{9,8},{10,11... | collective-permute-start | bytes 884744 | tf_op jit(solution)/shard_map/ppermute | solution.py:207
  (9 other events, 17.0 us)
Sparse Core Ops, SparseCore 0:
  49.0 37.6 all-gather.1

commit v4 on v3

--- a/solution.py
+++ b/solution.py
@@ -213,6 +213,7 @@
     for by in (1, 3, 2):
         found.append((0, by, plane_step(tile, 0, by)))
     far = found[-1][2]
+    far, _ = lax.optimization_barrier((far, other))
     for by in (1, 3):
         found.append((1, by, plane_step(other, 0, by)))
     found.append((1, 2, plane_step(far, 1, 0)))
@@ -294,79 +295,43 @@
     return pl.ds(pl.multiple_of((distance % 2 * 8 + half * 4 + distance // 2) * TILE, TILE), TILE)
 
 
-def early_kernel(early, late, *refs):
-    count = len(early)
-    tile_refs, column_refs, refs = refs[:count], refs[count : count + NROW], refs[count + NROW :]
-    out, rest, strip, column, sems, rest_sems = refs
-    copies = [pltpu.make_async_copy(ref, column.at[n * TILE : (n + 1) * TILE, :], sems.at[n]) for n, ref in enumerate(column_refs)]
-    for n, ref in enumerate(tile_refs):
-        copies.append(pltpu.make_async_copy(ref, strip.at[:, n * TILE : (n + 1) * TILE], sems.at[NROW + n]))
-    settle(run(copies))
-    leaving = []
-    for n, place in enumerate(late):
-        to = rest.at[n * TILE : (n + 1) * TILE, :]
-        leaving.append(pltpu.make_async_copy(column.at[rows_for(*place), :], to, rest_sems.at[n]))
-    run(leaving)
-    for n, place in enumerate(early):
-        part = jnp.dot(strip[:, n * TILE : (n + 1) * TILE], column[rows_for(*place), :], preferred_element_type=F32)
+def cube_kernel(places, square_ref, *refs):
+    tile_refs, column_refs, refs = refs[:NROW], refs[NROW : 2 * NROW], refs[2 * NROW :]
+    out, square, strip, column, sems = refs
+    copies = [pltpu.make_async_copy(ref, strip.at[:, rows_for(*place)], sems.at[n]) for n, (ref, place) in enumerate(zip(tile_refs, places))]
+    for n, ref in enumerate(column_refs):
+        copies.append(pltpu.make_async_copy(ref, column.at[n * TILE : (n + 1) * TILE, :], sems.at[NROW + n]))
+    copies.append(pltpu.make_async_copy(square_ref, square, sems.at[2 * NROW]))
+    run(copies)
+    settle(copies[:NROW])
+    for n in range(0, NROW, 4):
+        settle(copies[NROW + n : NROW + n + 4])
+        span = slice(n * TILE, (n + 4) * TILE)
+        part = jnp.dot(strip[:, span], column[span, :], preferred_element_type=F32)
         if n == 0:
             out[...] = part
+        elif n < NROW - 4:
+            out[...] += part
         else:
-            out[...] += part
-    settle(leaving)
-
-
-def early_of(tiles, columns, early, late):
-    count = len(early)
-    return pl.pallas_call(
-        functools.partial(early_kernel, early, late),
-        out_shape=[
-            jax.ShapeDtypeStruct((TILE, TILE), F32),
-            jax.ShapeDtypeStruct((len(late) * TILE, TILE), jnp.bfloat16),
-        ],
-        in_specs=[ANY] * (count + NROW),
-        out_specs=[VMEM, ANY],
+            settle(copies[2 * NROW :])
+            out[...] = 3.0 * square[...] - 2.0 * (out[...] + part)
+
+
+def cube_of(square, tiles, columns, places):
+    return pl.pallas_call(
+        functools.partial(cube_kernel, places),
+        out_shape=jax.ShapeDtypeStruct((TILE, TILE), F32),
+        in_specs=[ANY] * (1 + 2 * NROW),
+        out_specs=VMEM,
         scratch_shapes=[
-            pltpu.VMEM((TILE, count * TILE), jnp.bfloat16),
+            pltpu.VMEM((TILE, TILE), F32),
+            pltpu.VMEM((TILE, NROW * TILE), jnp.bfloat16),
             pltpu.VMEM((NROW * TILE, TILE), jnp.bfloat16),
-            pltpu.SemaphoreType.DMA((NROW + count,)),
-            pltpu.SemaphoreType.DMA((len(late),)),
+            pltpu.SemaphoreType.DMA((2 * NROW + 1,)),
         ],
         compiler_params=BIG,
         cost_estimate=cost(NROW),
-    )(*tiles, *columns)
-
-
-def late_kernel(count, square_ref, held_ref, rest_ref, *refs):
-    tile_refs, (out, square, held, rest, strip, sems) = refs[:count], refs[count:]
-    copies = [pltpu.make_async_copy(ref, strip.at[:, n * TILE : (n + 1) * TILE], sems.at[n]) for n, ref in enumerate(tile_refs)]
-    for n, (ref, to) in enumerate(((rest_ref, rest), (square_ref, square), (held_ref, held))):
-        copies.append(pltpu.make_async_copy(ref, to, sems.at[count + n]))
-    settle(run(copies))
-    part = jnp.dot(strip[...], rest[...], preferred_element_type=F32)
-    out[...] = 3.0 * square[...] - 2.0 * (held[...] + part)
-
-
-def late_of(square, held, rest, tiles):
-    count = len(tiles)
-    return pl.pallas_call(
-        functools.partial(late_kernel, count),
-        out_shape=jax.ShapeDtypeStruct((TILE, TILE), F32),
-        in_specs=[ANY] * (3 + count),
-        out_specs=VMEM,
-        scratch_shapes=[
-            pltpu.VMEM((TILE, TILE), F32),
-            pltpu.VMEM((TILE, TILE), F32),
-            pltpu.VMEM((count * TILE, TILE), jnp.bfloat16),
-            pltpu.VMEM((TILE, count * TILE), jnp.bfloat16),
-            pltpu.SemaphoreType.DMA((3 + count,)),
-        ],
-        compiler_params=BIG,
-        cost_estimate=cost(count),
-    )(square, held, rest, *tiles)
-
-
-EARLY = 10
+    )(square, *tiles, *columns)
 
 
 def per_device(charges, hubbard, coupling, orbital_atom, block_mask, bare_ham, intersection):
@@ -380,8 +345,7 @@
     square, square_low = square_of(initial_strip, held, found, LAST)
     tiles = square_tiles(square_low)
     places, values = [tile[:3] for tile in tiles], [tile[3] for tile in tiles]
-    held, rest = early_of(values[:EARLY], [found[place] for place in ORDER], places[:EARLY], places[EARLY:])
-    return late_of(square, held, rest, values[EARLY:])
+    return cube_of(square, values, [found[place] for place in ORDER], places)
 
 
 def solution(mesh):

time: 146 us -> 144 us (0.986)
  waiting for transfers between devices: 20.1 us -> 34.5 us
  starting transfers between devices: 50.6 us -> 39.7 us
  Pallas kernels: 27.4 us -> 22.7 us
    ppermute x7, waiting for transfers between devices: 0.02 us -> 6.89 us  [plane_step(): return lax.ppermute(value, 'col', pairs)]
    ppermute x14, waiting for transfers between devices: 20 us -> 26.5 us  [ring_step(): lax.ppermute(value, 'row', [(h * RING + i, h * RING + (i + by) % RING) fo...]
    ppermute x14, starting transfers between devices: 19 us -> 13.1 us  [ring_step(): lax.ppermute(value, 'row', [(h * RING + i, h * RING + (i + by) % RING) fo...]
    pallas_call x2 -> x1, Pallas kernels: 11.5 us -> 6.76 us  [cube_of(): pl.pallas_call(functools.partial(cube_kernel, places), out_shape=jax.Shap...]
    ppermute x8, starting transfers between devices: 20.9 us -> 17.4 us  [swap_core(): return lax.ppermute(value, 'col', [(i, i ^ 1) for i in range(NROW)])]
    ppermute x7, starting transfers between devices: 7.09 us -> 5.6 us  [plane_step(): return lax.ppermute(value, 'col', pairs)]
    unnamed x50 -> x52, local copies, waits for them, and re-layouts: 3.76 us -> 2.94 us
  transfers between devices with their start and end apart: 32 -> 32, of which waited for: 8 -> 11; matrix products, arithmetic and copies ran while one was open for 0% -> 0% of each run, Pallas kernels for 10% -> 5%
where the time goes in v4:
time: 144 us
  starting transfers between devices  39.7 us (28%)
  waiting for transfers between devices  34.5 us (24%)
  blocking collectives  30.4 us (21%)
  Pallas kernels  22.7 us (16%)
  between operations  13.7 us (10%)
  local copies, waits for them, and re-layouts  2.94 us (2%)
    all_to_all x2, blocking collectives, exchange(): lax.all_to_all(copies, ('row', 'col'), 0, 0, axis_index_groups=members)  30.4 us
    ppermute x14, waiting for transfers between devices, ring_step(): lax.ppermute(value, 'row', [(h * RING + i, h * RING + (i + by) % RING) fo...  26.5 us
    ppermute x8, starting transfers between devices, swap_core(): return lax.ppermute(value, 'col', [(i, i ^ 1) for i in range(NROW)])  17.4 us
    ppermute x14, starting transfers between devices, ring_step(): lax.ppermute(value, 'row', [(h * RING + i, h * RING + (i + by) % RING) fo...  13.1 us
    pallas_call x2, Pallas kernels, square_of(): pl.pallas_call(functools.partial(square_kernel, places, not held), out_sh...  9.01 us
    ppermute x7, waiting for transfers between devices, plane_step(): return lax.ppermute(value, 'col', pairs)  6.89 us
    pallas_call x1, Pallas kernels, cube_of(): pl.pallas_call(functools.partial(cube_kernel, places), out_shape=jax.Shap...  6.76 us
    ppermute x7, starting transfers between devices, plane_step(): return lax.ppermute(value, 'col', pairs)  5.6 us
  transfers between devices with their start and end apart: 32, of which 11 were waited for; matrix products, arithmetic and copies ran while one was open for 0% of the time, Pallas kernels for 5%

profile of v4, /device:TPU:1, one launch (start us, length us, event | category | flops | bytes accessed | tf_op | source)
XLA Modules:
  0.0 143.9 jit_solution(14651612908569737071)
XLA Ops:
  6.5 3.6 %collective-permute-start = (bf16[384,384]{1,0:T(8,128)(2,1)}, bf16[384,384]{1,0:T(8,128)(2,1)S(1)}, u32[]{:S(2)}, u32[]{:S(2)}) collective-permute-start(bf16[384,384]{1,0:T(8,128)(2,1)} %bare.1), channel_id=1, source_target_pairs={{0,128},{16,144},{32,160},{48,176},{64,192},{80,208},{96,224},{112... | collective-permute-start | bytes 884744 | tf_op jit(solution)/shard_map/ppermute | solution.py:181
  10.1 1.4 shard_map.73
  11.6 16.8 %all_to_all.10.parts = f32[16,1,128]{2,1,0:T(1,128)} all-to-all(f32[16,1,128]{2,1,0:T(1,128)} %shard_map.73), channel_id=1, replica_groups={{0,1,16,17,32,33,48,49,64,65,80,81,96,97,112,113},{2,3,18,19,34,35,50,5..., dimensions={0} | all-to-all | bytes 16384 | tf_op jit(solution)/shard_map/all_to_all | solution.py:81
  28.4 0.7 copy-done
  29.1 0.7 copy-done.1
  29.8 1.4 shard_map.74
  31.2 13.6 %all_to_all.11.parts = f32[16,16,128]{2,1,0:T(8,128)} all-to-all(f32[16,16,128]{2,1,0:T(8,128)} %shard_map.74), channel_id=1, replica_groups={{0,2,4,6,8,10,12,14,128,130,132,134,136,138,140,142},{1,3,5,7,9,11,13,1..., dimensions={0} | all-to-all | bytes 262144 | tf_op jit(solution)/shard_map/all_to_all | solution.py:81
  44.7 4.2 %shard_map.75 = (bf16[384,384]{1,0:T(8,128)(2,1)}, bf16[384,384]{1,0:T(8,128)(2,1)}) custom-call(f32[16,16,128]{2,1,0:T(8,128)} %all_to_all.11.parts, f32[3,3]{1,0:T(4,128)} %coupling.1, bf16[384,384]{1,0:T(8,128)(2,1)} %bare.1, bf16[384,384]{1,0:T(8,128)(2,1)} %inter.1, bf16[384,384]{1,0:T(8,128)(2,1)} %copy-done, bf16[384,384]{1,0:T(8,128)(2,1)} %copy-done.1), custom_call_target="tpu_custom_call" | custom-call | tf_op jit(solution)/shard_map/pallas_call | solution.py:167
  48.9 0.5 collective-permute-start.8
  49.4 1.1 collective-permute-start.2
  50.4 0.6 collective-permute-start.6
  51.0 2.1 %collective-permute-start.4 = (bf16[384,384]{1,0:T(8,128)(2,1)}, bf16[384,384]{1,0:T(8,128)(2,1)S(1)}, u32[]{:S(2)}, u32[]{:S(2)}) collective-permute-start(bf16[384,384]{1,0:T(8,128)(2,1)} %get-tuple-element.10.refs_1_.refs_16_), channel_id=1, source_target_pairs={{0,112},{16,0},{32,16},{48,32},{64,48},{80,64},{96,80},{112,96},{1... | collective-permute-start | bytes 884744 | tf_op jit(solution)/shard_map/ppermute | solution.py:177
  53.1 2.3 %collective-permute-done.8.refs_14_.refs_31_ = bf16[384,384]{1,0:T(8,128)(2,1)S(1)} collective-permute-done((bf16[384,384]{1,0:T(8,128)(2,1)}, bf16[384,384]{1,0:T(8,128)(2,1)S(1)}, u32[]{:S(2)}, u32[]{:S(2)}) %collective-permute-start.8) | collective-permute-done | bytes 294944 | tf_op jit(solution)/shard_map/ppermute | solution.py:177
  55.5 1.5 %collective-permute-start.9 = (bf16[384,384]{1,0:T(8,128)(2,1)S(1)}, bf16[384,384]{1,0:T(8,128)(2,1)S(1)}, u32[]{:S(2)}, u32[]{:S(2)}) collective-permute-start(bf16[384,384]{1,0:T(8,128)(2,1)S(1)} %collective-permute-done.8.refs_14_.refs_31_), channel_id=1, source_target_pairs={{0,112},{16,0},{32,16},{48,32},{64,48},{80,64},{96,80},{112,96},{1... | collective-permute-start | bytes 884744 | tf_op jit(solution)/shard_map/ppermute | solution.py:177
  56.9 6.0 %collective-permute-done.6.refs_11_.refs_28_ = bf16[384,384]{1,0:T(8,128)(2,1)S(1)} collective-permute-done((bf16[384,384]{1,0:T(8,128)(2,1)}, bf16[384,384]{1,0:T(8,128)(2,1)S(1)}, u32[]{:S(2)}, u32[]{:S(2)}) %collective-permute-start.6) | collective-permute-done | bytes 294944 | tf_op jit(solution)/shard_map/ppermute | solution.py:177
  63.0 0.1 collective-permute-start.7
  63.1 2.6 %collective-permute-start.5 = (bf16[384,384]{1,0:T(8,128)(2,1)S(1)}, bf16[384,384]{1,0:T(8,128)(2,1)S(1)}, u32[]{:S(2)}, u32[]{:S(2)}) collective-permute-start(bf16[384,384]{1,0:T(8,128)(2,1)S(1)} %collective-permute-done.4.refs_10_.refs_27_), channel_id=1, source_target_pairs={{0,112},{16,0},{32,16},{48,32},{64,48},{80,64},{96,80},{112,96},{1... | collective-permute-start | bytes 884744 | tf_op jit(solution)/shard_map/ppermute | solution.py:177
  65.7 2.5 %collective-permute-done.9.refs_6_.refs_23_ = bf16[384,384]{1,0:T(8,128)(2,1)S(1)} collective-permute-done((bf16[384,384]{1,0:T(8,128)(2,1)S(1)}, bf16[384,384]{1,0:T(8,128)(2,1)S(1)}, u32[]{:S(2)}, u32[]{:S(2)}) %collective-permute-start.9) | collective-permute-done | bytes 294944 | tf_op jit(solution)/shard_map/ppermute | solution.py:177
  68.2 1.7 %collective-permute-start.13 = (bf16[384,384]{1,0:T(8,128)(2,1)S(1)}, bf16[384,384]{1,0:T(8,128)(2,1)}, u32[]{:S(2)}, u32[]{:S(2)}) collective-permute-start(bf16[384,384]{1,0:T(8,128)(2,1)S(1)} %collective-permute-done.9.refs_6_.refs_23_), channel_id=1, source_target_pairs={{0,112},{16,0},{32,16},{48,32},{64,48},{80,64},{96,80},{112,96},{1... | collective-permute-start | bytes 884744 | tf_op jit(solution)/shard_map/ppermute | solution.py:177
  69.9 5.7 %collective-permute-done.7.refs_5_.refs_21_ = bf16[384,384]{1,0:T(8,128)(2,1)S(1)} collective-permute-done((bf16[384,384]{1,0:T(8,128)(2,1)S(1)}, bf16[384,384]{1,0:T(8,128)(2,1)S(1)}, u32[]{:S(2)}, u32[]{:S(2)}) %collective-permute-start.7) | collective-permute-done | bytes 294944 | tf_op jit(solution)/shard_map/ppermute | solution.py:177
  75.6 0.1 collective-permute-start.12
  75.7 2.6 %collective-permute-start.11 = (bf16[384,384]{1,0:T(8,128)(2,1)S(1)}, bf16[384,384]{1,0:T(8,128)(2,1)}, u32[]{:S(2)}, u32[]{:S(2)}) collective-permute-start(bf16[384,384]{1,0:T(8,128)(2,1)S(1)} %collective-permute-done.5.refs_3_.refs_19_), channel_id=1, source_target_pairs={{0,112},{16,0},{32,16},{48,32},{64,48},{80,64},{96,80},{112,96},{1... | collective-permute-start | bytes 884744 | tf_op jit(solution)/shard_map/ppermute | solution.py:177
  78.3 2.5 %collective-permute-done.13.refs_13_.refs_30_ = bf16[384,384]{1,0:T(8,128)(2,1)} collective-permute-done((bf16[384,384]{1,0:T(8,128)(2,1)S(1)}, bf16[384,384]{1,0:T(8,128)(2,1)}, u32[]{:S(2)}, u32[]{:S(2)}) %collective-permute-start.13) | collective-permute-done | bytes 294944 | tf_op jit(solution)/shard_map/ppermute | solution.py:177
  80.8 1.1 collective-permute-done.10.refs_8_.refs_25_
  81.9 0.4 collective-permute-start.14
  82.3 6.0 %collective-permute-done.12.refs_12_.refs_29_ = bf16[384,384]{1,0:T(8,128)(2,1)S(1)} collective-permute-done((bf16[384,384]{1,0:T(8,128)(2,1)S(1)}, bf16[384,384]{1,0:T(8,128)(2,1)S(1)}, u32[]{:S(2)}, u32[]{:S(2)}) %collective-permute-start.12) | collective-permute-done | bytes 294944 | tf_op jit(solution)/shard_map/ppermute | solution.py:177
  88.4 0.7 copy-done.10
  89.1 5.3 %shard_map.76.refs_1_ = f32[384,384]{1,0:T(8,128)} custom-call(bf16[384,6144]{1,0:T(8,128)(2,1)} %all-gather.2.cloned.1.call-done.refs_0_, bf16[384,384]{1,0:T(8,128)(2,1)} %get-tuple-element.10.refs_1_.refs_16_, bf16[384,384]{1,0:T(8,128)(2,1)} %copy-done.7, bf16[384,384]{1,0:T(8,128)(2,1)} %copy-done.9, ...), custom_call_target="tpu_custom_call" | custom-call | flops 1585446912 | bytes 8257536 | tf_op jit(solution)/shard_map/pallas_call | solution.py:267
  94.4 0.2 collective-permute-done.14.refs_2_.refs_18_
  94.6 3.7 %shard_map.77 = (f32[384,384]{1,0:T(8,128)}, bf16[384,384]{1,0:T(8,128)(2,1)}) custom-call(bf16[384,6144]{1,0:T(8,128)(2,1)} %all-gather.2.cloned.1.call-done.refs_0_, f32[384,384]{1,0:T(8,128)} %shard_map.76.refs_1_, bf16[384,384]{1,0:T(8,128)(2,1)} %collective-permute-done.14.refs_2_.refs_18_, bf16[384,384]{1,0:T(8,128)(2,1)} %collective-permute-done.15.refs_3_.refs_22_), custom_call_target="tpu_custom_call" | custom-call | flops 226492416 | bytes 1179648 | tf_op jit(solution)/shard_map/pallas_call | solution.py:267
  98.3 1.3 collective-permute-start.23
  99.6 0.2 collective-permute-start.17
  99.8 1.4 collective-permute-start.21
  101.3 7.6 %collective-permute-start.16 = (bf16[384,384]{1,0:T(8,128)(2,1)}, bf16[384,384]{1,0:T(8,128)(2,1)S(1)}, u32[]{:S(2)}, u32[]{:S(2)}) collective-permute-start(bf16[384,384]{1,0:T(8,128)(2,1)} %get-tuple-element.13.refs_0_), channel_id=1, source_target_pairs={{0,1},{1,0},{2,3},{3,2},{4,5},{5,4},{6,7},{7,6},{8,9},{9,8},{10,11... | collective-permute-start | bytes 884744 | tf_op jit(solution)/shard_map/ppermute | solution.py:207
  108.9 4.5 %collective-permute-start.24 = (bf16[384,384]{1,0:T(8,128)(2,1)S(1)}, bf16[384,384]{1,0:T(8,128)(2,1)S(1)}, u32[]{:S(2)}, u32[]{:S(2)}) collective-permute-start(bf16[384,384]{1,0:T(8,128)(2,1)S(1)} %collective-permute-done.23.refs_8_), channel_id=1, source_target_pairs={{0,1},{1,0},{2,3},{3,2},{4,5},{5,4},{6,7},{7,6},{8,9},{9,8},{10,11... | collective-permute-start | bytes 884744 | tf_op jit(solution)/shard_map/ppermute | solution.py:207
  113.4 1.6 %collective-permute-start.22 = (bf16[384,384]{1,0:T(8,128)(2,1)S(1)}, bf16[384,384]{1,0:T(8,128)(2,1)S(1)}, u32[]{:S(2)}, u32[]{:S(2)}) collective-permute-start(bf16[384,384]{1,0:T(8,128)(2,1)S(1)} %collective-permute-done.21.refs_6_), channel_id=1, source_target_pairs={{0,1},{1,0},{2,3},{3,2},{4,5},{5,4},{6,7},{7,6},{8,9},{9,8},{10,11... | collective-permute-start | bytes 884744 | tf_op jit(solution)/shard_map/ppermute | solution.py:207
  115.1 0.1 collective-permute-start.29
  115.2 2.5 %collective-permute-start.27 = (bf16[384,384]{1,0:T(8,128)(2,1)S(1)}, bf16[384,384]{1,0:T(8,128)(2,1)S(1)}, u32[]{:S(2)}, u32[]{:S(2)}) collective-permute-start(bf16[384,384]{1,0:T(8,128)(2,1)S(1)} %collective-permute-done.17.refs_2_), channel_id=1, source_target_pairs={{0,6},{1,7},{2,0},{3,1},{4,2},{5,3},{6,4},{7,5},{8,14},{9,15},{10,... | collective-permute-start | bytes 884744 | tf_op jit(solution)/shard_map/ppermute | solution.py:203
  117.7 1.0 collective-permute-start.18
  118.7 0.1 collective-permute-start.20
  118.8 4.9 %collective-permute-done.29.refs_14_ = bf16[384,384]{1,0:T(8,128)(2,1)S(1)} collective-permute-done((bf16[384,384]{1,0:T(8,128)(2,1)S(1)}, bf16[384,384]{1,0:T(8,128)(2,1)S(1)}, u32[]{:S(2)}, u32[]{:S(2)}) %collective-permute-start.29) | collective-permute-done | bytes 294944 | tf_op jit(solution)/shard_map/ppermute | solution.py:203
  123.7 0.8 collective-permute-start.30
  124.5 0.4 collective-permute-start.28
  124.9 2.0 %collective-permute-done.25.refs_10_ = bf16[384,384]{1,0:T(8,128)(2,1)S(1)} collective-permute-done((bf16[384,384]{1,0:T(8,128)(2,1)S(1)}, bf16[384,384]{1,0:T(8,128)(2,1)S(1)}, u32[]{:S(2)}, u32[]{:S(2)}) %collective-permute-start.25) | collective-permute-done | bytes 294944 | tf_op jit(solution)/shard_map/ppermute | solution.py:203
  126.9 1.4 collective-permute-start.26
  128.4 1.1 collective-permute-done.26.refs_11_
  129.5 0.7 copy-done.25
  130.3 6.8 %shard_map.78 = f32[384,384]{1,0:T(8,128)} custom-call(f32[384,384]{1,0:T(8,128)} %get-tuple-element.12.square_ref, bf16[384,384]{1,0:T(8,128)(2,1)} %get-tuple-element.13.refs_0_, bf16[384,384]{1,0:T(8,128)(2,1)} %copy-done.15, bf16[384,384]{1,0:T(8,128)(2,1)} %copy-done.12, bf16[384,384]{1,0:T(8,128)(2,1)} %copy-done.21, bf16[384,384]{1,0:T(8,128)(2,1)} %copy-done.14, ...), custom_call_target="tpu_custom_call" | custom-call | flops 1811939328 | bytes 9437184 | tf_op jit(solution)/shard_map/pallas_call | solution.py:321
  (77 shorter events, 0.3 us)
Async XLA Ops:
  6.5 82.5 %all-gather.2.cloned.1.call-start = ((), (), s32[]{:S(2)}) async-start(), calls=%async_computation.2 | async-start | bytes 5013504 | tf_op jit(solution)/shard_map/all_gather | solution.py:342
  6.5 21.8 %collective-permute-start = (bf16[384,384]{1,0:T(8,128)(2,1)}, bf16[384,384]{1,0:T(8,128)(2,1)S(1)}, u32[]{:S(2)}, u32[]{:S(2)}) collective-permute-start(bf16[384,384]{1,0:T(8,128)(2,1)} %bare.1), channel_id=1, source_target_pairs={{0,128},{16,144},{32,160},{48,176},{64,192},{80,208},{96,224},{112... | collective-permute-start | bytes 884744 | tf_op jit(solution)/shard_map/ppermute | solution.py:181
  10.1 18.2 %collective-permute-start.1 = (bf16[384,384]{1,0:T(8,128)(2,1)}, bf16[384,384]{1,0:T(8,128)(2,1)S(1)}, u32[]{:S(2)}, u32[]{:S(2)}) collective-permute-start(bf16[384,384]{1,0:T(8,128)(2,1)} %inter.1), channel_id=1, source_target_pairs={{0,128},{16,144},{32,160},{48,176},{64,192},{80,208},{96,224},{112... | collective-permute-start | bytes 884744 | tf_op jit(solution)/shard_map/ppermute | solution.py:181
  48.9 6.6 %collective-permute-start.8 = (bf16[384,384]{1,0:T(8,128)(2,1)}, bf16[384,384]{1,0:T(8,128)(2,1)S(1)}, u32[]{:S(2)}, u32[]{:S(2)}) collective-permute-start(bf16[384,384]{1,0:T(8,128)(2,1)} %get-tuple-element.11.refs_4_.refs_20_), channel_id=1, source_target_pairs={{0,112},{16,0},{32,16},{48,32},{64,48},{80,64},{96,80},{112,96},{1... | collective-permute-start | bytes 884744 | tf_op jit(solution)/shard_map/ppermute | solution.py:177
  49.4 7.6 %collective-permute-start.2 = (bf16[384,384]{1,0:T(8,128)(2,1)}, bf16[384,384]{1,0:T(8,128)(2,1)S(1)}, u32[]{:S(2)}, u32[]{:S(2)}) collective-permute-start(bf16[384,384]{1,0:T(8,128)(2,1)} %get-tuple-element.10.refs_1_.refs_16_), channel_id=1, source_target_pairs={{0,16},{16,32},{32,48},{48,64},{64,80},{80,96},{96,112},{112,0},{1... | collective-permute-start | bytes 884744 | tf_op jit(solution)/shard_map/ppermute | solution.py:177
  50.4 12.5 %collective-permute-start.6 = (bf16[384,384]{1,0:T(8,128)(2,1)}, bf16[384,384]{1,0:T(8,128)(2,1)S(1)}, u32[]{:S(2)}, u32[]{:S(2)}) collective-permute-start(bf16[384,384]{1,0:T(8,128)(2,1)} %get-tuple-element.11.refs_4_.refs_20_), channel_id=1, source_target_pairs={{0,16},{16,32},{32,48},{48,64},{64,80},{80,96},{96,112},{112,0},{1... | collective-permute-start | bytes 884744 | tf_op jit(solution)/shard_map/ppermute | solution.py:177
  51.0 12.1 %collective-permute-start.4 = (bf16[384,384]{1,0:T(8,128)(2,1)}, bf16[384,384]{1,0:T(8,128)(2,1)S(1)}, u32[]{:S(2)}, u32[]{:S(2)}) collective-permute-start(bf16[384,384]{1,0:T(8,128)(2,1)} %get-tuple-element.10.refs_1_.refs_16_), channel_id=1, source_target_pairs={{0,112},{16,0},{32,16},{48,32},{64,48},{80,64},{96,80},{112,96},{1... | collective-permute-start | bytes 884744 | tf_op jit(solution)/shard_map/ppermute | solution.py:177
  55.5 33.6 %copy-start.2 = (bf16[384,384]{1,0:T(8,128)(2,1)}, bf16[384,384]{1,0:T(8,128)(2,1)S(1)}, u32[]{:S(2)}) copy-start(bf16[384,384]{1,0:T(8,128)(2,1)S(1)} %collective-permute-done.8.refs_14_.refs_31_) | copy-start | bytes 884740
  55.5 12.7 %collective-permute-start.9 = (bf16[384,384]{1,0:T(8,128)(2,1)S(1)}, bf16[384,384]{1,0:T(8,128)(2,1)S(1)}, u32[]{:S(2)}, u32[]{:S(2)}) collective-permute-start(bf16[384,384]{1,0:T(8,128)(2,1)S(1)} %collective-permute-done.8.refs_14_.refs_31_), channel_id=1, source_target_pairs={{0,112},{16,0},{32,16},{48,32},{64,48},{80,64},{96,80},{112,96},{1... | collective-permute-start | bytes 884744 | tf_op jit(solution)/shard_map/ppermute | solution.py:177
  56.9 32.1 %copy-start.3 = (bf16[384,384]{1,0:T(8,128)(2,1)}, bf16[384,384]{1,0:T(8,128)(2,1)S(1)}, u32[]{:S(2)}) copy-start(bf16[384,384]{1,0:T(8,128)(2,1)S(1)} %collective-permute-done.2.refs_7_.refs_24_) | copy-start | bytes 884740
  56.9 12.9 %collective-permute-start.3 = (bf16[384,384]{1,0:T(8,128)(2,1)S(1)}, bf16[384,384]{1,0:T(8,128)(2,1)S(1)}, u32[]{:S(2)}, u32[]{:S(2)}) collective-permute-start(bf16[384,384]{1,0:T(8,128)(2,1)S(1)} %collective-permute-done.2.refs_7_.refs_24_), channel_id=1, source_target_pairs={{0,16},{16,32},{32,48},{48,64},{64,80},{80,96},{96,112},{112,0},{1... | collective-permute-start | bytes 884744 | tf_op jit(solution)/shard_map/ppermute | solution.py:177
  63.0 26.1 %copy-start.4 = (bf16[384,384]{1,0:T(8,128)(2,1)}, bf16[384,384]{1,0:T(8,128)(2,1)S(1)}, u32[]{:S(2)}) copy-start(bf16[384,384]{1,0:T(8,128)(2,1)S(1)} %collective-permute-done.6.refs_11_.refs_28_) | copy-start | bytes 884740
  63.0 12.6 %collective-permute-start.7 = (bf16[384,384]{1,0:T(8,128)(2,1)S(1)}, bf16[384,384]{1,0:T(8,128)(2,1)S(1)}, u32[]{:S(2)}, u32[]{:S(2)}) collective-permute-start(bf16[384,384]{1,0:T(8,128)(2,1)S(1)} %collective-permute-done.6.refs_11_.refs_28_), channel_id=1, source_target_pairs={{0,16},{16,32},{32,48},{48,64},{64,80},{80,96},{96,112},{112,0},{1... | collective-permute-start | bytes 884744 | tf_op jit(solution)/shard_map/ppermute | solution.py:177
  63.1 26.0 %copy-start.5 = (bf16[384,384]{1,0:T(8,128)(2,1)}, bf16[384,384]{1,0:T(8,128)(2,1)S(1)}, u32[]{:S(2)}) copy-start(bf16[384,384]{1,0:T(8,128)(2,1)S(1)} %collective-permute-done.4.refs_10_.refs_27_) | copy-start | bytes 884740
  63.1 12.6 %collective-permute-start.5 = (bf16[384,384]{1,0:T(8,128)(2,1)S(1)}, bf16[384,384]{1,0:T(8,128)(2,1)S(1)}, u32[]{:S(2)}, u32[]{:S(2)}) collective-permute-start(bf16[384,384]{1,0:T(8,128)(2,1)S(1)} %collective-permute-done.4.refs_10_.refs_27_), channel_id=1, source_target_pairs={{0,112},{16,0},{32,16},{48,32},{64,48},{80,64},{96,80},{112,96},{1... | collective-permute-start | bytes 884744 | tf_op jit(solution)/shard_map/ppermute | solution.py:177
  68.2 20.9 %copy-start.6 = (bf16[384,384]{1,0:T(8,128)(2,1)}, bf16[384,384]{1,0:T(8,128)(2,1)S(1)}, u32[]{:S(2)}) copy-start(bf16[384,384]{1,0:T(8,128)(2,1)S(1)} %collective-permute-done.9.refs_6_.refs_23_) | copy-start | bytes 884740
  68.2 12.6 %collective-permute-start.13 = (bf16[384,384]{1,0:T(8,128)(2,1)S(1)}, bf16[384,384]{1,0:T(8,128)(2,1)}, u32[]{:S(2)}, u32[]{:S(2)}) collective-permute-start(bf16[384,384]{1,0:T(8,128)(2,1)S(1)} %collective-permute-done.9.refs_6_.refs_23_), channel_id=1, source_target_pairs={{0,112},{16,0},{32,16},{48,32},{64,48},{80,64},{96,80},{112,96},{1... | collective-permute-start | bytes 884744 | tf_op jit(solution)/shard_map/ppermute | solution.py:177
  69.9 19.2 %copy-start.7 = (bf16[384,384]{1,0:T(8,128)(2,1)}, bf16[384,384]{1,0:T(8,128)(2,1)S(1)}, u32[]{:S(2)}) copy-start(bf16[384,384]{1,0:T(8,128)(2,1)S(1)} %collective-permute-done.3.refs_2_.refs_17_) | copy-start | bytes 884740
  69.9 12.0 %collective-permute-start.10 = (bf16[384,384]{1,0:T(8,128)(2,1)S(1)}, bf16[384,384]{1,0:T(8,128)(2,1)}, u32[]{:S(2)}, u32[]{:S(2)}) collective-permute-start(bf16[384,384]{1,0:T(8,128)(2,1)S(1)} %collective-permute-done.3.refs_2_.refs_17_), channel_id=1, source_target_pairs={{0,16},{16,32},{32,48},{48,64},{64,80},{80,96},{96,112},{112,0},{1... | collective-permute-start | bytes 884744 | tf_op jit(solution)/shard_map/ppermute | solution.py:177
  75.6 6.3 %copy-start.8 = (bf16[384,384]{1,0:T(8,128)(2,1)}, bf16[384,384]{1,0:T(8,128)(2,1)S(1)}, u32[]{:S(2)}) copy-start(bf16[384,384]{1,0:T(8,128)(2,1)S(1)} %collective-permute-done.7.refs_5_.refs_21_) | copy-start | bytes 884740
  75.6 12.7 %collective-permute-start.12 = (bf16[384,384]{1,0:T(8,128)(2,1)S(1)}, bf16[384,384]{1,0:T(8,128)(2,1)S(1)}, u32[]{:S(2)}, u32[]{:S(2)}) collective-permute-start(bf16[384,384]{1,0:T(8,128)(2,1)S(1)} %collective-permute-done.7.refs_5_.refs_21_), channel_id=1, source_target_pairs={{0,16},{16,32},{32,48},{48,64},{64,80},{80,96},{96,112},{112,0},{1... | collective-permute-start | bytes 884744 | tf_op jit(solution)/shard_map/ppermute | solution.py:177
  75.7 12.6 %copy-start.9 = (bf16[384,384]{1,0:T(8,128)(2,1)}, bf16[384,384]{1,0:T(8,128)(2,1)S(1)}, u32[]{:S(2)}) copy-start(bf16[384,384]{1,0:T(8,128)(2,1)S(1)} %collective-permute-done.5.refs_3_.refs_19_) | copy-start | bytes 884740
  75.7 13.4 %collective-permute-start.11 = (bf16[384,384]{1,0:T(8,128)(2,1)S(1)}, bf16[384,384]{1,0:T(8,128)(2,1)}, u32[]{:S(2)}, u32[]{:S(2)}) collective-permute-start(bf16[384,384]{1,0:T(8,128)(2,1)S(1)} %collective-permute-done.5.refs_3_.refs_19_), channel_id=1, source_target_pairs={{0,112},{16,0},{32,16},{48,32},{64,48},{80,64},{96,80},{112,96},{1... | collective-permute-start | bytes 884744 | tf_op jit(solution)/shard_map/ppermute | solution.py:177
  80.8 13.6 %collective-permute-start.15 = (bf16[384,384]{1,0:T(8,128)(2,1)}, bf16[384,384]{1,0:T(8,128)(2,1)}, u32[]{:S(2)}, u32[]{:S(2)}) collective-permute-start(bf16[384,384]{1,0:T(8,128)(2,1)} %collective-permute-done.13.refs_13_.refs_30_), channel_id=1, source_target_pairs={{0,112},{16,0},{32,16},{48,32},{64,48},{80,64},{96,80},{112,96},{1... | collective-permute-start | bytes 884744 | tf_op jit(solution)/shard_map/ppermute | solution.py:177
  81.9 12.6 %collective-permute-start.14 = (bf16[384,384]{1,0:T(8,128)(2,1)}, bf16[384,384]{1,0:T(8,128)(2,1)}, u32[]{:S(2)}, u32[]{:S(2)}) collective-permute-start(bf16[384,384]{1,0:T(8,128)(2,1)} %collective-permute-done.10.refs_8_.refs_25_), channel_id=1, source_target_pairs={{0,16},{16,32},{32,48},{48,64},{64,80},{80,96},{96,112},{112,0},{1... | collective-permute-start | bytes 884744 | tf_op jit(solution)/shard_map/ppermute | solution.py:177
  98.3 10.6 %collective-permute-start.23 = (bf16[384,384]{1,0:T(8,128)(2,1)}, bf16[384,384]{1,0:T(8,128)(2,1)S(1)}, u32[]{:S(2)}, u32[]{:S(2)}) collective-permute-start(bf16[384,384]{1,0:T(8,128)(2,1)} %get-tuple-element.13.refs_0_), channel_id=1, source_target_pairs={{0,4},{1,5},{2,6},{3,7},{4,0},{5,1},{6,2},{7,3},{8,12},{9,13},{10,... | collective-permute-start | bytes 884744 | tf_op jit(solution)/shard_map/ppermute | solution.py:203
  99.6 9.3 %collective-permute-start.17 = (bf16[384,384]{1,0:T(8,128)(2,1)}, bf16[384,384]{1,0:T(8,128)(2,1)S(1)}, u32[]{:S(2)}, u32[]{:S(2)}) collective-permute-start(bf16[384,384]{1,0:T(8,128)(2,1)} %get-tuple-element.13.refs_0_), channel_id=1, source_target_pairs={{0,8},{1,9},{2,10},{3,11},{4,12},{5,13},{6,14},{7,15},{8,0},{9,1},... | collective-permute-start | bytes 884744 | tf_op jit(solution)/shard_map/ppermute | solution.py:203
  99.8 13.6 %collective-permute-start.21 = (bf16[384,384]{1,0:T(8,128)(2,1)}, bf16[384,384]{1,0:T(8,128)(2,1)S(1)}, u32[]{:S(2)}, u32[]{:S(2)}) collective-permute-start(bf16[384,384]{1,0:T(8,128)(2,1)} %get-tuple-element.13.refs_0_), channel_id=1, source_target_pairs={{0,6},{1,7},{2,0},{3,1},{4,2},{5,3},{6,4},{7,5},{8,14},{9,15},{10,... | collective-permute-start | bytes 884744 | tf_op jit(solution)/shard_map/ppermute | solution.py:203
  101.2 13.9 %collective-permute-start.19 = (bf16[384,384]{1,0:T(8,128)(2,1)}, bf16[384,384]{1,0:T(8,128)(2,1)S(1)}, u32[]{:S(2)}, u32[]{:S(2)}) collective-permute-start(bf16[384,384]{1,0:T(8,128)(2,1)} %get-tuple-element.13.refs_0_), channel_id=1, source_target_pairs={{0,2},{1,3},{2,4},{3,5},{4,6},{5,7},{6,0},{7,1},{8,10},{9,11},{10,... | collective-permute-start | bytes 884744 | tf_op jit(solution)/shard_map/ppermute | solution.py:203
  101.3 16.3 %collective-permute-start.16 = (bf16[384,384]{1,0:T(8,128)(2,1)}, bf16[384,384]{1,0:T(8,128)(2,1)S(1)}, u32[]{:S(2)}, u32[]{:S(2)}) collective-permute-start(bf16[384,384]{1,0:T(8,128)(2,1)} %get-tuple-element.13.refs_0_), channel_id=1, source_target_pairs={{0,1},{1,0},{2,3},{3,2},{4,5},{5,4},{6,7},{7,6},{8,9},{9,8},{10,11... | collective-permute-start | bytes 884744 | tf_op jit(solution)/shard_map/ppermute | solution.py:207
  108.9 21.3 %copy-start.11 = (bf16[384,384]{1,0:T(8,128)(2,1)}, bf16[384,384]{1,0:T(8,128)(2,1)S(1)}, u32[]{:S(2)}) copy-start(bf16[384,384]{1,0:T(8,128)(2,1)S(1)} %collective-permute-done.23.refs_8_) | copy-start | bytes 884740
  108.9 21.3 %copy-start.12 = (bf16[384,384]{1,0:T(8,128)(2,1)}, bf16[384,384]{1,0:T(8,128)(2,1)S(1)}, u32[]{:S(2)}) copy-start(bf16[384,384]{1,0:T(8,128)(2,1)S(1)} %collective-permute-done.17.refs_2_) | copy-start | bytes 884740
  108.9 8.7 %collective-permute-start.24 = (bf16[384,384]{1,0:T(8,128)(2,1)S(1)}, bf16[384,384]{1,0:T(8,128)(2,1)S(1)}, u32[]{:S(2)}, u32[]{:S(2)}) collective-permute-start(bf16[384,384]{1,0:T(8,128)(2,1)S(1)} %collective-permute-done.23.refs_8_), channel_id=1, source_target_pairs={{0,1},{1,0},{2,3},{3,2},{4,5},{5,4},{6,7},{7,6},{8,9},{9,8},{10,11... | collective-permute-start | bytes 884744 | tf_op jit(solution)/shard_map/ppermute | solution.py:207
  113.4 16.8 %copy-start.13 = (bf16[384,384]{1,0:T(8,128)(2,1)}, bf16[384,384]{1,0:T(8,128)(2,1)S(1)}, u32[]{:S(2)}) copy-start(bf16[384,384]{1,0:T(8,128)(2,1)S(1)} %collective-permute-done.21.refs_6_) | copy-start | bytes 884740
  113.4 5.3 %collective-permute-start.22 = (bf16[384,384]{1,0:T(8,128)(2,1)S(1)}, bf16[384,384]{1,0:T(8,128)(2,1)S(1)}, u32[]{:S(2)}, u32[]{:S(2)}) collective-permute-start(bf16[384,384]{1,0:T(8,128)(2,1)S(1)} %collective-permute-done.21.refs_6_), channel_id=1, source_target_pairs={{0,1},{1,0},{2,3},{3,2},{4,5},{5,4},{6,7},{7,6},{8,9},{9,8},{10,11... | collective-permute-start | bytes 884744 | tf_op jit(solution)/shard_map/ppermute | solution.py:207
  115.1 8.6 %collective-permute-start.29 = (bf16[384,384]{1,0:T(8,128)(2,1)S(1)}, bf16[384,384]{1,0:T(8,128)(2,1)S(1)}, u32[]{:S(2)}, u32[]{:S(2)}) collective-permute-start(bf16[384,384]{1,0:T(8,128)(2,1)S(1)} %collective-permute-done.23.refs_8_), channel_id=1, source_target_pairs={{0,8},{1,9},{2,10},{3,11},{4,12},{5,13},{6,14},{7,15},{8,0},{9,1},... | collective-permute-start | bytes 884744 | tf_op jit(solution)/shard_map/ppermute | solution.py:203
  115.2 15.1 %copy-start.14 = (bf16[384,384]{1,0:T(8,128)(2,1)}, bf16[384,384]{1,0:T(8,128)(2,1)S(1)}, u32[]{:S(2)}) copy-start(bf16[384,384]{1,0:T(8,128)(2,1)S(1)} %collective-permute-done.19.refs_4_) | copy-start | bytes 884740
  115.2 9.3 %collective-permute-start.27 = (bf16[384,384]{1,0:T(8,128)(2,1)S(1)}, bf16[384,384]{1,0:T(8,128)(2,1)S(1)}, u32[]{:S(2)}, u32[]{:S(2)}) collective-permute-start(bf16[384,384]{1,0:T(8,128)(2,1)S(1)} %collective-permute-done.17.refs_2_), channel_id=1, source_target_pairs={{0,6},{1,7},{2,0},{3,1},{4,2},{5,3},{6,4},{7,5},{8,14},{9,15},{10,... | collective-permute-start | bytes 884744 | tf_op jit(solution)/shard_map/ppermute | solution.py:203
  117.7 12.6 %copy-start.15 = (bf16[384,384]{1,0:T(8,128)(2,1)}, bf16[384,384]{1,0:T(8,128)(2,1)S(1)}, u32[]{:S(2)}) copy-start(bf16[384,384]{1,0:T(8,128)(2,1)S(1)} %collective-permute-done.16.refs_1_) | copy-start | bytes 884740
  117.7 9.2 %collective-permute-start.25 = (bf16[384,384]{1,0:T(8,128)(2,1)S(1)}, bf16[384,384]{1,0:T(8,128)(2,1)S(1)}, u32[]{:S(2)}, u32[]{:S(2)}) collective-permute-start(bf16[384,384]{1,0:T(8,128)(2,1)S(1)} %collective-permute-done.17.refs_2_), channel_id=1, source_target_pairs={{0,2},{1,3},{2,4},{3,5},{4,6},{5,7},{6,0},{7,1},{8,10},{9,11},{10,... | collective-permute-start | bytes 884744 | tf_op jit(solution)/shard_map/ppermute | solution.py:203
  117.7 12.6 %copy-start.16 = (bf16[384,384]{1,0:T(8,128)(2,1)}, bf16[384,384]{1,0:T(8,128)(2,1)S(1)}, u32[]{:S(2)}) copy-start(bf16[384,384]{1,0:T(8,128)(2,1)S(1)} %collective-permute-done.24.refs_9_) | copy-start | bytes 884740
  117.7 10.6 %collective-permute-start.18 = (bf16[384,384]{1,0:T(8,128)(2,1)S(1)}, bf16[384,384]{1,0:T(8,128)(2,1)S(1)}, u32[]{:S(2)}, u32[]{:S(2)}) collective-permute-start(bf16[384,384]{1,0:T(8,128)(2,1)S(1)} %collective-permute-done.17.refs_2_), channel_id=1, source_target_pairs={{0,1},{1,0},{2,3},{3,2},{4,5},{5,4},{6,7},{7,6},{8,9},{9,8},{10,11... | collective-permute-start | bytes 884744 | tf_op jit(solution)/shard_map/ppermute | solution.py:207
  118.7 9.6 %copy-start.17 = (bf16[384,384]{1,0:T(8,128)(2,1)}, bf16[384,384]{1,0:T(8,128)(2,1)S(1)}, u32[]{:S(2)}) copy-start(bf16[384,384]{1,0:T(8,128)(2,1)S(1)} %collective-permute-done.22.refs_7_) | copy-start | bytes 884740
  118.7 9.6 %collective-permute-start.20 = (bf16[384,384]{1,0:T(8,128)(2,1)S(1)}, bf16[384,384]{1,0:T(8,128)(2,1)S(1)}, u32[]{:S(2)}, u32[]{:S(2)}) collective-permute-start(bf16[384,384]{1,0:T(8,128)(2,1)S(1)} %collective-permute-done.19.refs_4_), channel_id=1, source_target_pairs={{0,1},{1,0},{2,3},{3,2},{4,5},{5,4},{6,7},{7,6},{8,9},{9,8},{10,11... | collective-permute-start | bytes 884744 | tf_op jit(solution)/shard_map/ppermute | solution.py:207
  123.7 4.6 %copy-start.18 = (bf16[384,384]{1,0:T(8,128)(2,1)}, bf16[384,384]{1,0:T(8,128)(2,1)S(1)}, u32[]{:S(2)}) copy-start(bf16[384,384]{1,0:T(8,128)(2,1)S(1)} %collective-permute-done.29.refs_14_) | copy-start | bytes 884740
  123.7 4.6 %collective-permute-start.30 = (bf16[384,384]{1,0:T(8,128)(2,1)S(1)}, bf16[384,384]{1,0:T(8,128)(2,1)S(1)}, u32[]{:S(2)}, u32[]{:S(2)}) collective-permute-start(bf16[384,384]{1,0:T(8,128)(2,1)S(1)} %collective-permute-done.29.refs_14_), channel_id=1, source_target_pairs={{0,1},{1,0},{2,3},{3,2},{4,5},{5,4},{6,7},{7,6},{8,9},{9,8},{10,11... | collective-permute-start | bytes 884744 | tf_op jit(solution)/shard_map/ppermute | solution.py:207
  124.5 3.9 %collective-permute-start.28 = (bf16[384,384]{1,0:T(8,128)(2,1)S(1)}, bf16[384,384]{1,0:T(8,128)(2,1)S(1)}, u32[]{:S(2)}, u32[]{:S(2)}) collective-permute-start(bf16[384,384]{1,0:T(8,128)(2,1)S(1)} %collective-permute-done.27.refs_12_), channel_id=1, source_target_pairs={{0,1},{1,0},{2,3},{3,2},{4,5},{5,4},{6,7},{7,6},{8,9},{9,8},{10,11... | collective-permute-start | bytes 884744 | tf_op jit(solution)/shard_map/ppermute | solution.py:207
  126.9 2.6 %collective-permute-start.26 = (bf16[384,384]{1,0:T(8,128)(2,1)S(1)}, bf16[384,384]{1,0:T(8,128)(2,1)S(1)}, u32[]{:S(2)}, u32[]{:S(2)}) collective-permute-start(bf16[384,384]{1,0:T(8,128)(2,1)S(1)} %collective-permute-done.25.refs_10_), channel_id=1, source_target_pairs={{0,1},{1,0},{2,3},{3,2},{4,5},{5,4},{6,7},{7,6},{8,9},{9,8},{10,11... | collective-permute-start | bytes 884744 | tf_op jit(solution)/shard_map/ppermute | solution.py:207
  (10 other events, 14.1 us)
Sparse Core Ops, SparseCore 0:
  49.0 37.6 all-gather.1

commit v5 on v4

--- a/solution.py
+++ b/solution.py
@@ -90,25 +90,27 @@
     return jnp.concatenate([part.astype(F32) for part in parts], axis=1)
 
 
-def domain_row(parts, spread, q):
+def domain_row(parts, spread, q, wanted=range(13)):
     half, z = q // RING, q % RING
     domain = iota((NROW, LANES), 0)
     lane = iota((NROW, LANES), 1)
     block = parts[pl.ds(half * RING, RING), pl.ds(z * 2, 2), :]
     block = jnp.concatenate([block[n // 2, n % 2 : n % 2 + 1] for n in range(NROW)], axis=0)
-    wide = jnp.dot(block, spread, precision=HIGH, preferred_element_type=F32)
+    start = wanted[0]
+    lanes = slice(start * LANES, (start + len(wanted)) * LANES)
+    wide = jnp.dot(block, spread[:, lanes], precision=HIGH, preferred_element_type=F32)
     rows = []
-    for i in range(13):
+    for i in wanted:
         here = lane % 64 // 4 == domain
         if 6 <= i < 9:
             here = (lane + LANES * (i - 6)) // ORBD == domain
-        piece = wide[:, i * LANES : (i + 1) * LANES]
+        piece = wide[:, (i - start) * LANES : (i - start + 1) * LANES]
         rows.append(jnp.sum(jnp.where(here, piece, 0.0), axis=0, keepdims=True))
     return rows
 
 
 def row_shift(above, here, below, coupling):
-    atoms = [above[2], here[0], here[1], here[2], below[0]]
+    atoms = [above[0], here[0], here[1], here[2], below[0]]
     rolled = [[pltpu.roll(v, 1, 1), v, pltpu.roll(v, LANES - 1, 1)] for v in atoms]
     grids = []
     for i in range(3):
@@ -151,7 +153,8 @@
     spread = spread_of()
 
     def around(q):
-        return [domain_row(parts, spread, (q + by) % NROW) for by in (NROW - 1, 0, 1)]
+        above = domain_row(parts, spread, (q + NROW - 1) % NROW, range(2, 3))
+        return above, domain_row(parts, spread, q), domain_row(parts, spread, (q + 1) % NROW, range(1))
 
     along = row_shift(*around(col), coupling)
     for q, ham, overlap, to in ((row, bare, inter, out), ((row + RING) % NROW, bare_other, inter_other, out_other)):
@@ -246,8 +249,8 @@
         copies.append(pltpu.make_async_copy(tile_refs[n], column.at[n * TILE : (n + 1) * TILE, :], sems.at[2 * n]))
         copies.append(pltpu.make_async_copy(source, strip.at[:, n * TILE : (n + 1) * TILE], sems.at[2 * n + 1]))
     run(copies)
-    for n in range(0, count, 4):
-        upto = min(n + 4, count)
+    for n in range(0, count, 2):
+        upto = min(n + 2, count)
         settle(copies[2 * n : 2 * upto])
         span = slice(n * TILE, upto * TILE)
         part = jnp.dot(strip[:, span], column[span, :], preferred_element_type=F32)
@@ -274,7 +277,7 @@
             pltpu.VMEM((count * TILE, TILE), jnp.bfloat16),
             pltpu.SemaphoreType.DMA((2 * count,)),
         ],
-        compiler_params=BIG,
+        compiler_params=pltpu.CompilerParams(vmem_limit_bytes=16 << 20),
         cost_estimate=cost(count),
     )(strip, *held, *[found[place] for place in places])
 
@@ -304,13 +307,13 @@
     copies.append(pltpu.make_async_copy(square_ref, square, sems.at[2 * NROW]))
     run(copies)
     settle(copies[:NROW])
-    for n in range(0, NROW, 4):
-        settle(copies[NROW + n : NROW + n + 4])
-        span = slice(n * TILE, (n + 4) * TILE)
+    for n in range(0, NROW, 2):
+        settle(copies[NROW + n : NROW + n + 2])
+        span = slice(n * TILE, (n + 2) * TILE)
         part = jnp.dot(strip[:, span], column[span, :], preferred_element_type=F32)
         if n == 0:
             out[...] = part
-        elif n < NROW - 4:
+        elif n < NROW - 2:
             out[...] += part
         else:
             settle(copies[2 * NROW :])
@@ -329,7 +332,7 @@
             pltpu.VMEM((NROW * TILE, TILE), jnp.bfloat16),
             pltpu.SemaphoreType.DMA((2 * NROW + 1,)),
         ],
-        compiler_params=BIG,
+        compiler_params=pltpu.CompilerParams(vmem_limit_bytes=16 << 20),
         cost_estimate=cost(NROW),
     )(square, *tiles, *columns)
 

time: 144 us -> 143 us (level)
  Pallas kernels: 22.7 us -> 19 us
  local copies, waits for them, and re-layouts: 2.94 us -> 5.68 us
    pallas_call x2, Pallas kernels: 9.01 us -> 5.95 us  [square_of(): pl.pallas_call(functools.partial(square_kernel, places, not held), out_sh...]
    unnamed x52 -> x12, local copies, waits for them, and re-layouts: 2.94 us -> 5.68 us
  transfers between devices with their start and end apart: 32 -> 32, of which waited for: 11 -> 10; matrix products, arithmetic and copies ran while one was open for 0% -> 0% of each run, Pallas kernels for 5% -> 4%
where the time goes in v5:
time: 143 us
  starting transfers between devices  39.8 us (28%)
  waiting for transfers between devices  34.4 us (24%)
  blocking collectives  30.4 us (21%)
  Pallas kernels  19 us (13%)
  between operations  13.5 us (9%)
  local copies, waits for them, and re-layouts  5.68 us (4%)
    all_to_all x2, blocking collectives, exchange(): lax.all_to_all(copies, ('row', 'col'), 0, 0, axis_index_groups=members)  30.4 us
    ppermute x14, waiting for transfers between devices, ring_step(): lax.ppermute(value, 'row', [(h * RING + i, h * RING + (i + by) % RING) fo...  26.2 us
    ppermute x8, starting transfers between devices, swap_core(): return lax.ppermute(value, 'col', [(i, i ^ 1) for i in range(NROW)])  17.5 us
    ppermute x14, starting transfers between devices, ring_step(): lax.ppermute(value, 'row', [(h * RING + i, h * RING + (i + by) % RING) fo...  13.1 us
    ppermute x7, waiting for transfers between devices, plane_step(): return lax.ppermute(value, 'col', pairs)  6.93 us
    pallas_call x1, Pallas kernels, cube_of(): pl.pallas_call(functools.partial(cube_kernel, places), out_shape=jax.Shap...  6.13 us
    pallas_call x2, Pallas kernels, square_of(): pl.pallas_call(functools.partial(square_kernel, places, not held), out_sh...  5.95 us
    unnamed x12, local copies, waits for them, and re-layouts  5.68 us
  transfers between devices with their start and end apart: 32, of which 10 were waited for; matrix products, arithmetic and copies ran while one was open for 0% of the time, Pallas kernels for 4%

profile of v5, /device:TPU:1, one launch (start us, length us, event | category | flops | bytes accessed | tf_op | source)
XLA Modules:
  0.0 142.7 jit_solution(3016334153956606037)
XLA Ops:
  6.5 3.6 %collective-permute-start = (bf16[384,384]{1,0:T(8,128)(2,1)}, bf16[384,384]{1,0:T(8,128)(2,1)S(1)}, u32[]{:S(2)}, u32[]{:S(2)}) collective-permute-start(bf16[384,384]{1,0:T(8,128)(2,1)} %bare.1), channel_id=1, source_target_pairs={{0,128},{16,144},{32,160},{48,176},{64,192},{80,208},{96,224},{112... | collective-permute-start | bytes 884744 | tf_op jit(solution)/shard_map/ppermute | solution.py:184
  10.1 1.4 shard_map.73
  11.6 16.8 %all_to_all.10.parts = f32[16,1,128]{2,1,0:T(1,128)} all-to-all(f32[16,1,128]{2,1,0:T(1,128)} %shard_map.73), channel_id=1, replica_groups={{0,1,16,17,32,33,48,49,64,65,80,81,96,97,112,113},{2,3,18,19,34,35,50,5..., dimensions={0} | all-to-all | bytes 16384 | tf_op jit(solution)/shard_map/all_to_all | solution.py:81
  28.4 0.7 copy-done.4
  29.1 0.7 copy-done.5
  29.8 1.4 shard_map.74
  31.1 13.6 %all_to_all.11.parts = f32[16,16,128]{2,1,0:T(8,128)} all-to-all(f32[16,16,128]{2,1,0:T(8,128)} %shard_map.74), channel_id=1, replica_groups={{0,2,4,6,8,10,12,14,128,130,132,134,136,138,140,142},{1,3,5,7,9,11,13,1..., dimensions={0} | all-to-all | bytes 262144 | tf_op jit(solution)/shard_map/all_to_all | solution.py:81
  44.7 4.1 %shard_map.75 = (bf16[384,384]{1,0:T(8,128)(2,1)}, bf16[384,384]{1,0:T(8,128)(2,1)}) custom-call(f32[16,16,128]{2,1,0:T(8,128)} %all_to_all.11.parts, f32[3,3]{1,0:T(4,128)} %coupling.1, bf16[384,384]{1,0:T(8,128)(2,1)} %bare.1, bf16[384,384]{1,0:T(8,128)(2,1)} %inter.1, bf16[384,384]{1,0:T(8,128)(2,1)} %copy-done.4, bf16[384,384]{1,0:T(8,128)(2,1)} %copy-done.5), custom_call_target="tpu_custom_call" | custom-call | tf_op jit(solution)/shard_map/pallas_call | solution.py:170
  48.9 0.5 collective-permute-start.8
  49.3 1.1 collective-permute-start.2
  50.4 0.6 collective-permute-start.6
  51.0 2.1 %collective-permute-start.4 = (bf16[384,384]{1,0:T(8,128)(2,1)}, bf16[384,384]{1,0:T(8,128)(2,1)S(1)}, u32[]{:S(2)}, u32[]{:S(2)}) collective-permute-start(bf16[384,384]{1,0:T(8,128)(2,1)} %get-tuple-element.10.refs_1_.refs_16_), channel_id=1, source_target_pairs={{0,112},{16,0},{32,16},{48,32},{64,48},{80,64},{96,80},{112,96},{1... | collective-permute-start | bytes 884744 | tf_op jit(solution)/shard_map/ppermute | solution.py:180
  53.1 2.3 %collective-permute-done.8.refs_14_.refs_31_ = bf16[384,384]{1,0:T(8,128)(2,1)S(1)} collective-permute-done((bf16[384,384]{1,0:T(8,128)(2,1)}, bf16[384,384]{1,0:T(8,128)(2,1)S(1)}, u32[]{:S(2)}, u32[]{:S(2)}) %collective-permute-start.8) | collective-permute-done | bytes 294944 | tf_op jit(solution)/shard_map/ppermute | solution.py:180
  55.4 1.5 %collective-permute-start.9 = (bf16[384,384]{1,0:T(8,128)(2,1)S(1)}, bf16[384,384]{1,0:T(8,128)(2,1)S(1)}, u32[]{:S(2)}, u32[]{:S(2)}) collective-permute-start(bf16[384,384]{1,0:T(8,128)(2,1)S(1)} %collective-permute-done.8.refs_14_.refs_31_), channel_id=1, source_target_pairs={{0,112},{16,0},{32,16},{48,32},{64,48},{80,64},{96,80},{112,96},{1... | collective-permute-start | bytes 884744 | tf_op jit(solution)/shard_map/ppermute | solution.py:180
  56.9 6.0 %collective-permute-done.6.refs_11_.refs_28_ = bf16[384,384]{1,0:T(8,128)(2,1)S(1)} collective-permute-done((bf16[384,384]{1,0:T(8,128)(2,1)}, bf16[384,384]{1,0:T(8,128)(2,1)S(1)}, u32[]{:S(2)}, u32[]{:S(2)}) %collective-permute-start.6) | collective-permute-done | bytes 294944 | tf_op jit(solution)/shard_map/ppermute | solution.py:180
  62.9 0.1 collective-permute-start.7
  63.0 2.6 %collective-permute-start.5 = (bf16[384,384]{1,0:T(8,128)(2,1)S(1)}, bf16[384,384]{1,0:T(8,128)(2,1)S(1)}, u32[]{:S(2)}, u32[]{:S(2)}) collective-permute-start(bf16[384,384]{1,0:T(8,128)(2,1)S(1)} %collective-permute-done.4.refs_10_.refs_27_), channel_id=1, source_target_pairs={{0,112},{16,0},{32,16},{48,32},{64,48},{80,64},{96,80},{112,96},{1... | collective-permute-start | bytes 884744 | tf_op jit(solution)/shard_map/ppermute | solution.py:180
  65.6 2.6 %collective-permute-done.9.refs_6_.refs_23_ = bf16[384,384]{1,0:T(8,128)(2,1)S(1)} collective-permute-done((bf16[384,384]{1,0:T(8,128)(2,1)S(1)}, bf16[384,384]{1,0:T(8,128)(2,1)S(1)}, u32[]{:S(2)}, u32[]{:S(2)}) %collective-permute-start.9) | collective-permute-done | bytes 294944 | tf_op jit(solution)/shard_map/ppermute | solution.py:180
  68.2 1.7 %collective-permute-start.13 = (bf16[384,384]{1,0:T(8,128)(2,1)S(1)}, bf16[384,384]{1,0:T(8,128)(2,1)S(1)}, u32[]{:S(2)}, u32[]{:S(2)}) collective-permute-start(bf16[384,384]{1,0:T(8,128)(2,1)S(1)} %collective-permute-done.9.refs_6_.refs_23_), channel_id=1, source_target_pairs={{0,112},{16,0},{32,16},{48,32},{64,48},{80,64},{96,80},{112,96},{1... | collective-permute-start | bytes 884744 | tf_op jit(solution)/shard_map/ppermute | solution.py:180
  69.8 5.7 %collective-permute-done.7.refs_5_.refs_21_ = bf16[384,384]{1,0:T(8,128)(2,1)S(1)} collective-permute-done((bf16[384,384]{1,0:T(8,128)(2,1)S(1)}, bf16[384,384]{1,0:T(8,128)(2,1)S(1)}, u32[]{:S(2)}, u32[]{:S(2)}) %collective-permute-start.7) | collective-permute-done | bytes 294944 | tf_op jit(solution)/shard_map/ppermute | solution.py:180
  75.6 0.1 collective-permute-start.12
  75.7 2.6 %collective-permute-start.11 = (bf16[384,384]{1,0:T(8,128)(2,1)S(1)}, bf16[384,384]{1,0:T(8,128)(2,1)S(1)}, u32[]{:S(2)}, u32[]{:S(2)}) collective-permute-start(bf16[384,384]{1,0:T(8,128)(2,1)S(1)} %collective-permute-done.5.refs_3_.refs_19_), channel_id=1, source_target_pairs={{0,112},{16,0},{32,16},{48,32},{64,48},{80,64},{96,80},{112,96},{1... | collective-permute-start | bytes 884744 | tf_op jit(solution)/shard_map/ppermute | solution.py:180
  78.2 2.6 %collective-permute-done.13.refs_13_.refs_30_ = bf16[384,384]{1,0:T(8,128)(2,1)S(1)} collective-permute-done((bf16[384,384]{1,0:T(8,128)(2,1)S(1)}, bf16[384,384]{1,0:T(8,128)(2,1)S(1)}, u32[]{:S(2)}, u32[]{:S(2)}) %collective-permute-start.13) | collective-permute-done | bytes 294944 | tf_op jit(solution)/shard_map/ppermute | solution.py:180
  80.8 1.1 collective-permute-done.10.refs_8_.refs_25_
  81.9 0.4 collective-permute-start.14
  82.3 5.9 %collective-permute-done.12.refs_12_.refs_29_ = bf16[384,384]{1,0:T(8,128)(2,1)S(1)} collective-permute-done((bf16[384,384]{1,0:T(8,128)(2,1)S(1)}, bf16[384,384]{1,0:T(8,128)(2,1)S(1)}, u32[]{:S(2)}, u32[]{:S(2)}) %collective-permute-start.12) | collective-permute-done | bytes 294944 | tf_op jit(solution)/shard_map/ppermute | solution.py:180
  88.2 2.3 %copy-done = bf16[384,6144]{1,0:T(8,128)(2,1)S(1)} copy-done((bf16[384,6144]{1,0:T(8,128)(2,1)S(1)}, bf16[384,6144]{1,0:T(8,128)(2,1)}, u32[]{:S(2)}) %copy-start) | copy-done | bytes 4718616
  90.5 1.0 copy-done.2
  91.5 1.0 copy-done.3
  92.5 4.4 %shard_map.76.refs_1_ = f32[384,384]{1,0:T(8,128)S(1)} custom-call(bf16[384,6144]{1,0:T(8,128)(2,1)S(1)} %copy-done, bf16[384,384]{1,0:T(8,128)(2,1)S(1)} %copy-done.2, bf16[384,384]{1,0:T(8,128)(2,1)S(1)} %collective-permute-done.3.refs_2_.refs_17_, bf16[384,384]{1,0:T(8,128)(2,1)S(1)} %collective-permute-done.5.refs_3_.refs_19_, ...), custom_call_target="tpu_custom_call" | custom-call | flops 1585446912 | bytes 8257536 | tf_op jit(solution)/shard_map/pallas_call | solution.py:270
  96.9 1.6 %shard_map.77 = (f32[384,384]{1,0:T(8,128)S(1)}, bf16[384,384]{1,0:T(8,128)(2,1)S(1)}) custom-call(bf16[384,6144]{1,0:T(8,128)(2,1)S(1)} %copy-done.1, f32[384,384]{1,0:T(8,128)S(1)} %shard_map.76.refs_1_, bf16[384,384]{1,0:T(8,128)(2,1)} %collective-permute-done.14.refs_2_.refs_18_, bf16[384,384]{1,0:T(8,128)(2,1)} %collective-permute-done.15.refs_3_.refs_22_), custom_call_target="tpu_custom_call" | custom-call | flops 226492416 | bytes 1179648 | tf_op jit(solution)/shard_map/pallas_call | solution.py:270
  98.5 1.3 collective-permute-start.23
  99.8 0.2 collective-permute-start.17
  100.0 1.3 collective-permute-start.21
  101.3 0.1 collective-permute-start.19
  101.5 7.8 %collective-permute-start.16 = (bf16[384,384]{1,0:T(8,128)(2,1)S(1)}, bf16[384,384]{1,0:T(8,128)(2,1)S(1)}, u32[]{:S(2)}, u32[]{:S(2)}) collective-permute-start(bf16[384,384]{1,0:T(8,128)(2,1)S(1)} %get-tuple-element.13.refs_0_), channel_id=1, source_target_pairs={{0,1},{1,0},{2,3},{3,2},{4,5},{5,4},{6,7},{7,6},{8,9},{9,8},{10,11... | collective-permute-start | bytes 884744 | tf_op jit(solution)/shard_map/ppermute | solution.py:210
  109.3 4.2 %collective-permute-start.24 = (bf16[384,384]{1,0:T(8,128)(2,1)S(1)}, bf16[384,384]{1,0:T(8,128)(2,1)S(1)}, u32[]{:S(2)}, u32[]{:S(2)}) collective-permute-start(bf16[384,384]{1,0:T(8,128)(2,1)S(1)} %collective-permute-done.23.refs_8_), channel_id=1, source_target_pairs={{0,1},{1,0},{2,3},{3,2},{4,5},{5,4},{6,7},{7,6},{8,9},{9,8},{10,11... | collective-permute-start | bytes 884744 | tf_op jit(solution)/shard_map/ppermute | solution.py:210
  113.5 1.7 %collective-permute-start.22 = (bf16[384,384]{1,0:T(8,128)(2,1)S(1)}, bf16[384,384]{1,0:T(8,128)(2,1)S(1)}, u32[]{:S(2)}, u32[]{:S(2)}) collective-permute-start(bf16[384,384]{1,0:T(8,128)(2,1)S(1)} %collective-permute-done.21.refs_6_), channel_id=1, source_target_pairs={{0,1},{1,0},{2,3},{3,2},{4,5},{5,4},{6,7},{7,6},{8,9},{9,8},{10,11... | collective-permute-start | bytes 884744 | tf_op jit(solution)/shard_map/ppermute | solution.py:210
  115.3 0.1 collective-permute-start.29
  115.4 2.5 %collective-permute-start.27 = (bf16[384,384]{1,0:T(8,128)(2,1)S(1)}, bf16[384,384]{1,0:T(8,128)(2,1)S(1)}, u32[]{:S(2)}, u32[]{:S(2)}) collective-permute-start(bf16[384,384]{1,0:T(8,128)(2,1)S(1)} %collective-permute-done.17.refs_2_), channel_id=1, source_target_pairs={{0,6},{1,7},{2,0},{3,1},{4,2},{5,3},{6,4},{7,5},{8,14},{9,15},{10,... | collective-permute-start | bytes 884744 | tf_op jit(solution)/shard_map/ppermute | solution.py:206
  117.9 1.0 collective-permute-start.18
  119.0 4.9 %collective-permute-done.29.refs_14_ = bf16[384,384]{1,0:T(8,128)(2,1)S(1)} collective-permute-done((bf16[384,384]{1,0:T(8,128)(2,1)S(1)}, bf16[384,384]{1,0:T(8,128)(2,1)S(1)}, u32[]{:S(2)}, u32[]{:S(2)}) %collective-permute-start.29) | collective-permute-done | bytes 294944 | tf_op jit(solution)/shard_map/ppermute | solution.py:206
  123.9 0.8 collective-permute-start.30
  124.7 0.4 collective-permute-start.28
  125.1 2.0 %collective-permute-done.25.refs_10_ = bf16[384,384]{1,0:T(8,128)(2,1)S(1)} collective-permute-done((bf16[384,384]{1,0:T(8,128)(2,1)S(1)}, bf16[384,384]{1,0:T(8,128)(2,1)S(1)}, u32[]{:S(2)}, u32[]{:S(2)}) %collective-permute-start.25) | collective-permute-done | bytes 294944 | tf_op jit(solution)/shard_map/ppermute | solution.py:206
  127.1 1.4 collective-permute-start.26
  128.5 1.2 collective-permute-done.26.refs_11_
  129.7 6.1 %shard_map.78 = f32[384,384]{1,0:T(8,128)} custom-call(f32[384,384]{1,0:T(8,128)S(1)} %get-tuple-element.12.square_ref, bf16[384,384]{1,0:T(8,128)(2,1)S(1)} %get-tuple-element.13.refs_0_, bf16[384,384]{1,0:T(8,128)(2,1)S(1)} %collective-permute-done.16.refs_1_, bf16[384,384]{1,0:T(8,128)(2,1)S(1)} %collective-permute-done.17.refs_2_, ...), custom_call_target="tpu_custom_call" | custom-call | flops 1811939328 | bytes 9437184 | tf_op jit(solution)/shard_map/pallas_call | solution.py:324
  (37 shorter events, 0.2 us)
Async XLA Ops:
  6.5 81.7 %all-gather.2.cloned.1.call-start = ((), (), s32[]{:S(2)}) async-start(), calls=%async_computation.2 | async-start | bytes 5013504 | tf_op jit(solution)/shard_map/all_gather | solution.py:345
  6.5 21.8 %collective-permute-start = (bf16[384,384]{1,0:T(8,128)(2,1)}, bf16[384,384]{1,0:T(8,128)(2,1)S(1)}, u32[]{:S(2)}, u32[]{:S(2)}) collective-permute-start(bf16[384,384]{1,0:T(8,128)(2,1)} %bare.1), channel_id=1, source_target_pairs={{0,128},{16,144},{32,160},{48,176},{64,192},{80,208},{96,224},{112... | collective-permute-start | bytes 884744 | tf_op jit(solution)/shard_map/ppermute | solution.py:184
  10.1 18.2 %collective-permute-start.1 = (bf16[384,384]{1,0:T(8,128)(2,1)}, bf16[384,384]{1,0:T(8,128)(2,1)S(1)}, u32[]{:S(2)}, u32[]{:S(2)}) collective-permute-start(bf16[384,384]{1,0:T(8,128)(2,1)} %inter.1), channel_id=1, source_target_pairs={{0,128},{16,144},{32,160},{48,176},{64,192},{80,208},{96,224},{112... | collective-permute-start | bytes 884744 | tf_op jit(solution)/shard_map/ppermute | solution.py:184
  28.3 0.7 copy-start.4
  29.1 0.7 copy-start.5
  48.9 6.6 %collective-permute-start.8 = (bf16[384,384]{1,0:T(8,128)(2,1)}, bf16[384,384]{1,0:T(8,128)(2,1)S(1)}, u32[]{:S(2)}, u32[]{:S(2)}) collective-permute-start(bf16[384,384]{1,0:T(8,128)(2,1)} %get-tuple-element.11.refs_4_.refs_20_), channel_id=1, source_target_pairs={{0,112},{16,0},{32,16},{48,32},{64,48},{80,64},{96,80},{112,96},{1... | collective-permute-start | bytes 884744 | tf_op jit(solution)/shard_map/ppermute | solution.py:180
  49.3 7.6 %collective-permute-start.2 = (bf16[384,384]{1,0:T(8,128)(2,1)}, bf16[384,384]{1,0:T(8,128)(2,1)S(1)}, u32[]{:S(2)}, u32[]{:S(2)}) collective-permute-start(bf16[384,384]{1,0:T(8,128)(2,1)} %get-tuple-element.10.refs_1_.refs_16_), channel_id=1, source_target_pairs={{0,16},{16,32},{32,48},{48,64},{64,80},{80,96},{96,112},{112,0},{1... | collective-permute-start | bytes 884744 | tf_op jit(solution)/shard_map/ppermute | solution.py:180
  50.4 12.5 %collective-permute-start.6 = (bf16[384,384]{1,0:T(8,128)(2,1)}, bf16[384,384]{1,0:T(8,128)(2,1)S(1)}, u32[]{:S(2)}, u32[]{:S(2)}) collective-permute-start(bf16[384,384]{1,0:T(8,128)(2,1)} %get-tuple-element.11.refs_4_.refs_20_), channel_id=1, source_target_pairs={{0,16},{16,32},{32,48},{48,64},{64,80},{80,96},{96,112},{112,0},{1... | collective-permute-start | bytes 884744 | tf_op jit(solution)/shard_map/ppermute | solution.py:180
  51.0 12.1 %collective-permute-start.4 = (bf16[384,384]{1,0:T(8,128)(2,1)}, bf16[384,384]{1,0:T(8,128)(2,1)S(1)}, u32[]{:S(2)}, u32[]{:S(2)}) collective-permute-start(bf16[384,384]{1,0:T(8,128)(2,1)} %get-tuple-element.10.refs_1_.refs_16_), channel_id=1, source_target_pairs={{0,112},{16,0},{32,16},{48,32},{64,48},{80,64},{96,80},{112,96},{1... | collective-permute-start | bytes 884744 | tf_op jit(solution)/shard_map/ppermute | solution.py:180
  55.4 12.7 %collective-permute-start.9 = (bf16[384,384]{1,0:T(8,128)(2,1)S(1)}, bf16[384,384]{1,0:T(8,128)(2,1)S(1)}, u32[]{:S(2)}, u32[]{:S(2)}) collective-permute-start(bf16[384,384]{1,0:T(8,128)(2,1)S(1)} %collective-permute-done.8.refs_14_.refs_31_), channel_id=1, source_target_pairs={{0,112},{16,0},{32,16},{48,32},{64,48},{80,64},{96,80},{112,96},{1... | collective-permute-start | bytes 884744 | tf_op jit(solution)/shard_map/ppermute | solution.py:180
  56.9 13.0 %collective-permute-start.3 = (bf16[384,384]{1,0:T(8,128)(2,1)S(1)}, bf16[384,384]{1,0:T(8,128)(2,1)S(1)}, u32[]{:S(2)}, u32[]{:S(2)}) collective-permute-start(bf16[384,384]{1,0:T(8,128)(2,1)S(1)} %collective-permute-done.2.refs_7_.refs_24_), channel_id=1, source_target_pairs={{0,16},{16,32},{32,48},{48,64},{64,80},{80,96},{96,112},{112,0},{1... | collective-permute-start | bytes 884744 | tf_op jit(solution)/shard_map/ppermute | solution.py:180
  62.9 12.6 %collective-permute-start.7 = (bf16[384,384]{1,0:T(8,128)(2,1)S(1)}, bf16[384,384]{1,0:T(8,128)(2,1)S(1)}, u32[]{:S(2)}, u32[]{:S(2)}) collective-permute-start(bf16[384,384]{1,0:T(8,128)(2,1)S(1)} %collective-permute-done.6.refs_11_.refs_28_), channel_id=1, source_target_pairs={{0,16},{16,32},{32,48},{48,64},{64,80},{80,96},{96,112},{112,0},{1... | collective-permute-start | bytes 884744 | tf_op jit(solution)/shard_map/ppermute | solution.py:180
  63.0 12.6 %collective-permute-start.5 = (bf16[384,384]{1,0:T(8,128)(2,1)S(1)}, bf16[384,384]{1,0:T(8,128)(2,1)S(1)}, u32[]{:S(2)}, u32[]{:S(2)}) collective-permute-start(bf16[384,384]{1,0:T(8,128)(2,1)S(1)} %collective-permute-done.4.refs_10_.refs_27_), channel_id=1, source_target_pairs={{0,112},{16,0},{32,16},{48,32},{64,48},{80,64},{96,80},{112,96},{1... | collective-permute-start | bytes 884744 | tf_op jit(solution)/shard_map/ppermute | solution.py:180
  68.2 12.6 %collective-permute-start.13 = (bf16[384,384]{1,0:T(8,128)(2,1)S(1)}, bf16[384,384]{1,0:T(8,128)(2,1)S(1)}, u32[]{:S(2)}, u32[]{:S(2)}) collective-permute-start(bf16[384,384]{1,0:T(8,128)(2,1)S(1)} %collective-permute-done.9.refs_6_.refs_23_), channel_id=1, source_target_pairs={{0,112},{16,0},{32,16},{48,32},{64,48},{80,64},{96,80},{112,96},{1... | collective-permute-start | bytes 884744 | tf_op jit(solution)/shard_map/ppermute | solution.py:180
  69.8 12.0 %collective-permute-start.10 = (bf16[384,384]{1,0:T(8,128)(2,1)S(1)}, bf16[384,384]{1,0:T(8,128)(2,1)S(1)}, u32[]{:S(2)}, u32[]{:S(2)}) collective-permute-start(bf16[384,384]{1,0:T(8,128)(2,1)S(1)} %collective-permute-done.3.refs_2_.refs_17_), channel_id=1, source_target_pairs={{0,16},{16,32},{32,48},{48,64},{64,80},{80,96},{96,112},{112,0},{1... | collective-permute-start | bytes 884744 | tf_op jit(solution)/shard_map/ppermute | solution.py:180
  75.6 12.6 %collective-permute-start.12 = (bf16[384,384]{1,0:T(8,128)(2,1)S(1)}, bf16[384,384]{1,0:T(8,128)(2,1)S(1)}, u32[]{:S(2)}, u32[]{:S(2)}) collective-permute-start(bf16[384,384]{1,0:T(8,128)(2,1)S(1)} %collective-permute-done.7.refs_5_.refs_21_), channel_id=1, source_target_pairs={{0,16},{16,32},{32,48},{48,64},{64,80},{80,96},{96,112},{112,0},{1... | collective-permute-start | bytes 884744 | tf_op jit(solution)/shard_map/ppermute | solution.py:180
  75.7 12.5 %collective-permute-start.11 = (bf16[384,384]{1,0:T(8,128)(2,1)S(1)}, bf16[384,384]{1,0:T(8,128)(2,1)S(1)}, u32[]{:S(2)}, u32[]{:S(2)}) collective-permute-start(bf16[384,384]{1,0:T(8,128)(2,1)S(1)} %collective-permute-done.5.refs_3_.refs_19_), channel_id=1, source_target_pairs={{0,112},{16,0},{32,16},{48,32},{64,48},{80,64},{96,80},{112,96},{1... | collective-permute-start | bytes 884744 | tf_op jit(solution)/shard_map/ppermute | solution.py:180
  80.8 16.1 %collective-permute-start.15 = (bf16[384,384]{1,0:T(8,128)(2,1)S(1)}, bf16[384,384]{1,0:T(8,128)(2,1)}, u32[]{:S(2)}, u32[]{:S(2)}) collective-permute-start(bf16[384,384]{1,0:T(8,128)(2,1)S(1)} %collective-permute-done.13.refs_13_.refs_30_), channel_id=1, source_target_pairs={{0,112},{16,0},{32,16},{48,32},{64,48},{80,64},{96,80},{112,96},{1... | collective-permute-start | bytes 884744 | tf_op jit(solution)/shard_map/ppermute | solution.py:180
  81.9 15.0 %collective-permute-start.14 = (bf16[384,384]{1,0:T(8,128)(2,1)S(1)}, bf16[384,384]{1,0:T(8,128)(2,1)}, u32[]{:S(2)}, u32[]{:S(2)}) collective-permute-start(bf16[384,384]{1,0:T(8,128)(2,1)S(1)} %collective-permute-done.10.refs_8_.refs_25_), channel_id=1, source_target_pairs={{0,16},{16,32},{32,48},{48,64},{64,80},{80,96},{96,112},{112,0},{1... | collective-permute-start | bytes 884744 | tf_op jit(solution)/shard_map/ppermute | solution.py:180
  88.2 2.3 %copy-start = (bf16[384,6144]{1,0:T(8,128)(2,1)S(1)}, bf16[384,6144]{1,0:T(8,128)(2,1)}, u32[]{:S(2)}) copy-start(bf16[384,6144]{1,0:T(8,128)(2,1)} %all-gather.2.cloned.1.call-done.refs_0_) | copy-start | bytes 14155780
  90.5 1.0 copy-start.2
  91.5 1.0 copy-start.3
  92.5 4.4 %copy-start.1 = (bf16[384,6144]{1,0:T(8,128)(2,1)S(1)}, bf16[384,6144]{1,0:T(8,128)(2,1)}, u32[]{:S(2)}) copy-start(bf16[384,6144]{1,0:T(8,128)(2,1)} %all-gather.2.cloned.1.call-done.refs_0_) | copy-start | bytes 14155780
  98.5 10.9 %collective-permute-start.23 = (bf16[384,384]{1,0:T(8,128)(2,1)S(1)}, bf16[384,384]{1,0:T(8,128)(2,1)S(1)}, u32[]{:S(2)}, u32[]{:S(2)}) collective-permute-start(bf16[384,384]{1,0:T(8,128)(2,1)S(1)} %get-tuple-element.13.refs_0_), channel_id=1, source_target_pairs={{0,4},{1,5},{2,6},{3,7},{4,0},{5,1},{6,2},{7,3},{8,12},{9,13},{10,... | collective-permute-start | bytes 884744 | tf_op jit(solution)/shard_map/ppermute | solution.py:206
  99.8 9.5 %collective-permute-start.17 = (bf16[384,384]{1,0:T(8,128)(2,1)S(1)}, bf16[384,384]{1,0:T(8,128)(2,1)S(1)}, u32[]{:S(2)}, u32[]{:S(2)}) collective-permute-start(bf16[384,384]{1,0:T(8,128)(2,1)S(1)} %get-tuple-element.13.refs_0_), channel_id=1, source_target_pairs={{0,8},{1,9},{2,10},{3,11},{4,12},{5,13},{6,14},{7,15},{8,0},{9,1},... | collective-permute-start | bytes 884744 | tf_op jit(solution)/shard_map/ppermute | solution.py:206
  100.0 13.5 %collective-permute-start.21 = (bf16[384,384]{1,0:T(8,128)(2,1)S(1)}, bf16[384,384]{1,0:T(8,128)(2,1)S(1)}, u32[]{:S(2)}, u32[]{:S(2)}) collective-permute-start(bf16[384,384]{1,0:T(8,128)(2,1)S(1)} %get-tuple-element.13.refs_0_), channel_id=1, source_target_pairs={{0,6},{1,7},{2,0},{3,1},{4,2},{5,3},{6,4},{7,5},{8,14},{9,15},{10,... | collective-permute-start | bytes 884744 | tf_op jit(solution)/shard_map/ppermute | solution.py:206
  101.3 14.0 %collective-permute-start.19 = (bf16[384,384]{1,0:T(8,128)(2,1)S(1)}, bf16[384,384]{1,0:T(8,128)(2,1)S(1)}, u32[]{:S(2)}, u32[]{:S(2)}) collective-permute-start(bf16[384,384]{1,0:T(8,128)(2,1)S(1)} %get-tuple-element.13.refs_0_), channel_id=1, source_target_pairs={{0,2},{1,3},{2,4},{3,5},{4,6},{5,7},{6,0},{7,1},{8,10},{9,11},{10,... | collective-permute-start | bytes 884744 | tf_op jit(solution)/shard_map/ppermute | solution.py:206
  101.5 16.4 %collective-permute-start.16 = (bf16[384,384]{1,0:T(8,128)(2,1)S(1)}, bf16[384,384]{1,0:T(8,128)(2,1)S(1)}, u32[]{:S(2)}, u32[]{:S(2)}) collective-permute-start(bf16[384,384]{1,0:T(8,128)(2,1)S(1)} %get-tuple-element.13.refs_0_), channel_id=1, source_target_pairs={{0,1},{1,0},{2,3},{3,2},{4,5},{5,4},{6,7},{7,6},{8,9},{9,8},{10,11... | collective-permute-start | bytes 884744 | tf_op jit(solution)/shard_map/ppermute | solution.py:210
  109.3 8.5 %collective-permute-start.24 = (bf16[384,384]{1,0:T(8,128)(2,1)S(1)}, bf16[384,384]{1,0:T(8,128)(2,1)S(1)}, u32[]{:S(2)}, u32[]{:S(2)}) collective-permute-start(bf16[384,384]{1,0:T(8,128)(2,1)S(1)} %collective-permute-done.23.refs_8_), channel_id=1, source_target_pairs={{0,1},{1,0},{2,3},{3,2},{4,5},{5,4},{6,7},{7,6},{8,9},{9,8},{10,11... | collective-permute-start | bytes 884744 | tf_op jit(solution)/shard_map/ppermute | solution.py:210
  113.5 5.4 %collective-permute-start.22 = (bf16[384,384]{1,0:T(8,128)(2,1)S(1)}, bf16[384,384]{1,0:T(8,128)(2,1)S(1)}, u32[]{:S(2)}, u32[]{:S(2)}) collective-permute-start(bf16[384,384]{1,0:T(8,128)(2,1)S(1)} %collective-permute-done.21.refs_6_), channel_id=1, source_target_pairs={{0,1},{1,0},{2,3},{3,2},{4,5},{5,4},{6,7},{7,6},{8,9},{9,8},{10,11... | collective-permute-start | bytes 884744 | tf_op jit(solution)/shard_map/ppermute | solution.py:210
  115.3 8.6 %collective-permute-start.29 = (bf16[384,384]{1,0:T(8,128)(2,1)S(1)}, bf16[384,384]{1,0:T(8,128)(2,1)S(1)}, u32[]{:S(2)}, u32[]{:S(2)}) collective-permute-start(bf16[384,384]{1,0:T(8,128)(2,1)S(1)} %collective-permute-done.23.refs_8_), channel_id=1, source_target_pairs={{0,8},{1,9},{2,10},{3,11},{4,12},{5,13},{6,14},{7,15},{8,0},{9,1},... | collective-permute-start | bytes 884744 | tf_op jit(solution)/shard_map/ppermute | solution.py:206
  115.4 9.3 %collective-permute-start.27 = (bf16[384,384]{1,0:T(8,128)(2,1)S(1)}, bf16[384,384]{1,0:T(8,128)(2,1)S(1)}, u32[]{:S(2)}, u32[]{:S(2)}) collective-permute-start(bf16[384,384]{1,0:T(8,128)(2,1)S(1)} %collective-permute-done.17.refs_2_), channel_id=1, source_target_pairs={{0,6},{1,7},{2,0},{3,1},{4,2},{5,3},{6,4},{7,5},{8,14},{9,15},{10,... | collective-permute-start | bytes 884744 | tf_op jit(solution)/shard_map/ppermute | solution.py:206
  117.9 9.2 %collective-permute-start.25 = (bf16[384,384]{1,0:T(8,128)(2,1)S(1)}, bf16[384,384]{1,0:T(8,128)(2,1)S(1)}, u32[]{:S(2)}, u32[]{:S(2)}) collective-permute-start(bf16[384,384]{1,0:T(8,128)(2,1)S(1)} %collective-permute-done.17.refs_2_), channel_id=1, source_target_pairs={{0,2},{1,3},{2,4},{3,5},{4,6},{5,7},{6,0},{7,1},{8,10},{9,11},{10,... | collective-permute-start | bytes 884744 | tf_op jit(solution)/shard_map/ppermute | solution.py:206
  117.9 10.6 %collective-permute-start.18 = (bf16[384,384]{1,0:T(8,128)(2,1)S(1)}, bf16[384,384]{1,0:T(8,128)(2,1)S(1)}, u32[]{:S(2)}, u32[]{:S(2)}) collective-permute-start(bf16[384,384]{1,0:T(8,128)(2,1)S(1)} %collective-permute-done.17.refs_2_), channel_id=1, source_target_pairs={{0,1},{1,0},{2,3},{3,2},{4,5},{5,4},{6,7},{7,6},{8,9},{9,8},{10,11... | collective-permute-start | bytes 884744 | tf_op jit(solution)/shard_map/ppermute | solution.py:210
  118.9 9.6 %collective-permute-start.20 = (bf16[384,384]{1,0:T(8,128)(2,1)S(1)}, bf16[384,384]{1,0:T(8,128)(2,1)S(1)}, u32[]{:S(2)}, u32[]{:S(2)}) collective-permute-start(bf16[384,384]{1,0:T(8,128)(2,1)S(1)} %collective-permute-done.19.refs_4_), channel_id=1, source_target_pairs={{0,1},{1,0},{2,3},{3,2},{4,5},{5,4},{6,7},{7,6},{8,9},{9,8},{10,11... | collective-permute-start | bytes 884744 | tf_op jit(solution)/shard_map/ppermute | solution.py:210
  123.9 4.6 %collective-permute-start.30 = (bf16[384,384]{1,0:T(8,128)(2,1)S(1)}, bf16[384,384]{1,0:T(8,128)(2,1)S(1)}, u32[]{:S(2)}, u32[]{:S(2)}) collective-permute-start(bf16[384,384]{1,0:T(8,128)(2,1)S(1)} %collective-permute-done.29.refs_14_), channel_id=1, source_target_pairs={{0,1},{1,0},{2,3},{3,2},{4,5},{5,4},{6,7},{7,6},{8,9},{9,8},{10,11... | collective-permute-start | bytes 884744 | tf_op jit(solution)/shard_map/ppermute | solution.py:210
  124.7 3.8 %collective-permute-start.28 = (bf16[384,384]{1,0:T(8,128)(2,1)S(1)}, bf16[384,384]{1,0:T(8,128)(2,1)S(1)}, u32[]{:S(2)}, u32[]{:S(2)}) collective-permute-start(bf16[384,384]{1,0:T(8,128)(2,1)S(1)} %collective-permute-done.27.refs_12_), channel_id=1, source_target_pairs={{0,1},{1,0},{2,3},{3,2},{4,5},{5,4},{6,7},{7,6},{8,9},{9,8},{10,11... | collective-permute-start | bytes 884744 | tf_op jit(solution)/shard_map/ppermute | solution.py:210
  127.1 2.6 %collective-permute-start.26 = (bf16[384,384]{1,0:T(8,128)(2,1)S(1)}, bf16[384,384]{1,0:T(8,128)(2,1)S(1)}, u32[]{:S(2)}, u32[]{:S(2)}) collective-permute-start(bf16[384,384]{1,0:T(8,128)(2,1)S(1)} %collective-permute-done.25.refs_10_), channel_id=1, source_target_pairs={{0,1},{1,0},{2,3},{3,2},{4,5},{5,4},{6,7},{7,6},{8,9},{9,8},{10,11... | collective-permute-start | bytes 884744 | tf_op jit(solution)/shard_map/ppermute | solution.py:210
Sparse Core Ops, SparseCore 0:
  49.0 37.6 all-gather.1
